TPU v7x, 512 devices: a whole 4x8x8 slice. The times are simulated.
512 devices in a mesh: space: 64 (over z, y_hi, core), spec: 8 (over y_lo, x).
Axes of the slice: x: 4, y: 8 (y_hi: 4, y_lo: 2; y = y_hi * 2 + y_lo), z: 8, core: 2. Of those that a mesh axis runs over, the one named last changes fastest.
Arguments:
- spectrum: float32 [24, 25, 256, 1024], P('spec', None, 'space'), as said below
- sea_mask: int32 [256, 1024], P('space'), may hold values 0 or 1
- turning: float32 [256, 1024], P('space'), may hold values from -0.4 to 0.4
- wind_u: float32 [256, 1024], P('space'), may hold values from -4 to 4
- wind_v: float32 [256, 1024], P('space'), may hold values from -4 to 4
Outputs:
- updated: float32 [24, 25, 256, 1024], P('spec', None, 'space')
Inputs may be any that keep to these rules, and one draw needn't show every extreme that they name: `spectrum`: positive.
All inputs are finite; a program needn't handle non-finite values. No bound on the sum of `sea_mask` on one device may be relied on, other than what follows from the above.
Results may differ from a plain program's by a relative error of at most 0.00002.
Values sent between devices are 32-bit elements; how exact they have to be, the bound alone decides.
No kernel may reach another device: no remote copies, remote signals or barrier semaphores. Data moves between devices by JAX's collectives and lax.ppermute only.
A program may use at most 64 MiB of HBM per device.

v0:
```python
import jax
import jax.numpy as jnp
from jax import lax
from jax.sharding import PartitionSpec as P

DIRS = 24
FREQS = 25
SUB = 4


def extended(array, sides, width, wrap):
    for axis, dim in sides:
        size, length = (lax.axis_size(axis), array.shape[dim])
        up = [(i, (i + 1) % size) for i in range(size if wrap else size - 1)]
        down = [(j, i) for i, j in up]
        last = lax.slice_in_dim(array, length - width, length, axis=dim)
        leading = lax.slice_in_dim(array, 0, width, axis=dim)
        before = lax.ppermute(last, axis, up)
        after = lax.ppermute(leading, axis, down)
        array = jnp.concatenate([before, array, after], axis=dim)
    return array


def tables(dir_index):
    theta = 2.0 * jnp.pi * dir_index.astype(jnp.float32) / DIRS
    freq = jnp.arange(FREQS).astype(jnp.float32)
    fr = jnp.power(jnp.float32(1.1), freq - FREQS // 2)
    speed = jnp.power(jnp.float32(1.1), -freq)
    rfac = 0.5 + 0.5 * speed
    mux = (0.42 * speed[None, :] * jnp.cos(theta)[:, None])[:, :, None, None]
    muy = (0.42 * speed[None, :] * jnp.sin(theta)[:, None])[:, :, None, None]
    return (theta, fr, rfac, mux, muy)


def combine(action, west, east, south, north, before, after, sea_rows, turn_rows, mux, muy, rfac):
    mth = turn_rows[None, None] * rfac[None, :, None, None]
    fresh = (
        action - jnp.maximum(mux, 0.0) * (action - west) - jnp.maximum(-mux, 0.0) * (action - east)
    )
    fresh = (
        fresh - jnp.maximum(muy, 0.0) * (action - south) - jnp.maximum(-muy, 0.0) * (action - north)
    )
    fresh = (
        fresh
        - jnp.maximum(mth, 0.0) * (action - before)
        - jnp.maximum(-mth, 0.0) * (action - after)
    )
    return fresh * sea_rows


def advance(lat_ext, dir_ext, sea_rows, turn_rows, mux, muy, rfac):
    action = lat_ext[:, :, 1:-1]
    south = lat_ext[:, :, :-2]
    north = lat_ext[:, :, 2:]
    padded = jnp.pad(action, ((0, 0), (0, 0), (0, 0), (1, 1)))
    west = padded[:, :, :, :-2]
    east = padded[:, :, :, 2:]
    before = dir_ext[:-2]
    after = dir_ext[2:]
    return combine(
        action, west, east, south, north, before, after, sea_rows, turn_rows, mux, muy, rfac
    )


def forcing(theta, fr, wind_u, wind_v):
    along = (
        wind_u[None] * jnp.cos(theta)[:, None, None] + wind_v[None] * jnp.sin(theta)[:, None, None]
    )
    return 0.5 * fr[None, :, None, None] * jnp.maximum(along, 0.0)[:, None]


def sources(action, theta, fr, wind_u, wind_v):
    fr_sq = (fr * fr)[None, :, None, None]
    mean_zero = jnp.sum(action, axis=(0, 1)) / (DIRS * FREQS)
    mean_two = jnp.sum(action * fr_sq, axis=(0, 1)) / (DIRS * FREQS)
    growth = forcing(theta, fr, wind_u, wind_v)
    decay = 0.5 * fr_sq * (mean_two / (1.0 + mean_zero))[None, None]
    return action * (1.0 + growth) / (1.0 + decay)


def on_device(spectrum, sea_mask, turning, wind_u, wind_v):
    dir_count = spectrum.shape[0]
    columns = spectrum.shape[3]
    spec_size = lax.axis_size("spec")
    first_dir = lax.axis_index("spec") * dir_count
    own_dirs = first_dir + jnp.arange(dir_count)
    sea = (sea_mask == 1).astype(jnp.float32)
    action = spectrum * sea
    theta, fr, rfac, mux, muy = tables(own_dirs)
    for step in range(SUB):
        lat_ext = extended(action, (("space", 2),), 1, False)
        dir_ext = extended(action, (("spec", 0),), 1, True)
        action = advance(lat_ext, dir_ext, sea, turning, mux, muy, rfac)
    points = lax.all_to_all(action, "spec", split_axis=3, concat_axis=0, tiled=True)
    width = columns // spec_size
    start = lax.axis_index("spec") * width
    all_theta = 2.0 * jnp.pi * jnp.arange(DIRS).astype(jnp.float32) / DIRS
    local_u = lax.dynamic_slice_in_dim(wind_u, start, width, 1)
    local_v = lax.dynamic_slice_in_dim(wind_v, start, width, 1)
    result = sources(points, all_theta, fr, local_u, local_v)
    return lax.all_to_all(result, "spec", split_axis=0, concat_axis=3, tiled=True)


def solution(mesh):
    in_specs = (
        P("spec", None, "space", None),
        P("space", None),
        P("space", None),
        P("space", None),
        P("space", None),
    )
    out_specs = P("spec", None, "space", None)
    return jax.shard_map(
        on_device, mesh=mesh, in_specs=in_specs, out_specs=out_specs, check_vma=False
    )
```

profile of v0, /device:TPU:320, one launch (start us, length us, event | category | flops | bytes accessed | tf_op | source)
XLA Modules:
  0.0 208.2 jit_solution(1234317271154045595)
XLA Ops:
  0.0 0.7 compare_convert_fusion
  0.7 2.0 copy_multiply_fusion
  2.7 0.9 fusion.95
  3.7 3.4 %collective-permute-start.2 = (f32[1,25,4,1024]{3,1,2,0:T(8,128)}, f32[1,25,4,1024]{3,1,2,0:T(8,128)S(1)}, u32[]{:S(2)}, u32[]{:S(2)}) collective-permute-start(f32[1,25,4,1024]{3,1,2,0:T(8,128)} %get-tuple-element.21), channel_id=1, source_target_pairs={{0,1},{1,2},{2,3},{3,4},{4,5},{5,6},{6,7},{7,0},{8,9},{9,10},{10,1... | collective-permute-start | bytes 1228808 | tf_op jit(solution)/shard_map/ppermute | solution.py:18
  7.0 4.6 %collective-permute-start.3 = (f32[1,25,4,1024]{3,1,2,0:T(8,128)S(1)}, f32[1,25,4,1024]{3,1,2,0:T(8,128)S(1)}, u32[]{:S(2)}, u32[]{:S(2)}) collective-permute-start(f32[1,25,4,1024]{3,1,2,0:T(8,128)S(1)} %get-tuple-element.22), channel_id=1, source_target_pairs={{1,0},{2,1},{3,2},{4,3},{5,4},{6,5},{7,6},{0,7},{9,8},{10,9},{11,1... | collective-permute-start | bytes 1228808 | tf_op jit(solution)/shard_map/ppermute | solution.py:19
  11.6 1.0 fusion.94
  12.6 1.9 collective-permute-start
  14.5 6.7 %collective-permute-start.1 = (f32[3,25,1,1024]{3,1,2,0:T(8,128)}, f32[3,25,1,1024]{3,1,2,0:T(8,128)}, u32[]{:S(2)}, u32[]{:S(2)}) collective-permute-start(f32[3,25,1,1024]{3,1,2,0:T(8,128)} %get-tuple-element.20), channel_id=1, source_target_pairs={{8,0},{16,8},{24,16},{32,24},{40,32},{48,40},{56,48},{64,56},{72,6... | collective-permute-start | bytes 921608 | tf_op jit(solution)/shard_map/ppermute | solution.py:19
  21.2 0.6 fusion.83
  21.7 0.7 multiply_maximum_fusion.2
  22.5 0.9 multiply_maximum_fusion
  23.4 12.2 %collective-permute-done = f32[3,25,1,1024]{3,1,2,0:T(8,128)S(1)} collective-permute-done((f32[3,25,1,1024]{3,1,2,0:T(8,128)}, f32[3,25,1,1024]{3,1,2,0:T(8,128)S(1)}, u32[]{:S(2)}, u32[]{:S(2)}) %collective-permute-start) | collective-permute-done | bytes 307232 | tf_op jit(solution)/shard_map/ppermute | solution.py:18
  35.6 2.7 %fusion.8 = f32[3,25,4,1024]{3,1,2,0:T(8,128)S(1)} fusion(f32[3,25,4,1024]{3,1,2,0:T(8,128)S(1)} %copy_multiply_fusion, f32[1,25,4,1024]{3,1,2,0:T(8,128)S(1)} %collective-permute-done.3, f32[1,25,4,1024]{3,1,2,0:T(8,128)S(1)} %collective-permute-done.2, f32[3,25,1,1024]{3,1,2,0:T(8,128)} %collective-permute-done.1, ...), kind=kLoop, calls=%fused_computation.16 | loop fusion | flops 7065600 | bytes 4727984 | tf_op jit(solution)/shard_map/mul | solution.py:48
  38.5 1.9 collective-permute-start.6
  40.4 6.0 %collective-permute-start.7 = (f32[1,25,4,1024]{3,1,2,0:T(8,128)S(1)}, f32[1,25,4,1024]{3,1,2,0:T(8,128)S(1)}, u32[]{:S(2)}, u32[]{:S(2)}) collective-permute-start(f32[1,25,4,1024]{3,1,2,0:T(8,128)S(1)} %get-tuple-element.18), channel_id=1, source_target_pairs={{1,0},{2,1},{3,2},{4,3},{5,4},{6,5},{7,6},{0,7},{9,8},{10,9},{11,1... | collective-permute-start | bytes 1228808 | tf_op jit(solution)/shard_map/ppermute | solution.py:19
  46.5 1.9 collective-permute-start.4
  48.4 6.7 %collective-permute-start.5 = (f32[3,25,1,1024]{3,1,2,0:T(8,128)S(1)}, f32[3,25,1,1024]{3,1,2,0:T(8,128)S(1)}, u32[]{:S(2)}, u32[]{:S(2)}) collective-permute-start(f32[3,25,1,1024]{3,1,2,0:T(8,128)S(1)} %get-tuple-element.16), channel_id=1, source_target_pairs={{8,0},{16,8},{24,16},{32,24},{40,32},{48,40},{56,48},{64,56},{72,6... | collective-permute-start | bytes 921608 | tf_op jit(solution)/shard_map/ppermute | solution.py:19
  55.1 11.0 %collective-permute-done.4 = f32[3,25,1,1024]{3,1,2,0:T(8,128)S(1)} collective-permute-done((f32[3,25,1,1024]{3,1,2,0:T(8,128)S(1)}, f32[3,25,1,1024]{3,1,2,0:T(8,128)S(1)}, u32[]{:S(2)}, u32[]{:S(2)}) %collective-permute-start.4) | collective-permute-done | bytes 307232 | tf_op jit(solution)/shard_map/ppermute | solution.py:18
  66.1 1.9 fusion.19
  68.0 0.1 fusion.91
  68.2 1.9 collective-permute-start.10
  70.1 6.0 %collective-permute-start.11 = (f32[1,25,4,1024]{3,1,2,0:T(8,128)S(1)}, f32[1,25,4,1024]{3,1,2,0:T(8,128)S(1)}, u32[]{:S(2)}, u32[]{:S(2)}) collective-permute-start(f32[1,25,4,1024]{3,1,2,0:T(8,128)S(1)} %get-tuple-element.14), channel_id=1, source_target_pairs={{1,0},{2,1},{3,2},{4,3},{5,4},{6,5},{7,6},{0,7},{9,8},{10,9},{11,1... | collective-permute-start | bytes 1228808 | tf_op jit(solution)/shard_map/ppermute | solution.py:19
  76.2 1.9 collective-permute-start.8
  78.1 6.7 %collective-permute-start.9 = (f32[3,25,1,1024]{3,1,2,0:T(8,128)S(1)}, f32[3,25,1,1024]{3,1,2,0:T(8,128)S(1)}, u32[]{:S(2)}, u32[]{:S(2)}) collective-permute-start(f32[3,25,1,1024]{3,1,2,0:T(8,128)S(1)} %get-tuple-element.12), channel_id=1, source_target_pairs={{8,0},{16,8},{24,16},{32,24},{40,32},{48,40},{56,48},{64,56},{72,6... | collective-permute-start | bytes 921608 | tf_op jit(solution)/shard_map/ppermute | solution.py:19
  84.8 14.6 %collective-permute-done.8 = f32[3,25,1,1024]{3,1,2,0:T(8,128)S(1)} collective-permute-done((f32[3,25,1,1024]{3,1,2,0:T(8,128)S(1)}, f32[3,25,1,1024]{3,1,2,0:T(8,128)S(1)}, u32[]{:S(2)}, u32[]{:S(2)}) %collective-permute-start.8) | collective-permute-done | bytes 307232 | tf_op jit(solution)/shard_map/ppermute | solution.py:18
  99.4 1.9 fusion.30
  101.4 1.9 collective-permute-start.14
  103.4 6.0 %collective-permute-start.15 = (f32[1,25,4,1024]{3,1,2,0:T(8,128)S(1)}, f32[1,25,4,1024]{3,1,2,0:T(8,128)S(1)}, u32[]{:S(2)}, u32[]{:S(2)}) collective-permute-start(f32[1,25,4,1024]{3,1,2,0:T(8,128)S(1)} %get-tuple-element.10), channel_id=1, source_target_pairs={{1,0},{2,1},{3,2},{4,3},{5,4},{6,5},{7,6},{0,7},{9,8},{10,9},{11,1... | collective-permute-start | bytes 1228808 | tf_op jit(solution)/shard_map/ppermute | solution.py:19
  109.5 1.9 collective-permute-start.12
  111.4 6.7 %collective-permute-start.13 = (f32[3,25,1,1024]{3,1,2,0:T(8,128)S(1)}, f32[3,25,1,1024]{3,1,2,0:T(8,128)S(1)}, u32[]{:S(2)}, u32[]{:S(2)}) collective-permute-start(f32[3,25,1,1024]{3,1,2,0:T(8,128)S(1)} %get-tuple-element.8), channel_id=1, source_target_pairs={{8,0},{16,8},{24,16},{32,24},{40,32},{48,40},{56,48},{64,56},{72,6... | collective-permute-start | bytes 921608 | tf_op jit(solution)/shard_map/ppermute | solution.py:19
  118.1 8.8 %collective-permute-done.12 = f32[3,25,1,1024]{3,1,2,0:T(8,128)S(1)} collective-permute-done((f32[3,25,1,1024]{3,1,2,0:T(8,128)S(1)}, f32[3,25,1,1024]{3,1,2,0:T(8,128)S(1)}, u32[]{:S(2)}, u32[]{:S(2)}) %collective-permute-start.12) | collective-permute-done | bytes 307232 | tf_op jit(solution)/shard_map/ppermute | solution.py:18
  126.9 0.7 collective-permute-done.13
  127.5 1.9 fusion.41
  129.4 4.7 %copy.14 = f32[3,25,4,1024]{1,2,0,3:T(4,128)} copy(f32[3,25,4,1024]{3,1,2,0:T(8,128)S(1)} %fusion.41) | data formatting | bytes 2457600 | tf_op jit(solution)/shard_map/mul | solution.py:48
  134.1 9.8 %reshape.202 = f32[8,1,38400]{2,1,0:T(1,128)} reshape(f32[1024,3,4,25]{3,2,1,0:T(4,128)} %bitcast.21) | data formatting | bytes 2457600
  143.9 3.7 %all-to-all-start = ((f32[8,1,38400]{2,1,0:T(1,128)}), f32[8,1,38400]{2,1,0:T(1,128)S(1)}, u32[]{:S(2)}, u32[]{:S(2)}) async-start(f32[8,1,38400]{2,1,0:T(1,128)} %reshape.202), calls=%async_computation | async-start | bytes 2457600 | tf_op jit(solution)/shard_map/all_to_all | solution.py:94
  147.7 0.7 constant_dynamic-slice_fusion
  148.4 0.1 add_maximum_fusion
  148.6 14.4 %all-to-all-done = f32[8,1,38400]{2,1,0:T(1,128)S(1)} async-done(((f32[8,1,38400]{2,1,0:T(1,128)}), f32[8,1,38400]{2,1,0:T(1,128)S(1)}, u32[]{:S(2)}, u32[]{:S(2)}) %all-to-all-start) | async-done | bytes 1228832 | tf_op jit(solution)/shard_map/all_to_all | solution.py:94
  162.9 0.5 broadcast.311
  163.4 3.7 %reduce.2 = f32[8,38400]{1,0:T(8,128)S(1)} reduce(f32[8,1,38400]{2,1,0:T(1,128)S(1)} %all-to-all-done, f32[]{:T(128)} %broadcast.311), dimensions={1}, to_apply=%all_to_all.26.reduce_sub_computation | reduce | bytes 2457604 | tf_op jit(solution)/shard_map/all_to_all | solution.py:94
  167.1 11.7 %reshape.203 = f32[1024,3,4,25]{3,2,1,0:T(4,128)} reshape(f32[8,38400]{1,0:T(8,128)S(1)} %reduce.2) | data formatting | bytes 2457600
  178.8 5.2 %copy.15 = f32[3,25,4,8,128]{4,2,1,0,3:T(4,128)S(1)} copy(f32[3,25,4,8,128]{1,2,0,4,3:T(4,128)} %bitcast.20) | data formatting | bytes 2457600 | tf_op jit(solution)/shard_map/all_to_all | solution.py:94
  184.1 0.7 fusion.77
  184.8 0.1 multiply_add_fusion
  184.9 0.4 fusion.76
  185.4 21.4 %all_to_all.36 = f32[24,25,4,128]{3,2,1,0:T(4,128)S(1)} all-to-all(f32[24,25,4,128]{3,2,1,0:T(4,128)S(1)} %fusion.76), channel_id=1, replica_groups=mesh['space'=64,'spec'=8] {'spec'}, dimensions={0} | all-to-all | bytes 2457600 | tf_op jit(solution)/shard_map/all_to_all | solution.py:101
  206.8 1.4 copy.20
  (23 shorter events, 0.5 us)
Async XLA Ops:
  3.7 32.0 %collective-permute-start.2 = (f32[1,25,4,1024]{3,1,2,0:T(8,128)}, f32[1,25,4,1024]{3,1,2,0:T(8,128)S(1)}, u32[]{:S(2)}, u32[]{:S(2)}) collective-permute-start(f32[1,25,4,1024]{3,1,2,0:T(8,128)} %get-tuple-element.21), channel_id=1, source_target_pairs={{0,1},{1,2},{2,3},{3,4},{4,5},{5,6},{6,7},{7,0},{8,9},{9,10},{10,1... | collective-permute-start | bytes 1228808 | tf_op jit(solution)/shard_map/ppermute | solution.py:18
  7.0 28.6 %collective-permute-start.3 = (f32[1,25,4,1024]{3,1,2,0:T(8,128)S(1)}, f32[1,25,4,1024]{3,1,2,0:T(8,128)S(1)}, u32[]{:S(2)}, u32[]{:S(2)}) collective-permute-start(f32[1,25,4,1024]{3,1,2,0:T(8,128)S(1)} %get-tuple-element.22), channel_id=1, source_target_pairs={{1,0},{2,1},{3,2},{4,3},{5,4},{6,5},{7,6},{0,7},{9,8},{10,9},{11,1... | collective-permute-start | bytes 1228808 | tf_op jit(solution)/shard_map/ppermute | solution.py:19
  12.6 23.0 %collective-permute-start = (f32[3,25,1,1024]{3,1,2,0:T(8,128)}, f32[3,25,1,1024]{3,1,2,0:T(8,128)S(1)}, u32[]{:S(2)}, u32[]{:S(2)}) collective-permute-start(f32[3,25,1,1024]{3,1,2,0:T(8,128)} %get-tuple-element.19), channel_id=1, source_target_pairs={{0,8},{8,16},{16,24},{24,32},{32,40},{40,48},{48,56},{56,64},{64,7... | collective-permute-start | bytes 921608 | tf_op jit(solution)/shard_map/ppermute | solution.py:18
  14.5 21.1 %collective-permute-start.1 = (f32[3,25,1,1024]{3,1,2,0:T(8,128)}, f32[3,25,1,1024]{3,1,2,0:T(8,128)}, u32[]{:S(2)}, u32[]{:S(2)}) collective-permute-start(f32[3,25,1,1024]{3,1,2,0:T(8,128)} %get-tuple-element.20), channel_id=1, source_target_pairs={{8,0},{16,8},{24,16},{32,24},{40,32},{48,40},{56,48},{64,56},{72,6... | collective-permute-start | bytes 921608 | tf_op jit(solution)/shard_map/ppermute | solution.py:19
  38.5 27.7 %collective-permute-start.6 = (f32[1,25,4,1024]{3,1,2,0:T(8,128)S(1)}, f32[1,25,4,1024]{3,1,2,0:T(8,128)S(1)}, u32[]{:S(2)}, u32[]{:S(2)}) collective-permute-start(f32[1,25,4,1024]{3,1,2,0:T(8,128)S(1)} %get-tuple-element.17), channel_id=1, source_target_pairs={{0,1},{1,2},{2,3},{3,4},{4,5},{5,6},{6,7},{7,0},{8,9},{9,10},{10,1... | collective-permute-start | bytes 1228808 | tf_op jit(solution)/shard_map/ppermute | solution.py:18
  40.4 25.7 %collective-permute-start.7 = (f32[1,25,4,1024]{3,1,2,0:T(8,128)S(1)}, f32[1,25,4,1024]{3,1,2,0:T(8,128)S(1)}, u32[]{:S(2)}, u32[]{:S(2)}) collective-permute-start(f32[1,25,4,1024]{3,1,2,0:T(8,128)S(1)} %get-tuple-element.18), channel_id=1, source_target_pairs={{1,0},{2,1},{3,2},{4,3},{5,4},{6,5},{7,6},{0,7},{9,8},{10,9},{11,1... | collective-permute-start | bytes 1228808 | tf_op jit(solution)/shard_map/ppermute | solution.py:19
  46.5 19.6 %collective-permute-start.4 = (f32[3,25,1,1024]{3,1,2,0:T(8,128)S(1)}, f32[3,25,1,1024]{3,1,2,0:T(8,128)S(1)}, u32[]{:S(2)}, u32[]{:S(2)}) collective-permute-start(f32[3,25,1,1024]{3,1,2,0:T(8,128)S(1)} %get-tuple-element.15), channel_id=1, source_target_pairs={{0,8},{8,16},{16,24},{24,32},{32,40},{40,48},{48,56},{56,64},{64,7... | collective-permute-start | bytes 921608 | tf_op jit(solution)/shard_map/ppermute | solution.py:18
  48.4 17.7 %collective-permute-start.5 = (f32[3,25,1,1024]{3,1,2,0:T(8,128)S(1)}, f32[3,25,1,1024]{3,1,2,0:T(8,128)S(1)}, u32[]{:S(2)}, u32[]{:S(2)}) collective-permute-start(f32[3,25,1,1024]{3,1,2,0:T(8,128)S(1)} %get-tuple-element.16), channel_id=1, source_target_pairs={{8,0},{16,8},{24,16},{32,24},{40,32},{48,40},{56,48},{64,56},{72,6... | collective-permute-start | bytes 921608 | tf_op jit(solution)/shard_map/ppermute | solution.py:19
  68.2 31.3 %collective-permute-start.10 = (f32[1,25,4,1024]{3,1,2,0:T(8,128)S(1)}, f32[1,25,4,1024]{3,1,2,0:T(8,128)S(1)}, u32[]{:S(2)}, u32[]{:S(2)}) collective-permute-start(f32[1,25,4,1024]{3,1,2,0:T(8,128)S(1)} %get-tuple-element.13), channel_id=1, source_target_pairs={{0,1},{1,2},{2,3},{3,4},{4,5},{5,6},{6,7},{7,0},{8,9},{9,10},{10,1... | collective-permute-start | bytes 1228808 | tf_op jit(solution)/shard_map/ppermute | solution.py:18
  70.1 29.4 %collective-permute-start.11 = (f32[1,25,4,1024]{3,1,2,0:T(8,128)S(1)}, f32[1,25,4,1024]{3,1,2,0:T(8,128)S(1)}, u32[]{:S(2)}, u32[]{:S(2)}) collective-permute-start(f32[1,25,4,1024]{3,1,2,0:T(8,128)S(1)} %get-tuple-element.14), channel_id=1, source_target_pairs={{1,0},{2,1},{3,2},{4,3},{5,4},{6,5},{7,6},{0,7},{9,8},{10,9},{11,1... | collective-permute-start | bytes 1228808 | tf_op jit(solution)/shard_map/ppermute | solution.py:19
  76.2 23.2 %collective-permute-start.8 = (f32[3,25,1,1024]{3,1,2,0:T(8,128)S(1)}, f32[3,25,1,1024]{3,1,2,0:T(8,128)S(1)}, u32[]{:S(2)}, u32[]{:S(2)}) collective-permute-start(f32[3,25,1,1024]{3,1,2,0:T(8,128)S(1)} %get-tuple-element.11), channel_id=1, source_target_pairs={{0,8},{8,16},{16,24},{24,32},{32,40},{40,48},{48,56},{56,64},{64,7... | collective-permute-start | bytes 921608 | tf_op jit(solution)/shard_map/ppermute | solution.py:18
  78.1 21.3 %collective-permute-start.9 = (f32[3,25,1,1024]{3,1,2,0:T(8,128)S(1)}, f32[3,25,1,1024]{3,1,2,0:T(8,128)S(1)}, u32[]{:S(2)}, u32[]{:S(2)}) collective-permute-start(f32[3,25,1,1024]{3,1,2,0:T(8,128)S(1)} %get-tuple-element.12), channel_id=1, source_target_pairs={{8,0},{16,8},{24,16},{32,24},{40,32},{48,40},{56,48},{64,56},{72,6... | collective-permute-start | bytes 921608 | tf_op jit(solution)/shard_map/ppermute | solution.py:19
  101.4 26.1 %collective-permute-start.14 = (f32[1,25,4,1024]{3,1,2,0:T(8,128)S(1)}, f32[1,25,4,1024]{3,1,2,0:T(8,128)S(1)}, u32[]{:S(2)}, u32[]{:S(2)}) collective-permute-start(f32[1,25,4,1024]{3,1,2,0:T(8,128)S(1)} %get-tuple-element.9), channel_id=1, source_target_pairs={{0,1},{1,2},{2,3},{3,4},{4,5},{5,6},{6,7},{7,0},{8,9},{9,10},{10,1... | collective-permute-start | bytes 1228808 | tf_op jit(solution)/shard_map/ppermute | solution.py:18
  103.4 24.2 %collective-permute-start.15 = (f32[1,25,4,1024]{3,1,2,0:T(8,128)S(1)}, f32[1,25,4,1024]{3,1,2,0:T(8,128)S(1)}, u32[]{:S(2)}, u32[]{:S(2)}) collective-permute-start(f32[1,25,4,1024]{3,1,2,0:T(8,128)S(1)} %get-tuple-element.10), channel_id=1, source_target_pairs={{1,0},{2,1},{3,2},{4,3},{5,4},{6,5},{7,6},{0,7},{9,8},{10,9},{11,1... | collective-permute-start | bytes 1228808 | tf_op jit(solution)/shard_map/ppermute | solution.py:19
  109.5 17.4 %collective-permute-start.12 = (f32[3,25,1,1024]{3,1,2,0:T(8,128)S(1)}, f32[3,25,1,1024]{3,1,2,0:T(8,128)S(1)}, u32[]{:S(2)}, u32[]{:S(2)}) collective-permute-start(f32[3,25,1,1024]{3,1,2,0:T(8,128)S(1)} %get-tuple-element.7), channel_id=1, source_target_pairs={{0,8},{8,16},{16,24},{24,32},{32,40},{40,48},{48,56},{56,64},{64,7... | collective-permute-start | bytes 921608 | tf_op jit(solution)/shard_map/ppermute | solution.py:18
  111.4 16.1 %collective-permute-start.13 = (f32[3,25,1,1024]{3,1,2,0:T(8,128)S(1)}, f32[3,25,1,1024]{3,1,2,0:T(8,128)S(1)}, u32[]{:S(2)}, u32[]{:S(2)}) collective-permute-start(f32[3,25,1,1024]{3,1,2,0:T(8,128)S(1)} %get-tuple-element.8), channel_id=1, source_target_pairs={{8,0},{16,8},{24,16},{32,24},{40,32},{48,40},{56,48},{64,56},{72,6... | collective-permute-start | bytes 921608 | tf_op jit(solution)/shard_map/ppermute | solution.py:19
  143.9 19.0 %all-to-all-start = ((f32[8,1,38400]{2,1,0:T(1,128)}), f32[8,1,38400]{2,1,0:T(1,128)S(1)}, u32[]{:S(2)}, u32[]{:S(2)}) async-start(f32[8,1,38400]{2,1,0:T(1,128)} %reshape.202), calls=%async_computation | async-start | bytes 2457600 | tf_op jit(solution)/shard_map/all_to_all | solution.py:94
where the time goes:
time: 209 us; the launch traced here: 208 us
  starting transfers between devices  69.8 us (33%)
  waiting for transfers between devices  61.8 us (30%)
  local copies, waits for them, and re-layouts  36.4 us (17%)
  blocking collectives  21.4 us (10%)
  other arithmetic  18.5 us (9%)
    ppermute x8, starting transfers between devices, extended(): after = lax.ppermute(leading, axis, down)  49.3 us
    ppermute x8, waiting for transfers between devices, extended(): before = lax.ppermute(last, axis, up)  46.7 us
    unnamed x2, local copies, waits for them, and re-layouts  21.5 us
    all_to_all x1, blocking collectives, on_device(): lax.all_to_all(result, 'spec', split_axis=0, concat_axis=3, tiled=True)  21.4 us
    ppermute x8, starting transfers between devices, extended(): before = lax.ppermute(last, axis, up)  16.8 us
    all_to_all x1, waiting for transfers between devices, on_device(): lax.all_to_all(action, 'spec', split_axis=3, concat_axis=0, tiled=True)  14.4 us
    mul x4, other arithmetic, combine(): return fresh * sea_rows  8.4 us
    all_to_all x2, local copies, waits for them, and re-layouts, on_device(): lax.all_to_all(action, 'spec', split_axis=3, concat_axis=0, tiled=True)  5.73 us
  transfers between devices with their start and end apart: 17, of which 6 were waited for; matrix products, arithmetic and copies ran while one was open for 2% of the time, Pallas kernels for 0%

commit v1 on v0

v1 whole, which is shorter than its diff:
```python
import functools

import jax
import jax.numpy as jnp
import numpy as np
from jax import lax
from jax.experimental import pallas as pl
from jax.experimental.pallas import tpu as pltpu
from jax.sharding import PartitionSpec as P

DIRS = 24
FREQS = 25
SUB = 4
INTERPRET = False

THETA = (np.float32(2.0 * np.pi) * np.arange(DIRS, dtype=np.float32) / np.float32(DIRS)).astype(
    np.float32
)
COS = np.cos(THETA).astype(np.float32)
SIN = np.sin(THETA).astype(np.float32)
FREQ = np.arange(FREQS, dtype=np.float64)
FR = (1.1 ** (FREQ - FREQS // 2)).astype(np.float32)
SPEED = (1.1 ** (-FREQ)).astype(np.float32)
RFAC = (np.float32(0.5) + np.float32(0.5) * SPEED).astype(np.float32)
CX = np.abs(np.float32(0.42) * SPEED[:, None] * COS[None, :]).astype(np.float32)
CY = np.abs(np.float32(0.42) * SPEED[:, None] * SIN[None, :]).astype(np.float32)
C0 = (1.0 - CX.astype(np.float64) - CY.astype(np.float64)).astype(np.float32)

LANES = 128
FULL = 3
TILES = FULL * 8 + 3
SLOTS = TILES + FULL + 2

SOUTH = [d for d in range(DIRS) if SIN[d] >= 0]
NORTH = [d for d in range(DIRS) if SIN[d] < 0]
REACH = SUB - 1
S_DIRS = [(SOUTH[0] - REACH + i) % DIRS for i in range(len(SOUTH) + 2 * REACH)]
N_DIRS = [(NORTH[0] - REACH + i) % DIRS for i in range(len(NORTH) + 2 * REACH)]
EXTRAS = []
for k in range(1, REACH + 1):
    EXTRAS += [
        ("s", (SOUTH[-1] + k) % DIRS, k),
        ("s", (SOUTH[0] - k) % DIRS, k),
        ("n", (NORTH[-1] + k) % DIRS, k),
        ("n", (NORTH[0] - k) % DIRS, k),
    ]
EXTRA_AT = {(w, d): i for i, (w, d, _) in enumerate(EXTRAS)}


def window(d):
    return "s" if d in SOUTH else "n"


def step_kernel(group, cx, cy, c0, rfac, frsq, own, south, north, sea, turn, out, st_a, st_b, ex_a, ex_b):
    me = group[0]
    f_of = lambda t: jnp.where(t < FULL * 8, me * FULL + t // 8, FREQS - 1)
    map_of = lambda t: jnp.where(t < FULL * 8, t % 8, t - FULL * 8 + 8)
    slot_of = lambda t: t + t // 8 + 1
    lane = lax.broadcasted_iota(jnp.int32, (8, LANES), 1)
    row = lax.broadcasted_iota(jnp.int32, (8, LANES), 0)
    first, last, mine = lane == 0, lane == LANES - 1, row >= 4
    zero = jnp.zeros((8, LANES), jnp.float32)
    pads = [i * 9 for i in range(FULL + 1)] + [SLOTS - 1]
    for p in pads:
        for d in range(DIRS):
            st_a[d, p] = zero
            st_b[d, p] = zero
        for i in range(len(EXTRAS)):
            ex_a[i, p] = zero
            ex_b[i, p] = zero

    def fill(t, carry):
        slot, m = slot_of(t), map_of(t)
        seas = {"s": sea[0, m], "n": sea[1, m]}
        halo = {"s": (south, S_DIRS), "n": (north, N_DIRS)}

        def whole(w, d):
            ref, dirs = halo[w]
            return jnp.concatenate([ref[dirs.index(d), t], own[d, t]], axis=0) * seas[w]

        for d in range(DIRS):
            st_a[d, slot] = whole(window(d), d)
        for i, (w, d, _) in enumerate(EXTRAS):
            ex_a[i, slot] = whole(w, d)
        return carry

    lax.fori_loop(0, TILES, fill, 0)

    def make(step, src, src_ex, dst, dst_ex):
        def body(t, carry):
            slot, m, f = slot_of(t), map_of(t), f_of(t)
            rf = rfac[f]
            seas = {"s": sea[0, m], "n": sea[1, m]}
            raw = {"s": turn[0, m], "n": turn[1, m]}
            mth = {w: jnp.abs(raw[w]) * rf for w in "sn"}
            ahead = {w: raw[w] > 0 for w in "sn"}
            loaded = {}

            def tile(w, d):
                d = d % DIRS
                key = (w, d)
                if window(d) == w or step == SUB - 1:
                    key = (window(d), d)
                if key not in loaded:
                    if key[0] == window(d):
                        loaded[key] = (src, d, src[d, slot])
                    else:
                        i = EXTRA_AT[key]
                        loaded[key] = (src_ex, i, src_ex[i, slot])
                return loaded[key]

            def update(w, d):
                ref, i, a = tile(w, d)
                before, after = tile(w, d - 1)[2], tile(w, d + 1)[2]
                if COS[d] >= 0:
                    x = jnp.where(first, pltpu.roll(ref[i, slot - 1], 1, 1), pltpu.roll(a, 1, 1))
                else:
                    x = jnp.where(
                        last,
                        pltpu.roll(ref[i, slot + 1], LANES - 1, 1),
                        pltpu.roll(a, LANES - 1, 1),
                    )
                y = pltpu.roll(a, 1 if SIN[d] >= 0 else 7, 0)
                turned = mth[w] * (jnp.where(ahead[w], before, after) - a)
                return (a * c0[f, d] + x * cx[f, d] + y * cy[f, d] + turned) * seas[w]

            fresh = {}
            total = None
            for d in range(DIRS):
                new = update(window(d), d)
                if step < SUB - 1:
                    fresh[d] = new
                    dst[d, slot] = new
                else:
                    total = new if total is None else total + new
                    keep(t, d, new)
            for i, (w, d, k) in enumerate(EXTRAS):
                if k < REACH - step:
                    dst_ex[i, slot] = jnp.where(mine, fresh[d], update(w, d))
            if total is not None:
                sums(t, f, total[4:8])
            return carry

        return body

    def keep(t, d, new):
        base = (d % 3) * FULL * 8

        @pl.when(t < FULL * 8)
        def _():
            out[d // 3, base + t] = new[4:8]

        @pl.when(t == FULL * 8 + 1)
        def _():
            out[d // 3, 3 * FULL * 8 + d % 3] = new[4:8]

    def sums(t, f, total):
        at = 3 * (FULL * 8 + 1)
        weighted = total * frsq[f]

        @pl.when(t < 8)
        def _():
            out[0, at + t] = total
            out[0, at + 8 + t] = weighted

        @pl.when(jnp.logical_and(t >= 8, t < FULL * 8))
        def _():
            out[0, at + t % 8] += total
            out[0, at + 8 + t % 8] += weighted

        @pl.when(t == FULL * 8 + 1)
        def _():
            out[0, at + me] += total
            out[0, at + 8 + me] += weighted

    bufs = [(st_a, ex_a), (st_b, ex_b)]
    for step in range(SUB):
        (src, src_ex), (dst, dst_ex) = bufs[step % 2], bufs[(step + 1) % 2]
        lax.fori_loop(0, TILES, make(step, src, src_ex, dst, dst_ex), 0)
    at = 3 * (FULL * 8 + 1)
    for i in range(16):
        value = out[0, at + i]
        for s in range(1, 8):
            out[s, at + i] = value


OUT_TILES = 3 * (FULL * 8 + 1) + 16


def step_call(group, own, south, north, sea, turn):
    smem = pl.BlockSpec(memory_space=pltpu.SMEM)
    vmem = pl.BlockSpec(memory_space=pltpu.VMEM)
    state = pltpu.VMEM((DIRS, SLOTS, 8, LANES), jnp.float32)
    extra = pltpu.VMEM((len(EXTRAS), SLOTS, 8, LANES), jnp.float32)
    return pl.pallas_call(
        step_kernel,
        out_shape=jax.ShapeDtypeStruct((8, OUT_TILES, 4, LANES), jnp.float32),
        in_specs=[smem] * 6 + [vmem] * 5,
        out_specs=vmem,
        scratch_shapes=[state, state, extra, extra],
        compiler_params=pltpu.CompilerParams(vmem_limit_bytes=40 * 1024 * 1024),
        interpret=INTERPRET,
        name="steps",
    )(group, CX, CY, C0, RFAC, FR * FR, own, south, north, sea, turn)


def source_kernel(cos, sin, got, wind_u, wind_v, out):
    at = 3 * (FULL * 8 + 1)
    inverse = 1.0 / (DIRS * FREQS)

    def body(t, carry):
        m0 = got[0, at + t]
        m2 = got[0, at + 8 + t]
        for j in range(1, 8):
            m0 = m0 + got[j, at + t]
            m2 = m2 + got[j, at + 8 + t]
        ratio = 0.5 * (m2 * inverse) / (1.0 + m0 * inverse)
        u, v = wind_u[t], wind_v[t]
        gain = [0.5 * jnp.maximum(u * cos[d] + v * sin[d], 0.0) for d in range(3)]
        for f in range(FREQS):
            fr = float(FR[f])
            shrink = 1.0 / (1.0 + ratio * (fr * fr))
            for d in range(3):
                if f < 8 * FULL:
                    a = got[f // FULL, (d * FULL + f % FULL) * 8 + t]
                else:
                    a = got[t, 3 * FULL * 8 + d]
                out[d, f, t] = a * (1.0 + gain[d] * fr) * shrink
        return carry

    lax.fori_loop(0, 8, body, 0)


def source_call(cos, sin, got, wind_u, wind_v):
    smem = pl.BlockSpec(memory_space=pltpu.SMEM)
    vmem = pl.BlockSpec(memory_space=pltpu.VMEM)
    return pl.pallas_call(
        source_kernel,
        out_shape=jax.ShapeDtypeStruct((3, FREQS, 8, 4, LANES), jnp.float32),
        in_specs=[smem] * 2 + [vmem] * 3,
        out_specs=vmem,
        compiler_params=pltpu.CompilerParams(vmem_limit_bytes=40 * 1024 * 1024),
        interpret=INTERPRET,
        name="source",
    )(cos, sin, got, wind_u, wind_v)


def tiled(rows):
    return jnp.swapaxes(rows.reshape(rows.shape[:-1] + (8, LANES)), -2, -3)


def on_device(spectrum, sea_mask, turning, wind_u, wind_v):
    me = lax.axis_index("spec")
    count = lax.axis_size("space")
    up = [(i, i + 1) for i in range(count - 1)]
    down = [(j, i) for i, j in up]

    maps = jnp.stack([tiled((sea_mask == 1).astype(jnp.float32)), tiled(turning)])
    maps_south = lax.ppermute(maps, "space", up)
    maps_north = lax.ppermute(maps, "space", down)

    x = tiled(spectrum)
    whole = x[:, : 8 * FULL].reshape(3, 8, FULL * 8, 4, LANES).transpose(1, 0, 2, 3, 4)
    lastf = jnp.pad(x[:, 8 * FULL], ((0, 0), (1, 1), (0, 0), (0, 0)))
    lastf = jnp.stack([lastf[:, j : j + 3] for j in range(8)])
    packed = jnp.concatenate([whole, lastf], axis=2)
    own = lax.all_to_all(packed, "spec", 0, 0, tiled=True).reshape(DIRS, TILES, 4, LANES)

    def pick(dirs):
        cut = next((i for i in range(1, len(dirs)) if dirs[i] < dirs[i - 1]), len(dirs))
        parts = [dirs[:cut], dirs[cut:]]
        return jnp.concatenate([own[p[0] : p[-1] + 1] for p in parts if p])

    south = lax.ppermute(pick(S_DIRS), "space", up)
    north = lax.ppermute(pick(N_DIRS), "space", down)

    pair = jnp.stack(
        [jnp.concatenate([maps_south, maps], axis=2), jnp.concatenate([maps_north, maps], axis=2)]
    )
    around = jnp.pad(pair, ((0, 0), (0, 0), (1, 1), (0, 0), (0, 0)))
    around = lax.dynamic_slice_in_dim(around, me, 3, axis=2)
    pair = jnp.concatenate([pair, around], axis=2)
    made = step_call(me.reshape(1), own, south, north, pair[:, 0], pair[:, 1])
    got = lax.all_to_all(made, "spec", 0, 0, tiled=True)
    cos = lax.dynamic_slice_in_dim(jnp.asarray(COS), me * 3, 3)
    sin = lax.dynamic_slice_in_dim(jnp.asarray(SIN), me * 3, 3)
    result = source_call(cos, sin, got, tiled(wind_u), tiled(wind_v))
    return jnp.swapaxes(result, -2, -3).reshape(3, FREQS, 4, 8 * LANES)


def solution(mesh):
    rows = P("space", None)
    bins = P("spec", None, "space", None)
    return jax.shard_map(
        on_device,
        mesh=mesh,
        in_specs=(bins, rows, rows, rows, rows),
        out_specs=bins,
        check_vma=False,
    )
```

time: 209 us -> 151 us (0.72)
  the two profiles are of different devices: /device:TPU:320 before, /device:TPU:448 now
where the time goes in v1:
time: 151 us; the launch traced here: 148 us
  Pallas kernels  66.1 us (44%)
  waiting for transfers between devices  34 us (23%)
  blocking collectives  24.2 us (16%)
  starting transfers between devices  17.5 us (12%)
  local copies, waits for them, and re-layouts  3.5 us (2%)
  other arithmetic  2.74 us (2%)
    pallas_call x1, Pallas kernels, step_call(): pl.pallas_call(step_kernel, out_shape=jax.ShapeDtypeStruct((8, OUT_TILES,...  63.9 us
    all_to_all x1, blocking collectives, on_device(): lax.all_to_all(packed, 'spec', 0, 0, tiled=True)  24.2 us
    ppermute x1, waiting for transfers between devices, on_device(): maps_south = lax.ppermute(maps, 'space', up)  18.7 us
    all_to_all x1, waiting for transfers between devices, on_device(): got = lax.all_to_all(made, 'spec', 0, 0, tiled=True)  15.3 us
    ppermute x1, starting transfers between devices, on_device(): maps_north = lax.ppermute(maps, 'space', down)  5.21 us
    all_to_all x1, starting transfers between devices, on_device(): got = lax.all_to_all(made, 'spec', 0, 0, tiled=True)  3.72 us
    ppermute x1, starting transfers between devices, on_device(): maps_south = lax.ppermute(maps, 'space', up)  3.36 us
    ppermute x1, starting transfers between devices, on_device(): north = lax.ppermute(pick(N_DIRS), 'space', down)  3.28 us
  transfers between devices with their start and end apart: 5, of which 2 were waited for; matrix products, arithmetic and copies ran while one was open for 1% of the time, Pallas kernels for 0%

profile of v1, /device:TPU:448, one launch (start us, length us, event | category | flops | bytes accessed | tf_op | source)
XLA Modules:
  0.0 148.4 jit_solution(4167472763571850862)
XLA Ops:
  0.0 1.8 %reshape.33 = f32[3,25,4,8,128]{4,3,2,1,0:T(8,128)S(1)} reshape(f32[3,25,4,1024]{3,2,1,0:T(4,128)} %param.12) | data formatting | bytes 2457600 | tf_op jit(solution)/shard_map/reshape | solution.py:249
  1.8 0.3 copy.20
  2.1 0.1 slice.86
  2.3 0.1 copy.15
  2.4 0.8 copy.21
  3.2 0.3 pad_maximum_fusion
  3.5 24.2 %all_to_all.10 = f32[8,3,27,4,128]{4,3,2,1,0:T(4,128)S(1)} all-to-all(f32[8,3,27,4,128]{4,3,2,1,0:T(4,128)S(1)} %pad_maximum_fusion), channel_id=1, replica_groups=mesh['space'=64,'spec'=8] {'spec'}, dimensions={0} | all-to-all | bytes 2654208 | tf_op jit(solution)/shard_map/all_to_all | solution.py:267
  27.7 0.2 fusion.18
  27.9 1.2 pad_maximum_fusion.2
  29.1 0.0 copy-start.8
  29.1 0.0 copy-start.7
  29.1 3.3 %collective-permute-start.1 = (f32[18,27,4,128]{3,2,1,0:T(4,128)}, f32[18,27,4,128]{3,2,1,0:T(4,128)S(1)}, u32[]{:S(2)}, u32[]{:S(2)}) collective-permute-start(f32[18,27,4,128]{3,2,1,0:T(4,128)} %pad_maximum_fusion.2), channel_id=1, source_target_pairs={{8,0},{16,8},{24,16},{32,24},{40,32},{48,40},{56,48},{64,56},{72,6... | collective-permute-start | bytes 2985992 | tf_op jit(solution)/shard_map/ppermute | solution.py:275
  32.4 0.0 copy-start.2
  32.4 0.0 copy-start.3
  32.4 0.0 copy-start.4
  32.4 0.0 copy-start.5
  32.5 0.0 copy-start.6
  32.5 1.2 pad_maximum_fusion.1
  33.6 1.9 %collective-permute-start = (f32[18,27,4,128]{3,2,1,0:T(4,128)}, f32[18,27,4,128]{3,2,1,0:T(4,128)S(1)}, u32[]{:S(2)}, u32[]{:S(2)}) collective-permute-start(f32[18,27,4,128]{3,2,1,0:T(4,128)} %pad_maximum_fusion.1), channel_id=1, source_target_pairs={{0,8},{8,16},{16,24},{24,32},{32,40},{40,48},{48,56},{56,64},{64,7... | collective-permute-start | bytes 2985992 | tf_op jit(solution)/shard_map/ppermute | solution.py:274
  35.6 0.0 copy-done.8
  35.6 0.0 copy-done.7
  35.6 3.4 %collective-permute-start.2 = (f32[2,8,4,128]{3,2,1,0:T(4,128)S(1)}, f32[2,8,4,128]{3,2,1,0:T(4,128)S(1)}, u32[]{:S(2)}, u32[]{:S(2)}) collective-permute-start(f32[2,8,4,128]{3,2,1,0:T(4,128)S(1)} %pad_maximum_fusion.5), channel_id=1, source_target_pairs={{0,8},{8,16},{16,24},{24,32},{32,40},{40,48},{48,56},{56,64},{64,7... | collective-permute-start | bytes 98312 | tf_op jit(solution)/shard_map/ppermute | solution.py:259
  39.0 5.2 %collective-permute-start.3 = (f32[2,8,4,128]{3,2,1,0:T(4,128)S(1)}, f32[2,8,4,128]{3,2,1,0:T(4,128)S(1)}, u32[]{:S(2)}, u32[]{:S(2)}) collective-permute-start(f32[2,8,4,128]{3,2,1,0:T(4,128)S(1)} %pad_maximum_fusion.5), channel_id=1, source_target_pairs={{8,0},{16,8},{24,16},{32,24},{40,32},{48,40},{56,48},{64,56},{72,6... | collective-permute-start | bytes 98312 | tf_op jit(solution)/shard_map/ppermute | solution.py:260
  44.2 18.7 %collective-permute-done.2 = f32[2,8,4,128]{3,2,1,0:T(4,128)S(1)} collective-permute-done((f32[2,8,4,128]{3,2,1,0:T(4,128)S(1)}, f32[2,8,4,128]{3,2,1,0:T(4,128)S(1)}, u32[]{:S(2)}, u32[]{:S(2)}) %collective-permute-start.2) | collective-permute-done | bytes 32800 | tf_op jit(solution)/shard_map/ppermute | solution.py:259
  62.9 0.0 collective-permute-done.3
  63.0 0.0 collective-permute-done.1.north
  63.0 0.0 collective-permute-done.south
  63.0 0.0 copy-done.2
  63.0 0.0 copy-done.3
  63.0 0.0 copy-done.4
  63.1 0.0 copy-done.5
  63.1 0.0 copy-done.6
  63.1 63.9 %steps.1 = f32[8,91,4,128]{3,2,1,0:T(4,128)} custom-call(s32[1]{0:T(128)} %bitcast.group, f32[25,24]{1,0:T(8,128)S(1)} %copy-done.2, f32[25,24]{1,0:T(8,128)S(1)} %copy-done.3, f32[25,24]{1,0:T(8,128)S(1)} %copy-done.4, f32[25]{0:T(128)S(1)} %copy-done.5, f32[25]{0:T(128)S(1)} %copy-done.6, f32[24,27,4,128]{3,2,1,0:T(4,128)S(1)} %bitcast.79, ...), custom_call_target="tpu_custom_call" | custom-call | tf_op jit(solution)/shard_map/steps/pallas_call | solution.py:195
  127.0 0.0 copy-start.10
  127.0 0.0 copy-start.9
  127.0 0.0 copy-start
  127.0 0.0 copy-start.1
  127.0 3.7 %all-to-all-start.1 = ((f32[8,91,4,128]{3,2,1,0:T(4,128)}), f32[8,91,4,128]{3,2,1,0:T(4,128)S(1)}, u32[]{:S(2)}, u32[]{:S(2)}) async-start(f32[8,91,4,128]{3,2,1,0:T(4,128)} %steps.1), calls=%async_computation.1 | async-start | bytes 2981888 | tf_op jit(solution)/shard_map/all_to_all | solution.py:284
  130.8 0.0 copy-done.10
  130.8 0.1 dynamic_slice.10.sin
  130.8 0.0 copy-done.9
  130.9 0.1 dynamic_slice.9.cos
  130.9 15.3 %all-to-all-done.1.got = f32[8,91,4,128]{3,2,1,0:T(4,128)S(1)} async-done(((f32[8,91,4,128]{3,2,1,0:T(4,128)}), f32[8,91,4,128]{3,2,1,0:T(4,128)S(1)}, u32[]{:S(2)}, u32[]{:S(2)}) %all-to-all-start.1) | async-done | bytes 1490976 | tf_op jit(solution)/shard_map/all_to_all | solution.py:284
  146.2 0.0 copy-done
  146.2 0.0 copy-done.1
  146.2 2.2 %source.1 = f32[3,25,8,4,128]{4,3,2,1,0:T(4,128)} custom-call(f32[3]{0:T(128)S(1)} %dynamic_slice.9.cos, f32[3]{0:T(128)S(1)} %dynamic_slice.10.sin, f32[8,91,4,128]{3,2,1,0:T(4,128)S(1)} %all-to-all-done.1.got, f32[8,4,128]{2,1,0:T(4,128)S(1)} %bitcast.80, f32[8,4,128]{2,1,0:T(4,128)S(1)} %bitcast.81), custom_call_target="tpu_custom_call" | custom-call | tf_op jit(solution)/shard_map/source/pallas_call | solution.py:237
  (16 shorter events, 0.2 us)
Async XLA Ops:
  29.1 6.4 %copy-start.8 = (s32[4,1024]{1,0:T(4,128)S(1)}, s32[4,1024]{1,0:T(4,128)}, u32[]{:S(2)}) copy-start(s32[4,1024]{1,0:T(4,128)} %param.13) | copy-start | bytes 49156
  29.1 6.5 %copy-start.7 = (f32[4,1024]{1,0:T(4,128)S(1)}, f32[4,1024]{1,0:T(4,128)}, u32[]{:S(2)}) copy-start(f32[4,1024]{1,0:T(4,128)} %param.14) | copy-start | bytes 49156
  29.1 33.9 %collective-permute-start.1 = (f32[18,27,4,128]{3,2,1,0:T(4,128)}, f32[18,27,4,128]{3,2,1,0:T(4,128)S(1)}, u32[]{:S(2)}, u32[]{:S(2)}) collective-permute-start(f32[18,27,4,128]{3,2,1,0:T(4,128)} %pad_maximum_fusion.2), channel_id=1, source_target_pairs={{8,0},{16,8},{24,16},{32,24},{40,32},{48,40},{56,48},{64,56},{72,6... | collective-permute-start | bytes 2985992 | tf_op jit(solution)/shard_map/ppermute | solution.py:275
  32.4 30.6 %copy-start.2 = (f32[25,24]{1,0:T(8,128)S(1)}, f32[25,24]{1,0:T(8,128)}, u32[]{:S(2)}) copy-start(f32[25,24]{1,0:T(8,128)} %constant.30.clone.cx) | copy-start | bytes 7204
  32.4 30.6 %copy-start.3 = (f32[25,24]{1,0:T(8,128)S(1)}, f32[25,24]{1,0:T(8,128)}, u32[]{:S(2)}) copy-start(f32[25,24]{1,0:T(8,128)} %constant.31.clone.cy) | copy-start | bytes 7204
  32.4 30.6 %copy-start.4 = (f32[25,24]{1,0:T(8,128)S(1)}, f32[25,24]{1,0:T(8,128)}, u32[]{:S(2)}) copy-start(f32[25,24]{1,0:T(8,128)} %constant.32.clone.c0) | copy-start | bytes 7204
  32.4 30.6 %copy-start.5 = (f32[25]{0:T(128)S(1)}, f32[25]{0:T(128)}, u32[]{:S(2)}) copy-start(f32[25]{0:T(128)} %constant.33.clone.rfac) | copy-start | bytes 304
  32.5 30.6 %copy-start.6 = (f32[25]{0:T(128)S(1)}, f32[25]{0:T(128)}, u32[]{:S(2)}) copy-start(f32[25]{0:T(128)} %constant.34.clone.frsq) | copy-start | bytes 304
  33.6 29.4 %collective-permute-start = (f32[18,27,4,128]{3,2,1,0:T(4,128)}, f32[18,27,4,128]{3,2,1,0:T(4,128)S(1)}, u32[]{:S(2)}, u32[]{:S(2)}) collective-permute-start(f32[18,27,4,128]{3,2,1,0:T(4,128)} %pad_maximum_fusion.1), channel_id=1, source_target_pairs={{0,8},{8,16},{16,24},{24,32},{32,40},{40,48},{48,56},{56,64},{64,7... | collective-permute-start | bytes 2985992 | tf_op jit(solution)/shard_map/ppermute | solution.py:274
  35.6 27.3 %collective-permute-start.2 = (f32[2,8,4,128]{3,2,1,0:T(4,128)S(1)}, f32[2,8,4,128]{3,2,1,0:T(4,128)S(1)}, u32[]{:S(2)}, u32[]{:S(2)}) collective-permute-start(f32[2,8,4,128]{3,2,1,0:T(4,128)S(1)} %pad_maximum_fusion.5), channel_id=1, source_target_pairs={{0,8},{8,16},{16,24},{24,32},{32,40},{40,48},{48,56},{56,64},{64,7... | collective-permute-start | bytes 98312 | tf_op jit(solution)/shard_map/ppermute | solution.py:259
  39.0 23.9 %collective-permute-start.3 = (f32[2,8,4,128]{3,2,1,0:T(4,128)S(1)}, f32[2,8,4,128]{3,2,1,0:T(4,128)S(1)}, u32[]{:S(2)}, u32[]{:S(2)}) collective-permute-start(f32[2,8,4,128]{3,2,1,0:T(4,128)S(1)} %pad_maximum_fusion.5), channel_id=1, source_target_pairs={{8,0},{16,8},{24,16},{32,24},{40,32},{48,40},{56,48},{64,56},{72,6... | collective-permute-start | bytes 98312 | tf_op jit(solution)/shard_map/ppermute | solution.py:260
  127.0 3.7 %copy-start.10 = (f32[24]{0:T(128)S(1)}, f32[24]{0:T(128)}, u32[]{:S(2)}) copy-start(f32[24]{0:T(128)} %constant.36.clone) | copy-start | bytes 292
  127.0 3.8 %copy-start.9 = (f32[24]{0:T(128)S(1)}, f32[24]{0:T(128)}, u32[]{:S(2)}) copy-start(f32[24]{0:T(128)} %constant.35.clone) | copy-start | bytes 292
  127.0 19.2 %copy-start = (f32[4,1024]{1,0:T(4,128)S(1)}, f32[4,1024]{1,0:T(4,128)}, u32[]{:S(2)}) copy-start(f32[4,1024]{1,0:T(4,128)} %param.15) | copy-start | bytes 49156
  127.0 19.2 %copy-start.1 = (f32[4,1024]{1,0:T(4,128)S(1)}, f32[4,1024]{1,0:T(4,128)}, u32[]{:S(2)}) copy-start(f32[4,1024]{1,0:T(4,128)} %param.16) | copy-start | bytes 49156
  127.0 19.2 %all-to-all-start.1 = ((f32[8,91,4,128]{3,2,1,0:T(4,128)}), f32[8,91,4,128]{3,2,1,0:T(4,128)S(1)}, u32[]{:S(2)}, u32[]{:S(2)}) async-start(f32[8,91,4,128]{3,2,1,0:T(4,128)} %steps.1), calls=%async_computation.1 | async-start | bytes 2981888 | tf_op jit(solution)/shard_map/all_to_all | solution.py:284

commit v2 on v1

--- a/solution.py
+++ b/solution.py
@@ -53,8 +53,17 @@
 
 def step_kernel(group, cx, cy, c0, rfac, frsq, own, south, north, sea, turn, out, st_a, st_b, ex_a, ex_b):
     me = group[0]
-    f_of = lambda t: jnp.where(t < FULL * 8, me * FULL + t // 8, FREQS - 1)
-    map_of = lambda t: jnp.where(t < FULL * 8, t % 8, t - FULL * 8 + 8)
+
+    def f_of(t):
+        if isinstance(t, int):
+            return FREQS - 1
+        return jnp.where(t < FULL * 8, me * FULL + t // 8, FREQS - 1)
+
+    def map_of(t):
+        if isinstance(t, int):
+            return t - FULL * 8 + 8
+        return jnp.where(t < FULL * 8, t % 8, t - FULL * 8 + 8)
+
     slot_of = lambda t: t + t // 8 + 1
     lane = lax.broadcasted_iota(jnp.int32, (8, LANES), 1)
     row = lax.broadcasted_iota(jnp.int32, (8, LANES), 0)
@@ -143,41 +152,31 @@
 
         return body
 
+    at = 3 * (FULL * 8 + 1)
+
     def keep(t, d, new):
-        base = (d % 3) * FULL * 8
-
-        @pl.when(t < FULL * 8)
-        def _():
-            out[d // 3, base + t] = new[4:8]
-
-        @pl.when(t == FULL * 8 + 1)
-        def _():
+        if isinstance(t, int):
             out[d // 3, 3 * FULL * 8 + d % 3] = new[4:8]
+        else:
+            out[d // 3, (d % 3) * FULL * 8 + t] = new[4:8]
 
     def sums(t, f, total):
-        at = 3 * (FULL * 8 + 1)
-        weighted = total * frsq[f]
-
-        @pl.when(t < 8)
-        def _():
-            out[0, at + t] = total
-            out[0, at + 8 + t] = weighted
-
-        @pl.when(jnp.logical_and(t >= 8, t < FULL * 8))
-        def _():
-            out[0, at + t % 8] += total
-            out[0, at + 8 + t % 8] += weighted
-
-        @pl.when(t == FULL * 8 + 1)
-        def _():
-            out[0, at + me] += total
-            out[0, at + 8 + me] += weighted
+        place = me if isinstance(t, int) else t % 8
+        out[0, at + place] += total
+        out[0, at + 8 + place] += total * frsq[f]
+
+    for i in range(16):
+        out[0, at + i] = jnp.zeros((4, LANES), jnp.float32)
 
     bufs = [(st_a, ex_a), (st_b, ex_b)]
     for step in range(SUB):
         (src, src_ex), (dst, dst_ex) = bufs[step % 2], bufs[(step + 1) % 2]
-        lax.fori_loop(0, TILES, make(step, src, src_ex, dst, dst_ex), 0)
-    at = 3 * (FULL * 8 + 1)
+        body = make(step, src, src_ex, dst, dst_ex)
+        if step < SUB - 1:
+            lax.fori_loop(0, TILES, body, 0)
+        else:
+            lax.fori_loop(0, FULL * 8, body, 0)
+            body(FULL * 8 + 1, 0)
     for i in range(16):
         value = out[0, at + i]
         for s in range(1, 8):

time: 151 us -> 104 us (0.69)
  the two profiles are of different devices: /device:TPU:448 before, /device:TPU:248 now
where the time goes in v2:
time: 104 us
  waiting for transfers between devices  37.9 us (36%)
  blocking collectives  23.2 us (22%)
  Pallas kernels  19.8 us (19%)
  starting transfers between devices  16.4 us (16%)
  local copies, waits for them, and re-layouts  3.5 us (3%)
  other arithmetic  2.74 us (3%)
    all_to_all x1, blocking collectives, on_device(): lax.all_to_all(packed, 'spec', 0, 0, tiled=True)  23.2 us
    all_to_all x1, waiting for transfers between devices, on_device(): got = lax.all_to_all(made, 'spec', 0, 0, tiled=True)  19.8 us
    ppermute x1, waiting for transfers between devices, on_device(): maps_south = lax.ppermute(maps, 'space', up)  18.1 us
    pallas_call x1, Pallas kernels, step_call(): pl.pallas_call(step_kernel, out_shape=jax.ShapeDtypeStruct((8, OUT_TILES,...  17.7 us
    ppermute x1, starting transfers between devices, on_device(): maps_south = lax.ppermute(maps, 'space', up)  5.69 us
    all_to_all x1, starting transfers between devices, on_device(): got = lax.all_to_all(made, 'spec', 0, 0, tiled=True)  4.36 us
    concatenate x2, other arithmetic, pick(): return jnp.concatenate([own[p[0]:p[-1] + 1] for p in parts if p])  2.35 us
    ppermute x1, starting transfers between devices, on_device(): south = lax.ppermute(pick(S_DIRS), 'space', up)  2.34 us
  transfers between devices with their start and end apart: 5, of which 2 were waited for; matrix products, arithmetic and copies ran while one was open for 1% of the time, Pallas kernels for 0%

profile of v2, /device:TPU:248, one launch (start us, length us, event | category | flops | bytes accessed | tf_op | source)
XLA Modules:
  0.0 103.9 jit_solution(1753656222154923612)
XLA Ops:
  0.0 1.8 %reshape.33 = f32[3,25,4,8,128]{4,3,2,1,0:T(8,128)S(1)} reshape(f32[3,25,4,1024]{3,2,1,0:T(4,128)} %param.12) | data formatting | bytes 2457600 | tf_op jit(solution)/shard_map/reshape | solution.py:248
  1.8 0.3 copy.20
  2.1 0.1 slice.86
  2.3 0.1 copy.15
  2.4 0.8 copy.21
  3.2 0.3 pad_maximum_fusion
  3.5 23.2 %all_to_all.10 = f32[8,3,27,4,128]{4,3,2,1,0:T(4,128)S(1)} all-to-all(f32[8,3,27,4,128]{4,3,2,1,0:T(4,128)S(1)} %pad_maximum_fusion), channel_id=1, replica_groups=mesh['space'=64,'spec'=8] {'spec'}, dimensions={0} | all-to-all | bytes 2654208 | tf_op jit(solution)/shard_map/all_to_all | solution.py:266
  26.7 0.2 fusion.18
  26.9 1.2 %pad_maximum_fusion.2 = f32[18,27,4,128]{3,2,1,0:T(4,128)} fusion(f32[3,27,4,128]{3,2,1,0:T(4,128)S(1)} %get-tuple-element.7, f32[15,27,4,128]{3,2,1,0:T(4,128)S(1)} %bitcast.87), kind=kLoop, calls=%fused_computation.4 | loop fusion | flops 248832 | bytes 1990656 | tf_op jit(solution)/shard_map/concatenate | solution.py:271
  28.1 0.0 copy-start.8
  28.1 0.0 copy-start.7
  28.1 2.1 %collective-permute-start.1 = (f32[18,27,4,128]{3,2,1,0:T(4,128)}, f32[18,27,4,128]{3,2,1,0:T(4,128)S(1)}, u32[]{:S(2)}, u32[]{:S(2)}) collective-permute-start(f32[18,27,4,128]{3,2,1,0:T(4,128)} %pad_maximum_fusion.2), channel_id=1, source_target_pairs={{8,0},{16,8},{24,16},{32,24},{40,32},{48,40},{56,48},{64,56},{72,6... | collective-permute-start | bytes 2985992 | tf_op jit(solution)/shard_map/ppermute | solution.py:274
  30.2 0.0 copy-start.2
  30.2 0.0 copy-start.3
  30.2 0.0 copy-start.4
  30.2 0.0 copy-start.5
  30.3 0.0 copy-start.6
  30.3 1.2 %pad_maximum_fusion.1 = f32[18,27,4,128]{3,2,1,0:T(4,128)} fusion(f32[15,27,4,128]{3,2,1,0:T(4,128)S(1)} %bitcast.86, f32[3,27,4,128]{3,2,1,0:T(4,128)S(1)} %get-tuple-element.8), kind=kLoop, calls=%fused_computation.3 | loop fusion | flops 248832 | bytes 1990656 | tf_op jit(solution)/shard_map/concatenate | solution.py:271
  31.4 2.3 %collective-permute-start = (f32[18,27,4,128]{3,2,1,0:T(4,128)}, f32[18,27,4,128]{3,2,1,0:T(4,128)S(1)}, u32[]{:S(2)}, u32[]{:S(2)}) collective-permute-start(f32[18,27,4,128]{3,2,1,0:T(4,128)} %pad_maximum_fusion.1), channel_id=1, source_target_pairs={{0,8},{8,16},{16,24},{24,32},{32,40},{40,48},{48,56},{56,64},{64,7... | collective-permute-start | bytes 2985992 | tf_op jit(solution)/shard_map/ppermute | solution.py:273
  33.8 0.0 copy-done.8
  33.8 0.0 copy-done.7
  33.8 5.7 %collective-permute-start.2 = (f32[2,8,4,128]{3,2,1,0:T(4,128)S(1)}, f32[2,8,4,128]{3,2,1,0:T(4,128)S(1)}, u32[]{:S(2)}, u32[]{:S(2)}) collective-permute-start(f32[2,8,4,128]{3,2,1,0:T(4,128)S(1)} %pad_maximum_fusion.5), channel_id=1, source_target_pairs={{0,8},{8,16},{16,24},{24,32},{32,40},{40,48},{48,56},{56,64},{64,7... | collective-permute-start | bytes 98312 | tf_op jit(solution)/shard_map/ppermute | solution.py:258
  39.5 1.9 %collective-permute-start.3 = (f32[2,8,4,128]{3,2,1,0:T(4,128)S(1)}, f32[2,8,4,128]{3,2,1,0:T(4,128)S(1)}, u32[]{:S(2)}, u32[]{:S(2)}) collective-permute-start(f32[2,8,4,128]{3,2,1,0:T(4,128)S(1)} %pad_maximum_fusion.5), channel_id=1, source_target_pairs={{8,0},{16,8},{24,16},{32,24},{40,32},{48,40},{56,48},{64,56},{72,6... | collective-permute-start | bytes 98312 | tf_op jit(solution)/shard_map/ppermute | solution.py:259
  41.5 18.1 %collective-permute-done.2 = f32[2,8,4,128]{3,2,1,0:T(4,128)S(1)} collective-permute-done((f32[2,8,4,128]{3,2,1,0:T(4,128)S(1)}, f32[2,8,4,128]{3,2,1,0:T(4,128)S(1)}, u32[]{:S(2)}, u32[]{:S(2)}) %collective-permute-start.2) | collective-permute-done | bytes 32800 | tf_op jit(solution)/shard_map/ppermute | solution.py:258
  59.5 0.0 collective-permute-done.3
  59.6 0.0 collective-permute-done.1.north
  59.7 0.0 collective-permute-done.south
  59.7 0.0 copy-done.2
  59.7 0.0 copy-done.3
  59.7 0.0 copy-done.4
  59.7 0.0 copy-done.5
  59.7 0.0 copy-done.6
  59.7 17.7 %steps.1 = f32[8,91,4,128]{3,2,1,0:T(4,128)} custom-call(s32[1]{0:T(128)} %bitcast.group, f32[25,24]{1,0:T(8,128)S(1)} %copy-done.2, f32[25,24]{1,0:T(8,128)S(1)} %copy-done.3, f32[25,24]{1,0:T(8,128)S(1)} %copy-done.4, f32[25]{0:T(128)S(1)} %copy-done.5, f32[25]{0:T(128)S(1)} %copy-done.6, f32[24,27,4,128]{3,2,1,0:T(4,128)S(1)} %bitcast.79, ...), custom_call_target="tpu_custom_call" | custom-call | tf_op jit(solution)/shard_map/steps/pallas_call | solution.py:194
  77.4 0.0 copy-start.10
  77.4 0.0 copy-start.9
  77.4 0.0 copy-start
  77.4 0.0 copy-start.1
  77.4 4.4 %all-to-all-start.1 = ((f32[8,91,4,128]{3,2,1,0:T(4,128)}), f32[8,91,4,128]{3,2,1,0:T(4,128)S(1)}, u32[]{:S(2)}, u32[]{:S(2)}) async-start(f32[8,91,4,128]{3,2,1,0:T(4,128)} %steps.1), calls=%async_computation.1 | async-start | bytes 2981888 | tf_op jit(solution)/shard_map/all_to_all | solution.py:283
  81.7 0.0 copy-done.10
  81.7 0.1 dynamic_slice.10.sin
  81.8 0.0 copy-done.9
  81.8 0.1 dynamic_slice.9.cos
  81.9 19.8 %all-to-all-done.1.got = f32[8,91,4,128]{3,2,1,0:T(4,128)S(1)} async-done(((f32[8,91,4,128]{3,2,1,0:T(4,128)}), f32[8,91,4,128]{3,2,1,0:T(4,128)S(1)}, u32[]{:S(2)}, u32[]{:S(2)}) %all-to-all-start.1) | async-done | bytes 1490976 | tf_op jit(solution)/shard_map/all_to_all | solution.py:283
  101.7 0.0 copy-done
  101.7 0.0 copy-done.1
  101.7 2.2 %source.1 = f32[3,25,8,4,128]{4,3,2,1,0:T(4,128)} custom-call(f32[3]{0:T(128)S(1)} %dynamic_slice.9.cos, f32[3]{0:T(128)S(1)} %dynamic_slice.10.sin, f32[8,91,4,128]{3,2,1,0:T(4,128)S(1)} %all-to-all-done.1.got, f32[8,4,128]{2,1,0:T(4,128)S(1)} %bitcast.80, f32[8,4,128]{2,1,0:T(4,128)S(1)} %bitcast.81), custom_call_target="tpu_custom_call" | custom-call | tf_op jit(solution)/shard_map/source/pallas_call | solution.py:236
  (16 shorter events, 0.2 us)
Async XLA Ops:
  28.1 5.7 %copy-start.8 = (s32[4,1024]{1,0:T(4,128)S(1)}, s32[4,1024]{1,0:T(4,128)}, u32[]{:S(2)}) copy-start(s32[4,1024]{1,0:T(4,128)} %param.13) | copy-start | bytes 49156
  28.1 5.7 %copy-start.7 = (f32[4,1024]{1,0:T(4,128)S(1)}, f32[4,1024]{1,0:T(4,128)}, u32[]{:S(2)}) copy-start(f32[4,1024]{1,0:T(4,128)} %param.14) | copy-start | bytes 49156
  28.1 31.5 %collective-permute-start.1 = (f32[18,27,4,128]{3,2,1,0:T(4,128)}, f32[18,27,4,128]{3,2,1,0:T(4,128)S(1)}, u32[]{:S(2)}, u32[]{:S(2)}) collective-permute-start(f32[18,27,4,128]{3,2,1,0:T(4,128)} %pad_maximum_fusion.2), channel_id=1, source_target_pairs={{8,0},{16,8},{24,16},{32,24},{40,32},{48,40},{56,48},{64,56},{72,6... | collective-permute-start | bytes 2985992 | tf_op jit(solution)/shard_map/ppermute | solution.py:274
  30.2 29.5 %copy-start.2 = (f32[25,24]{1,0:T(8,128)S(1)}, f32[25,24]{1,0:T(8,128)}, u32[]{:S(2)}) copy-start(f32[25,24]{1,0:T(8,128)} %constant.30.clone.cx) | copy-start | bytes 7204
  30.2 29.5 %copy-start.3 = (f32[25,24]{1,0:T(8,128)S(1)}, f32[25,24]{1,0:T(8,128)}, u32[]{:S(2)}) copy-start(f32[25,24]{1,0:T(8,128)} %constant.31.clone.cy) | copy-start | bytes 7204
  30.2 29.5 %copy-start.4 = (f32[25,24]{1,0:T(8,128)S(1)}, f32[25,24]{1,0:T(8,128)}, u32[]{:S(2)}) copy-start(f32[25,24]{1,0:T(8,128)} %constant.32.clone.c0) | copy-start | bytes 7204
  30.2 29.5 %copy-start.5 = (f32[25]{0:T(128)S(1)}, f32[25]{0:T(128)}, u32[]{:S(2)}) copy-start(f32[25]{0:T(128)} %constant.33.clone.rfac) | copy-start | bytes 304
  30.3 29.5 %copy-start.6 = (f32[25]{0:T(128)S(1)}, f32[25]{0:T(128)}, u32[]{:S(2)}) copy-start(f32[25]{0:T(128)} %constant.34.clone.frsq) | copy-start | bytes 304
  31.4 28.2 %collective-permute-start = (f32[18,27,4,128]{3,2,1,0:T(4,128)}, f32[18,27,4,128]{3,2,1,0:T(4,128)S(1)}, u32[]{:S(2)}, u32[]{:S(2)}) collective-permute-start(f32[18,27,4,128]{3,2,1,0:T(4,128)} %pad_maximum_fusion.1), channel_id=1, source_target_pairs={{0,8},{8,16},{16,24},{24,32},{32,40},{40,48},{48,56},{56,64},{64,7... | collective-permute-start | bytes 2985992 | tf_op jit(solution)/shard_map/ppermute | solution.py:273
  33.8 25.7 %collective-permute-start.2 = (f32[2,8,4,128]{3,2,1,0:T(4,128)S(1)}, f32[2,8,4,128]{3,2,1,0:T(4,128)S(1)}, u32[]{:S(2)}, u32[]{:S(2)}) collective-permute-start(f32[2,8,4,128]{3,2,1,0:T(4,128)S(1)} %pad_maximum_fusion.5), channel_id=1, source_target_pairs={{0,8},{8,16},{16,24},{24,32},{32,40},{40,48},{48,56},{56,64},{64,7... | collective-permute-start | bytes 98312 | tf_op jit(solution)/shard_map/ppermute | solution.py:258
  39.5 20.0 %collective-permute-start.3 = (f32[2,8,4,128]{3,2,1,0:T(4,128)S(1)}, f32[2,8,4,128]{3,2,1,0:T(4,128)S(1)}, u32[]{:S(2)}, u32[]{:S(2)}) collective-permute-start(f32[2,8,4,128]{3,2,1,0:T(4,128)S(1)} %pad_maximum_fusion.5), channel_id=1, source_target_pairs={{8,0},{16,8},{24,16},{32,24},{40,32},{48,40},{56,48},{64,56},{72,6... | collective-permute-start | bytes 98312 | tf_op jit(solution)/shard_map/ppermute | solution.py:259
  77.4 4.4 %copy-start.10 = (f32[24]{0:T(128)S(1)}, f32[24]{0:T(128)}, u32[]{:S(2)}) copy-start(f32[24]{0:T(128)} %constant.36.clone) | copy-start | bytes 292
  77.4 4.5 %copy-start.9 = (f32[24]{0:T(128)S(1)}, f32[24]{0:T(128)}, u32[]{:S(2)}) copy-start(f32[24]{0:T(128)} %constant.35.clone) | copy-start | bytes 292
  77.4 24.4 %copy-start = (f32[4,1024]{1,0:T(4,128)S(1)}, f32[4,1024]{1,0:T(4,128)}, u32[]{:S(2)}) copy-start(f32[4,1024]{1,0:T(4,128)} %param.15) | copy-start | bytes 49156
  77.4 24.4 %copy-start.1 = (f32[4,1024]{1,0:T(4,128)S(1)}, f32[4,1024]{1,0:T(4,128)}, u32[]{:S(2)}) copy-start(f32[4,1024]{1,0:T(4,128)} %param.16) | copy-start | bytes 49156
  77.4 24.3 %all-to-all-start.1 = ((f32[8,91,4,128]{3,2,1,0:T(4,128)}), f32[8,91,4,128]{3,2,1,0:T(4,128)S(1)}, u32[]{:S(2)}, u32[]{:S(2)}) async-start(f32[8,91,4,128]{3,2,1,0:T(4,128)} %steps.1), calls=%async_computation.1 | async-start | bytes 2981888 | tf_op jit(solution)/shard_map/all_to_all | solution.py:283

commit v3 on v2

v3 whole, which is shorter than its diff:
```python
import functools

import jax
import jax.numpy as jnp
import numpy as np
from jax import lax
from jax.experimental import pallas as pl
from jax.experimental.pallas import tpu as pltpu
from jax.sharding import PartitionSpec as P

DIRS = 24
FREQS = 25
SUB = 4
INTERPRET = False
LANES = 128
BLOCKS = 8

THETA = (np.float32(2.0 * np.pi) * np.arange(DIRS, dtype=np.float32) / np.float32(DIRS)).astype(
    np.float32
)
COS = np.cos(THETA).astype(np.float32)
SIN = np.sin(THETA).astype(np.float32)
FREQ = np.arange(FREQS, dtype=np.float64)
FR = (1.1 ** (FREQ - FREQS // 2)).astype(np.float32)
SPEED = (1.1 ** (-FREQ)).astype(np.float32)
RFAC = (np.float32(0.5) + np.float32(0.5) * SPEED).astype(np.float32)


def grouped(values):
    kept, place = [], []
    for v in values:
        near = [i for i, k in enumerate(kept) if abs(k - v) <= 4e-7 * abs(k)]
        if not near:
            kept.append(float(v))
        place.append(near[0] if near else len(kept) - 1)
    return kept, place


WEIGHTS, PLACE = grouped(np.abs(np.concatenate([COS, SIN])).astype(np.float64))
KX, KY = PLACE[:DIRS], PLACE[DIRS:]
REST, K0 = grouped([WEIGHTS[KX[d]] + WEIGHTS[KY[d]] for d in range(DIRS)])
COEF = np.concatenate(
    [
        0.42 * SPEED.astype(np.float64)[:, None] * np.array(WEIGHTS)[None, :],
        1.0 - 0.42 * SPEED.astype(np.float64)[:, None] * np.array(REST)[None, :],
    ],
    axis=1,
).astype(np.float32)

FULL = 3
CHUNKS = ((0, 2, False), (2, 1, True))

SOUTH = [d for d in range(DIRS) if SIN[d] >= 0]
NORTH = [d for d in range(DIRS) if SIN[d] < 0]
REACH = SUB - 1
PLANES = len(SOUTH) + REACH
EXTRAS = []
for k in range(1, REACH + 1):
    EXTRAS += [
        ("s", (SOUTH[-1] + k) % DIRS, k),
        ("s", (SOUTH[0] - k) % DIRS, k),
        ("n", (NORTH[-1] + k) % DIRS, k),
        ("n", (NORTH[0] - k) % DIRS, k),
    ]
EXTRA_AT = {(w, d): i for i, (w, d, _) in enumerate(EXTRAS)}
VMEM_LIMIT = 40 * 1024 * 1024


def window(d):
    return "s" if d in SOUTH else "n"


def tiles_of(chunk):
    return chunk[1] * BLOCKS + (3 if chunk[2] else 0)


def slots_of(chunk):
    return tiles_of(chunk) + chunk[1] + (2 if chunk[2] else 1)


def made_of(chunk):
    return 3 * (chunk[1] * BLOCKS + (1 if chunk[2] else 0))


def smem():
    return pl.BlockSpec(memory_space=pltpu.SMEM)


def vmem():
    return pl.BlockSpec(memory_space=pltpu.VMEM)


def call(kernel, name, out, args, n_smem, scratch=(), cost=4_000_000):
    return pl.pallas_call(
        kernel,
        out_shape=jax.tree.map(lambda s: jax.ShapeDtypeStruct(s, jnp.float32), out, is_leaf=lambda s: isinstance(s, tuple) and isinstance(s[0], int)),
        in_specs=[smem()] * n_smem + [vmem()] * (len(args) - n_smem),
        out_specs=jax.tree.map(lambda s: vmem(), out, is_leaf=lambda s: isinstance(s, tuple) and isinstance(s[0], int)),
        scratch_shapes=list(scratch),
        compiler_params=pltpu.CompilerParams(vmem_limit_bytes=VMEM_LIMIT),
        cost_estimate=pl.CostEstimate(flops=1000, bytes_accessed=cost, transcendentals=0),
        interpret=INTERPRET,
        name=name,
    )(*args)


def pack_kernel(x, *outs):
    zero = jnp.zeros((4, LANES), jnp.float32)
    for (first, count, tail), out in zip(CHUNKS, outs):
        for d in range(3):
            for j in range(BLOCKS):
                for i in range(count):
                    for l in range(BLOCKS):
                        f = j * FULL + first + i
                        out[j, d, i * BLOCKS + l] = x[d, f, :, l * LANES : (l + 1) * LANES]
                if tail:
                    for i in range(3):
                        l = j + i - 1
                        inside = 0 <= l < BLOCKS
                        value = x[d, FREQS - 1, :, l * LANES : (l + 1) * LANES] if inside else zero
                        out[j, d, count * BLOCKS + i] = value


def halo_kernel(tiles, with_maps, *refs):
    if with_maps:
        own, maps, up, down = refs
        for k in range(2):
            for l in range(BLOCKS):
                value = maps[k, :, l * LANES : (l + 1) * LANES]
                up[PLANES * tiles + k * BLOCKS + l] = value
                down[PLANES * tiles + k * BLOCKS + l] = value
    else:
        own, up, down = refs
    ends = {
        "s": (SOUTH[-1], SOUTH[0]),
        "n": (NORTH[0], NORTH[-1]),
    }
    n = len(SOUTH)

    def body(t, carry):
        for i, d in enumerate(SOUTH):
            up[i * tiles + t] = own[d, t]
        for i, d in enumerate(NORTH):
            down[i * tiles + t] = own[d, t]
        top, low = ends["s"]
        a = [own[(top + k) % DIRS, t] for k in range(1, 4)]
        b = [own[(low - k) % DIRS, t] for k in range(1, 4)]
        up[n * tiles + t] = jnp.concatenate([a[2][3:4], a[0][1:4]], axis=0)
        up[(n + 1) * tiles + t] = jnp.concatenate([b[1][2:4], a[1][2:4]], axis=0)
        up[(n + 2) * tiles + t] = jnp.concatenate([b[2][3:4], b[0][1:4]], axis=0)
        low, top = ends["n"]
        a = [own[(low - k) % DIRS, t] for k in range(1, 4)]
        b = [own[(top + k) % DIRS, t] for k in range(1, 4)]
        down[n * tiles + t] = jnp.concatenate([a[0][0:3], a[2][0:1]], axis=0)
        down[(n + 1) * tiles + t] = jnp.concatenate([a[1][0:2], b[1][0:2]], axis=0)
        down[(n + 2) * tiles + t] = jnp.concatenate([b[0][0:3], b[2][0:1]], axis=0)
        return carry

    lax.fori_loop(0, tiles, body, 0)


def step_kernel(chunk, first_call, group, coef, rfac, frsq, own, south, north, *refs):
    begin, count, tail = chunk
    tiles, slots, made = tiles_of(chunk), slots_of(chunk), made_of(chunk)
    if first_call:
        maps, out, around, sums, st_a, st_b, ex_a, ex_b = refs
    else:
        around, given, out, st_a, st_b, ex_a, ex_b = refs
        sums = None
    me = group[0]
    whole = count * BLOCKS

    def f_of(t):
        if isinstance(t, int):
            return FREQS - 1
        f = me * FULL + begin + t // BLOCKS
        return jnp.where(t < whole, f, FREQS - 1) if tail else f

    def map_of(t):
        if isinstance(t, int):
            return me + t - whole
        l = t % BLOCKS + 1
        return jnp.where(t < whole, l, me + t - whole) if tail else l

    def slot_of(t):
        return t + t // BLOCKS + 1

    lane = lax.broadcasted_iota(jnp.int32, (8, LANES), 1)
    row = lax.broadcasted_iota(jnp.int32, (8, LANES), 0)
    start, end, mine = lane == 0, lane == LANES - 1, row < 4
    zero = jnp.zeros((8, LANES), jnp.float32)
    for p in [i * (BLOCKS + 1) for i in range(count + 1)] + ([slots - 1] if tail else []):
        for d in range(DIRS):
            st_a[d, p] = zero
            st_b[d, p] = zero
        for i in range(len(EXTRAS)):
            ex_a[i, p] = zero
            ex_b[i, p] = zero

    if first_call:
        at = PLANES * tiles
        for k in range(2):
            for w, ref in enumerate((south, north)):
                around[k, w, 0] = zero
                around[k, w, BLOCKS + 1] = zero
                for l in range(BLOCKS):
                    mid = maps[k, :, l * LANES : (l + 1) * LANES]
                    around[k, w, l + 1] = jnp.concatenate([mid, ref[at + k * BLOCKS + l]], axis=0)

    def fill(t, carry):
        slot, m = slot_of(t), map_of(t)
        seas = {"s": around[0, 0, m], "n": around[0, 1, m]}
        n = len(SOUTH)

        def whole_tile(w, d, rows):
            return jnp.concatenate([own[d, t], rows], axis=0) * seas[w]

        for i, d in enumerate(SOUTH):
            st_a[d, slot] = whole_tile("s", d, south[i * tiles + t])
        for i, d in enumerate(NORTH):
            st_a[d, slot] = whole_tile("n", d, north[i * tiles + t])
        for w, ref in (("s", south), ("n", north)):
            a, b, c = (ref[(n + i) * tiles + t] for i in range(3))
            swap = jnp.concatenate([b[2:4], b[0:2]], axis=0)
            pick = slice(0, 1) if w == "s" else slice(3, 4)
            far_a = jnp.broadcast_to(a[pick], (4, LANES))
            far_c = jnp.broadcast_to(c[pick], (4, LANES))
            if w == "s":
                top, low = SOUTH[-1], SOUTH[0]
                line = [(top + 1, a), (top + 2, b), (top + 3, far_a)]
                line += [(low - 1, c), (low - 2, swap), (low - 3, far_c)]
            else:
                low, top = NORTH[0], NORTH[-1]
                line = [(low - 1, a), (low - 2, b), (low - 3, far_a)]
                line += [(top + 1, c), (top + 2, swap), (top + 3, far_c)]
            for d, rows in line:
                ex_a[EXTRA_AT[w, d % DIRS], slot] = whole_tile(w, d % DIRS, rows)
        return carry

    lax.fori_loop(0, tiles, fill, 0)

    if first_call:
        for i in range(2 * BLOCKS):
            sums[i] = jnp.zeros((4, LANES), jnp.float32)
    else:
        for i in range(2 * BLOCKS):
            out[0, made + i] = given[i]

    def keep(t, d, new):
        if isinstance(t, int):
            out[d // 3, 3 * whole + d % 3] = new[0:4]
        else:
            out[d // 3, (d % 3) * whole + t] = new[0:4]

    def add_up(t, f, total):
        place = me if isinstance(t, int) else t % BLOCKS
        total = total[0:4]
        if first_call:
            sums[place] += total
            sums[BLOCKS + place] += total * frsq[f]
        else:
            out[0, made + place] += total
            out[0, made + BLOCKS + place] += total * frsq[f]

    def make(step, src, src_ex, dst, dst_ex):
        def body(t, carry):
            slot, m, f = slot_of(t), map_of(t), f_of(t)
            rf = rfac[f]
            coefs = [coef[f, i] for i in range(COEF.shape[1])]
            seas = {"s": around[0, 0, m], "n": around[0, 1, m]}
            raw = {"s": around[1, 0, m], "n": around[1, 1, m]}
            mth = {w: jnp.abs(raw[w]) * rf for w in "sn"}
            ahead = {w: raw[w] > 0 for w in "sn"}
            loaded = {}

            def tile(w, d):
                d = d % DIRS
                key = (w, d)
                if window(d) == w or step == SUB - 1:
                    key = (window(d), d)
                if key not in loaded:
                    if key[0] == window(d):
                        loaded[key] = (src, d, src[d, slot])
                    else:
                        i = EXTRA_AT[key]
                        loaded[key] = (src_ex, i, src_ex[i, slot])
                return loaded[key]

            def update(w, d):
                ref, i, a = tile(w, d)
                before, after = tile(w, d - 1)[2], tile(w, d + 1)[2]
                if COS[d] >= 0:
                    x = pltpu.roll(jnp.where(end, ref[i, slot - 1], a), 1, 1)
                else:
                    x = pltpu.roll(jnp.where(start, ref[i, slot + 1], a), LANES - 1, 1)
                y = pltpu.roll(a, 1 if SIN[d] >= 0 else 7, 0)
                turned = mth[w] * (jnp.where(ahead[w], before, after) - a)
                stay = coefs[len(WEIGHTS) + K0[d]]
                return (a * stay + x * coefs[KX[d]] + y * coefs[KY[d]] + turned) * seas[w]

            fresh = {}
            total = None
            for d in range(DIRS):
                new = update(window(d), d)
                if step < SUB - 1:
                    fresh[d] = new
                    dst[d, slot] = new
                else:
                    keep(t, d, new)
                    total = new if total is None else total + new
            for i, (w, d, k) in enumerate(EXTRAS):
                if k < REACH - step:
                    dst_ex[i, slot] = jnp.where(mine, fresh[d], update(w, d))
            if total is not None:
                add_up(t, f, total)
            return carry

        return body

    bufs = [(st_a, ex_a), (st_b, ex_b)]
    for step in range(SUB):
        (src, src_ex), (dst, dst_ex) = bufs[step % 2], bufs[(step + 1) % 2]
        body = make(step, src, src_ex, dst, dst_ex)
        if step < SUB - 1:
            lax.fori_loop(0, tiles, body, 0)
        else:
            lax.fori_loop(0, whole, body, 0)
            if tail:
                body(whole + 1, 0)
    if not first_call:
        for i in range(2 * BLOCKS):
            value = out[0, made + i]
            for s in range(1, BLOCKS):
                out[s, made + i] = value


def step_call(chunk, first_call, group, own, south, north, rest):
    slots, made = slots_of(chunk), made_of(chunk)
    state = pltpu.VMEM((DIRS, slots, 8, LANES), jnp.float32)
    extra = pltpu.VMEM((len(EXTRAS), slots, 8, LANES), jnp.float32)
    if first_call:
        out = [(BLOCKS, made, 4, LANES), (2, 2, BLOCKS + 2, 8, LANES), (2 * BLOCKS, 4, LANES)]
    else:
        out = [(BLOCKS, made + 2 * BLOCKS, 4, LANES)]
    args = (group, COEF, RFAC, FR * FR, own, south, north, *rest)
    return call(
        functools.partial(step_kernel, chunk, first_call),
        "steps",
        out,
        args,
        4,
        [state, state, extra, extra],
        20_000_000,
    )


def source_kernel(cos, sin, *refs):
    gots, (wind_u, wind_v, out) = refs[: len(CHUNKS)], refs[len(CHUNKS) :]
    last = gots[-1]
    at = made_of(CHUNKS[-1])
    inverse = 1.0 / (DIRS * FREQS)

    for t in range(BLOCKS):
        cols = slice(t * LANES, (t + 1) * LANES)
        m0 = last[0, at + t]
        m2 = last[0, at + BLOCKS + t]
        for j in range(1, BLOCKS):
            m0 = m0 + last[j, at + t]
            m2 = m2 + last[j, at + BLOCKS + t]
        ratio = 0.5 * (m2 * inverse) / (1.0 + m0 * inverse)
        u, v = wind_u[:, cols], wind_v[:, cols]
        gain = [0.5 * jnp.maximum(u * cos[d] + v * sin[d], 0.0) for d in range(3)]
        for (first, count, tail), got in zip(CHUNKS, gots):
            where = [
                (j * FULL + first + i, j, i * BLOCKS + t, count * BLOCKS)
                for j in range(BLOCKS)
                for i in range(count)
            ]
            if tail:
                where.append((FREQS - 1, t, 3 * count * BLOCKS, 1))
            for f, j, base, stride in where:
                fr = float(FR[f])
                shrink = 1.0 / (1.0 + ratio * (fr * fr))
                for d in range(3):
                    out[d, f, :, cols] = got[j, base + d * stride] * (1.0 + gain[d] * fr) * shrink


def on_device(spectrum, sea_mask, turning, wind_u, wind_v):
    me = lax.axis_index("spec")
    group = me.reshape(1)
    count = lax.axis_size("space")
    up = [(i, i + 1) for i in range(count - 1)]
    down = [(j, i) for i, j in up]

    maps = jnp.stack([(sea_mask == 1).astype(jnp.float32), turning])
    packs = call(
        pack_kernel,
        "pack",
        [(BLOCKS, 3, tiles_of(c), 4, LANES) for c in CHUNKS],
        (spectrum,),
        0,
    )
    rows = []
    hold = None
    for i, chunk in enumerate(CHUNKS):
        tiles = tiles_of(chunk)
        pack = packs[i]
        if hold is not None:
            pack, hold = lax.optimization_barrier((pack, hold))
            rows[-1] = (rows[-1][0],) + tuple(hold)
        own = lax.all_to_all(pack, "spec", 0, 0, tiled=True).reshape(DIRS, tiles, 4, LANES)
        size = PLANES * tiles + (2 * BLOCKS if i == 0 else 0)
        args = (own, maps) if i == 0 else (own,)
        edges = call(
            functools.partial(halo_kernel, tiles, i == 0), "halo", [(size, 4, LANES)] * 2, args, 0
        )
        rows.append((own, edges[0], edges[1]))
        hold = (edges[0], edges[1])
    (own, u, d), (own_2, u_2, d_2) = rows
    south, north = lax.ppermute(u, "space", up), lax.ppermute(d, "space", down)
    south, north, _, _ = lax.optimization_barrier((south, north, u_2, d_2))
    south_2, north_2 = lax.ppermute(u_2, "space", up), lax.ppermute(d_2, "space", down)
    rows = [(own, south, north), (own_2, south_2, north_2)]

    made, around, sums = step_call(CHUNKS[0], True, group, *rows[0], (maps,))
    made, south_2, north_2 = lax.optimization_barrier((made, south_2, north_2))
    gots = [lax.all_to_all(made, "spec", 0, 0, tiled=True)]
    (made,) = step_call(CHUNKS[1], False, group, own_2, south_2, north_2, (around, sums))
    made, gots = lax.optimization_barrier((made, gots))
    gots.append(lax.all_to_all(made, "spec", 0, 0, tiled=True))
    cos = lax.dynamic_slice_in_dim(jnp.asarray(COS), me * 3, 3)
    sin = lax.dynamic_slice_in_dim(jnp.asarray(SIN), me * 3, 3)
    return call(
        source_kernel,
        "source",
        (3, FREQS, 4, BLOCKS * LANES),
        (cos, sin, *gots, wind_u, wind_v),
        2,
    )


def solution(mesh):
    rows = P("space", None)
    bins = P("spec", None, "space", None)
    return jax.shard_map(
        on_device,
        mesh=mesh,
        in_specs=(bins, rows, rows, rows, rows),
        out_specs=bins,
        check_vma=False,
    )
```

time: 104 us -> 91.8 us (0.88)
  the two profiles are of different devices: /device:TPU:248 before, /device:TPU:448 now
where the time goes in v3:
time: 91.8 us; the launch traced here: 90.5 us
  starting transfers between devices  34.9 us (38%)
  waiting for transfers between devices  32.7 us (36%)
  Pallas kernels  21.4 us (23%)
  local copies, waits for them, and re-layouts  1.47 us (2%)
    pallas_call x6, Pallas kernels, call(): pl.pallas_call(kernel, out_shape=jax.tree.map(lambda s: jax.ShapeDtypeStr...  21.4 us
    all_to_all x2, waiting for transfers between devices, on_device(): lax.all_to_all(pack, 'spec', 0, 0, tiled=True)  13.1 us
    all_to_all x1, waiting for transfers between devices, on_device(): gots.append(lax.all_to_all(made, 'spec', 0, 0, tiled=True))  11.2 us
    all_to_all x2, starting transfers between devices, on_device(): lax.all_to_all(pack, 'spec', 0, 0, tiled=True)  8.95 us
    ppermute x1, starting transfers between devices, on_device(): lax.ppermute(d, 'space', down)  6.65 us
    ppermute x1, starting transfers between devices, on_device(): lax.ppermute(d_2, 'space', down)  6.65 us
    all_to_all x1, waiting for transfers between devices, on_device(): gots = [lax.all_to_all(made, 'spec', 0, 0, tiled=True)]  6.37 us
    all_to_all x1, starting transfers between devices, on_device(): gots = [lax.all_to_all(made, 'spec', 0, 0, tiled=True)]  4.83 us
  transfers between devices with their start and end apart: 8, of which 5 were waited for; matrix products, arithmetic and copies ran while one was open for 0% of the time, Pallas kernels for 19%

profile of v3, /device:TPU:448, one launch (start us, length us, event | category | flops | bytes accessed | tf_op | source)
XLA Modules:
  0.0 90.5 jit_solution(11181865762049618910)
XLA Ops:
  0.0 0.0 copy-start
  0.0 1.3 %copy-done = f32[3,25,4,1024]{3,2,1,0:T(4,128)S(1)} copy-done((f32[3,25,4,1024]{3,2,1,0:T(4,128)S(1)}, f32[3,25,4,1024]{3,2,1,0:T(4,128)}, u32[]{:S(2)}) %copy-start) | copy-done | bytes 1228824
  1.3 0.0 copy-start.6
  1.3 0.0 copy-start.7
  1.3 1.1 %pack.1 = (f32[8,3,16,4,128]{4,3,2,1,0:T(4,128)}, f32[8,3,11,4,128]{4,3,2,1,0:T(4,128)}) custom-call(f32[3,25,4,1024]{3,2,1,0:T(4,128)S(1)} %copy-done), custom_call_target="tpu_custom_call" | custom-call | flops 1000 | bytes 4000000 | tf_op jit(solution)/shard_map/pack/pallas_call | solution.py:94
  2.4 5.3 %all-to-all-start = ((f32[8,3,16,4,128]{4,3,2,1,0:T(4,128)}), f32[8,3,16,4,128]{4,3,2,1,0:T(4,128)S(1)}, u32[]{:S(2)}, u32[]{:S(2)}) async-start(f32[8,3,16,4,128]{4,3,2,1,0:T(4,128)} %get-tuple-element.25), calls=%async_computation | async-start | bytes 1572864 | tf_op jit(solution)/shard_map/all_to_all | solution.py:411
  7.8 0.0 copy-done.6
  7.8 0.0 copy-done.7
  7.8 11.9 %all-to-all-done = f32[8,3,16,4,128]{4,3,2,1,0:T(4,128)S(1)} async-done(((f32[8,3,16,4,128]{4,3,2,1,0:T(4,128)}), f32[8,3,16,4,128]{4,3,2,1,0:T(4,128)S(1)}, u32[]{:S(2)}, u32[]{:S(2)}) %all-to-all-start) | async-done | bytes 786464 | tf_op jit(solution)/shard_map/all_to_all | solution.py:411
  19.7 0.0 copy-start.1
  19.7 0.0 copy-start.4
  19.8 0.0 copy-start.5
  19.8 1.3 %halo.2 = (f32[256,4,128]{2,1,0:T(4,128)}, f32[256,4,128]{2,1,0:T(4,128)}) custom-call(f32[24,16,4,128]{3,2,1,0:T(4,128)S(1)} %bitcast.6, f32[2,4,1024]{2,1,0:T(4,128)S(1)} %pad_maximum_fusion.refs_1_.refs_0_), custom_call_target="tpu_custom_call" | custom-call | flops 1000 | bytes 4000000 | tf_op jit(solution)/shard_map/halo/pallas_call | solution.py:94
  21.0 3.6 %all-to-all-start.1 = ((f32[8,3,11,4,128]{4,3,2,1,0:T(4,128)}), f32[8,3,11,4,128]{4,3,2,1,0:T(4,128)S(1)}, u32[]{:S(2)}, u32[]{:S(2)}) async-start(f32[8,3,11,4,128]{4,3,2,1,0:T(4,128)} %get-tuple-element.28), calls=%async_computation.1 | async-start | bytes 1081344 | tf_op jit(solution)/shard_map/all_to_all | solution.py:411
  24.7 1.9 %collective-permute-start = (f32[256,4,128]{2,1,0:T(4,128)}, f32[256,4,128]{2,1,0:T(4,128)S(1)}, u32[]{:S(2)}, u32[]{:S(2)}) collective-permute-start(f32[256,4,128]{2,1,0:T(4,128)} %get-tuple-element.29), channel_id=1, source_target_pairs={{0,8},{8,16},{16,24},{24,32},{32,40},{40,48},{48,56},{56,64},{64,7... | collective-permute-start | bytes 1572872 | tf_op jit(solution)/shard_map/ppermute | solution.py:420
  26.6 6.7 %collective-permute-start.1 = (f32[256,4,128]{2,1,0:T(4,128)}, f32[256,4,128]{2,1,0:T(4,128)S(1)}, u32[]{:S(2)}, u32[]{:S(2)}) collective-permute-start(f32[256,4,128]{2,1,0:T(4,128)} %get-tuple-element.30), channel_id=1, source_target_pairs={{8,0},{16,8},{24,16},{32,24},{40,32},{48,40},{56,48},{64,56},{72,6... | collective-permute-start | bytes 1572872 | tf_op jit(solution)/shard_map/ppermute | solution.py:420
  33.2 1.2 %all-to-all-done.1 = f32[8,3,11,4,128]{4,3,2,1,0:T(4,128)S(1)} async-done(((f32[8,3,11,4,128]{4,3,2,1,0:T(4,128)}), f32[8,3,11,4,128]{4,3,2,1,0:T(4,128)S(1)}, u32[]{:S(2)}, u32[]{:S(2)}) %all-to-all-start.1) | async-done | bytes 540704 | tf_op jit(solution)/shard_map/all_to_all | solution.py:411
  34.4 1.0 %halo.3 = (f32[165,4,128]{2,1,0:T(4,128)}, f32[165,4,128]{2,1,0:T(4,128)}) custom-call(f32[24,11,4,128]{3,2,1,0:T(4,128)S(1)} %bitcast.8), custom_call_target="tpu_custom_call" | custom-call | flops 1000 | bytes 4000000 | tf_op jit(solution)/shard_map/halo/pallas_call | solution.py:94
  35.4 1.9 %collective-permute-start.2 = (f32[165,4,128]{2,1,0:T(4,128)}, f32[165,4,128]{2,1,0:T(4,128)S(1)}, u32[]{:S(2)}, u32[]{:S(2)}) collective-permute-start(f32[165,4,128]{2,1,0:T(4,128)} %get-tuple-element.31), channel_id=1, source_target_pairs={{0,8},{8,16},{16,24},{24,32},{32,40},{40,48},{48,56},{56,64},{64,7... | collective-permute-start | bytes 1013768 | tf_op jit(solution)/shard_map/ppermute | solution.py:422
  37.4 6.7 %collective-permute-start.3 = (f32[165,4,128]{2,1,0:T(4,128)}, f32[165,4,128]{2,1,0:T(4,128)S(1)}, u32[]{:S(2)}, u32[]{:S(2)}) collective-permute-start(f32[165,4,128]{2,1,0:T(4,128)} %get-tuple-element.32), channel_id=1, source_target_pairs={{8,0},{16,8},{24,16},{32,24},{40,32},{48,40},{56,48},{64,56},{72,6... | collective-permute-start | bytes 1013768 | tf_op jit(solution)/shard_map/ppermute | solution.py:422
  44.0 1.9 %collective-permute-done.south = f32[256,4,128]{2,1,0:T(4,128)S(1)} collective-permute-done((f32[256,4,128]{2,1,0:T(4,128)}, f32[256,4,128]{2,1,0:T(4,128)S(1)}, u32[]{:S(2)}, u32[]{:S(2)}) %collective-permute-start) | collective-permute-done | bytes 524320 | tf_op jit(solution)/shard_map/ppermute | solution.py:420
  45.9 0.0 collective-permute-done.1.north
  45.9 0.0 copy-done.1
  45.9 0.0 copy-done.4
  45.9 0.0 copy-done.5
  45.9 9.2 %steps.2 = (f32[8,48,4,128]{3,2,1,0:T(4,128)}, f32[2,2,10,8,128]{4,3,2,1,0:T(8,128)S(1)}, f32[16,4,128]{2,1,0:T(4,128)S(1)}) custom-call(s32[1]{0:T(128)} %bitcast.group, f32[25,18]{1,0:T(8,128)S(1)} %copy-done.1, f32[25]{0:T(128)S(1)} %copy-done.4, f32[25]{0:T(128)S(1)} %copy-done.5, f32[24,16,4,128]{3,2,1,0:T(4,128)S(1)} %bitcast.7, ...), custom_call_target="tpu_custom_call" | custom-call | flops 1000 | bytes 20000000 | tf_op jit(solution)/shard_map/steps/pallas_call | solution.py:94
  55.2 0.0 collective-permute-done.2.south
  55.2 0.0 collective-permute-done.3.north
  55.2 4.8 %all-to-all-start.2 = ((f32[8,48,4,128]{3,2,1,0:T(4,128)}), f32[8,48,4,128]{3,2,1,0:T(4,128)S(1)}, u32[]{:S(2)}, u32[]{:S(2)}) async-start(f32[8,48,4,128]{3,2,1,0:T(4,128)} %get-tuple-element.40), calls=%async_computation.2 | async-start | bytes 1572864 | tf_op jit(solution)/shard_map/all_to_all | solution.py:427
  60.0 6.6 %steps.3 = f32[8,43,4,128]{3,2,1,0:T(4,128)} custom-call(s32[1]{0:T(128)} %bitcast.group, f32[25,18]{1,0:T(8,128)S(1)} %copy-done.1, f32[25]{0:T(128)S(1)} %copy-done.4, f32[25]{0:T(128)S(1)} %copy-done.5, f32[24,11,4,128]{3,2,1,0:T(4,128)S(1)} %bitcast.9, f32[165,4,128]{2,1,0:T(4,128)S(1)} %collective-permute-done.2.south, ...), custom_call_target="tpu_custom_call" | custom-call | flops 1000 | bytes 20000000 | tf_op jit(solution)/shard_map/steps/pallas_call | solution.py:94
  66.6 0.0 copy-start.9
  66.6 0.0 copy-start.8
  66.6 0.0 copy-start.2
  66.6 0.0 copy-start.3
  66.6 6.4 %all-to-all-done.2.refs_0_ = f32[8,48,4,128]{3,2,1,0:T(4,128)S(1)} async-done(((f32[8,48,4,128]{3,2,1,0:T(4,128)}), f32[8,48,4,128]{3,2,1,0:T(4,128)S(1)}, u32[]{:S(2)}, u32[]{:S(2)}) %all-to-all-start.2) | async-done | bytes 786464 | tf_op jit(solution)/shard_map/all_to_all | solution.py:427
  73.0 4.0 %all-to-all-start.3 = ((f32[8,43,4,128]{3,2,1,0:T(4,128)}), f32[8,43,4,128]{3,2,1,0:T(4,128)S(1)}, u32[]{:S(2)}, u32[]{:S(2)}) async-start(f32[8,43,4,128]{3,2,1,0:T(4,128)} %steps.3), calls=%async_computation.3 | async-start | bytes 1409024 | tf_op jit(solution)/shard_map/all_to_all | solution.py:430
  77.0 0.0 copy-done.9
  77.0 0.1 dynamic_slice.6.cos
  77.0 0.0 copy-done.8
  77.0 0.1 dynamic_slice.7.sin
  77.1 11.2 %all-to-all-done.3.refs_1_ = f32[8,43,4,128]{3,2,1,0:T(4,128)S(1)} async-done(((f32[8,43,4,128]{3,2,1,0:T(4,128)}), f32[8,43,4,128]{3,2,1,0:T(4,128)S(1)}, u32[]{:S(2)}, u32[]{:S(2)}) %all-to-all-start.3) | async-done | bytes 704544 | tf_op jit(solution)/shard_map/all_to_all | solution.py:430
  88.4 0.0 copy-done.2
  88.4 0.0 copy-done.3
  88.4 2.1 %source.1 = f32[3,25,4,1024]{3,2,1,0:T(4,128)} custom-call(f32[3]{0:T(128)S(1)} %dynamic_slice.6.cos, f32[3]{0:T(128)S(1)} %dynamic_slice.7.sin, f32[8,48,4,128]{3,2,1,0:T(4,128)S(1)} %all-to-all-done.2.refs_0_, f32[8,43,4,128]{3,2,1,0:T(4,128)S(1)} %all-to-all-done.3.refs_1_, f32[4,1024]{1,0:T(4,128)S(1)} %copy-done.2, f32[4,1024]{1,0:T(4,128)S(1)} %copy-done.3), custom_call_target="tpu_custom_call" | custom-call | flops 1000 | bytes 4000000 | tf_op jit(solution)/shard_map/source/pallas_call | solution.py:94
  (2 shorter events, 0.0 us)
Async XLA Ops:
  0.0 1.3 %copy-start = (f32[3,25,4,1024]{3,2,1,0:T(4,128)S(1)}, f32[3,25,4,1024]{3,2,1,0:T(4,128)}, u32[]{:S(2)}) copy-start(f32[3,25,4,1024]{3,2,1,0:T(4,128)} %x.1) | copy-start | bytes 3686404
  1.3 6.5 %copy-start.6 = (s32[4,1024]{1,0:T(4,128)S(1)}, s32[4,1024]{1,0:T(4,128)}, u32[]{:S(2)}) copy-start(s32[4,1024]{1,0:T(4,128)} %param.12) | copy-start | bytes 49156
  1.3 6.5 %copy-start.7 = (f32[4,1024]{1,0:T(4,128)S(1)}, f32[4,1024]{1,0:T(4,128)}, u32[]{:S(2)}) copy-start(f32[4,1024]{1,0:T(4,128)} %param.13) | copy-start | bytes 49156
  2.4 17.3 %all-to-all-start = ((f32[8,3,16,4,128]{4,3,2,1,0:T(4,128)}), f32[8,3,16,4,128]{4,3,2,1,0:T(4,128)S(1)}, u32[]{:S(2)}, u32[]{:S(2)}) async-start(f32[8,3,16,4,128]{4,3,2,1,0:T(4,128)} %get-tuple-element.25), calls=%async_computation | async-start | bytes 1572864 | tf_op jit(solution)/shard_map/all_to_all | solution.py:411
  19.7 26.2 %copy-start.1 = (f32[25,18]{1,0:T(8,128)S(1)}, f32[25,18]{1,0:T(8,128)}, u32[]{:S(2)}) copy-start(f32[25,18]{1,0:T(8,128)} %constant.22.clone.coef) | copy-start | bytes 5404
  19.7 26.2 %copy-start.4 = (f32[25]{0:T(128)S(1)}, f32[25]{0:T(128)}, u32[]{:S(2)}) copy-start(f32[25]{0:T(128)} %constant.23.clone.rfac) | copy-start | bytes 304
  19.8 26.2 %copy-start.5 = (f32[25]{0:T(128)S(1)}, f32[25]{0:T(128)}, u32[]{:S(2)}) copy-start(f32[25]{0:T(128)} %constant.24.clone.frsq) | copy-start | bytes 304
  21.0 13.4 %all-to-all-start.1 = ((f32[8,3,11,4,128]{4,3,2,1,0:T(4,128)}), f32[8,3,11,4,128]{4,3,2,1,0:T(4,128)S(1)}, u32[]{:S(2)}, u32[]{:S(2)}) async-start(f32[8,3,11,4,128]{4,3,2,1,0:T(4,128)} %get-tuple-element.28), calls=%async_computation.1 | async-start | bytes 1081344 | tf_op jit(solution)/shard_map/all_to_all | solution.py:411
  24.7 21.3 %collective-permute-start = (f32[256,4,128]{2,1,0:T(4,128)}, f32[256,4,128]{2,1,0:T(4,128)S(1)}, u32[]{:S(2)}, u32[]{:S(2)}) collective-permute-start(f32[256,4,128]{2,1,0:T(4,128)} %get-tuple-element.29), channel_id=1, source_target_pairs={{0,8},{8,16},{16,24},{24,32},{32,40},{40,48},{48,56},{56,64},{64,7... | collective-permute-start | bytes 1572872 | tf_op jit(solution)/shard_map/ppermute | solution.py:420
  26.6 19.4 %collective-permute-start.1 = (f32[256,4,128]{2,1,0:T(4,128)}, f32[256,4,128]{2,1,0:T(4,128)S(1)}, u32[]{:S(2)}, u32[]{:S(2)}) collective-permute-start(f32[256,4,128]{2,1,0:T(4,128)} %get-tuple-element.30), channel_id=1, source_target_pairs={{8,0},{16,8},{24,16},{32,24},{40,32},{48,40},{56,48},{64,56},{72,6... | collective-permute-start | bytes 1572872 | tf_op jit(solution)/shard_map/ppermute | solution.py:420
  35.4 19.7 %collective-permute-start.2 = (f32[165,4,128]{2,1,0:T(4,128)}, f32[165,4,128]{2,1,0:T(4,128)S(1)}, u32[]{:S(2)}, u32[]{:S(2)}) collective-permute-start(f32[165,4,128]{2,1,0:T(4,128)} %get-tuple-element.31), channel_id=1, source_target_pairs={{0,8},{8,16},{16,24},{24,32},{32,40},{40,48},{48,56},{56,64},{64,7... | collective-permute-start | bytes 1013768 | tf_op jit(solution)/shard_map/ppermute | solution.py:422
  37.4 17.8 %collective-permute-start.3 = (f32[165,4,128]{2,1,0:T(4,128)}, f32[165,4,128]{2,1,0:T(4,128)S(1)}, u32[]{:S(2)}, u32[]{:S(2)}) collective-permute-start(f32[165,4,128]{2,1,0:T(4,128)} %get-tuple-element.32), channel_id=1, source_target_pairs={{8,0},{16,8},{24,16},{32,24},{40,32},{48,40},{56,48},{64,56},{72,6... | collective-permute-start | bytes 1013768 | tf_op jit(solution)/shard_map/ppermute | solution.py:422
  55.2 17.8 %all-to-all-start.2 = ((f32[8,48,4,128]{3,2,1,0:T(4,128)}), f32[8,48,4,128]{3,2,1,0:T(4,128)S(1)}, u32[]{:S(2)}, u32[]{:S(2)}) async-start(f32[8,48,4,128]{3,2,1,0:T(4,128)} %get-tuple-element.40), calls=%async_computation.2 | async-start | bytes 1572864 | tf_op jit(solution)/shard_map/all_to_all | solution.py:427
  66.6 10.4 %copy-start.9 = (f32[24]{0:T(128)S(1)}, f32[24]{0:T(128)}, u32[]{:S(2)}) copy-start(f32[24]{0:T(128)} %constant.25.clone) | copy-start | bytes 292
  66.6 10.5 %copy-start.8 = (f32[24]{0:T(128)S(1)}, f32[24]{0:T(128)}, u32[]{:S(2)}) copy-start(f32[24]{0:T(128)} %constant.26.clone) | copy-start | bytes 292
  66.6 21.8 %copy-start.2 = (f32[4,1024]{1,0:T(4,128)S(1)}, f32[4,1024]{1,0:T(4,128)}, u32[]{:S(2)}) copy-start(f32[4,1024]{1,0:T(4,128)} %refs_2_.1) | copy-start | bytes 49156
  66.6 21.8 %copy-start.3 = (f32[4,1024]{1,0:T(4,128)S(1)}, f32[4,1024]{1,0:T(4,128)}, u32[]{:S(2)}) copy-start(f32[4,1024]{1,0:T(4,128)} %refs_3_.1) | copy-start | bytes 49156
  73.0 15.4 %all-to-all-start.3 = ((f32[8,43,4,128]{3,2,1,0:T(4,128)}), f32[8,43,4,128]{3,2,1,0:T(4,128)S(1)}, u32[]{:S(2)}, u32[]{:S(2)}) async-start(f32[8,43,4,128]{3,2,1,0:T(4,128)} %steps.3), calls=%async_computation.3 | async-start | bytes 1409024 | tf_op jit(solution)/shard_map/all_to_all | solution.py:430

commit v4 on v3

--- a/solution.py
+++ b/solution.py
@@ -49,6 +49,10 @@
 
 FULL = 3
 CHUNKS = ((0, 2, False), (2, 1, True))
+WHOLE = FULL * BLOCKS
+TILES = WHOLE + 3
+SUMS_AT = 3 * (WHOLE + 1)
+MADE = SUMS_AT + 2 * BLOCKS
 
 SOUTH = [d for d in range(DIRS) if SIN[d] >= 0]
 NORTH = [d for d in range(DIRS) if SIN[d] < 0]
@@ -78,10 +82,6 @@
     return tiles_of(chunk) + chunk[1] + (2 if chunk[2] else 1)
 
 
-def made_of(chunk):
-    return 3 * (chunk[1] * BLOCKS + (1 if chunk[2] else 0))
-
-
 def smem():
     return pl.BlockSpec(memory_space=pltpu.SMEM)
 
@@ -104,24 +104,26 @@
     )(*args)
 
 
-def pack_kernel(x, *outs):
+def pack_kernel(spectrum, out, x, arrived):
+    copies = [pltpu.make_async_copy(spectrum.at[d], x.at[d], arrived.at[d]) for d in range(3)]
+    for copy in copies:
+        copy.start()
     zero = jnp.zeros((4, LANES), jnp.float32)
-    for (first, count, tail), out in zip(CHUNKS, outs):
-        for d in range(3):
-            for j in range(BLOCKS):
-                for i in range(count):
-                    for l in range(BLOCKS):
-                        f = j * FULL + first + i
-                        out[j, d, i * BLOCKS + l] = x[d, f, :, l * LANES : (l + 1) * LANES]
-                if tail:
-                    for i in range(3):
-                        l = j + i - 1
-                        inside = 0 <= l < BLOCKS
-                        value = x[d, FREQS - 1, :, l * LANES : (l + 1) * LANES] if inside else zero
-                        out[j, d, count * BLOCKS + i] = value
-
-
-def halo_kernel(tiles, with_maps, *refs):
+    for d in range(3):
+        copies[d].wait()
+        for j in range(BLOCKS):
+            for i in range(FULL):
+                for l in range(BLOCKS):
+                    value = x[d, j * FULL + i, :, l * LANES : (l + 1) * LANES]
+                    out[j, d, i * BLOCKS + l] = value
+            for i in range(3):
+                l = j + i - 1
+                inside = 0 <= l < BLOCKS
+                value = x[d, FREQS - 1, :, l * LANES : (l + 1) * LANES] if inside else zero
+                out[j, d, WHOLE + i] = value
+
+
+def halo_kernel(origin, tiles, with_maps, *refs):
     if with_maps:
         own, maps, up, down = refs
         for k in range(2):
@@ -138,19 +140,20 @@
     n = len(SOUTH)
 
     def body(t, carry):
+        at = origin + t
         for i, d in enumerate(SOUTH):
-            up[i * tiles + t] = own[d, t]
+            up[i * tiles + t] = own[d, at]
         for i, d in enumerate(NORTH):
-            down[i * tiles + t] = own[d, t]
+            down[i * tiles + t] = own[d, at]
         top, low = ends["s"]
-        a = [own[(top + k) % DIRS, t] for k in range(1, 4)]
-        b = [own[(low - k) % DIRS, t] for k in range(1, 4)]
+        a = [own[(top + k) % DIRS, at] for k in range(1, 4)]
+        b = [own[(low - k) % DIRS, at] for k in range(1, 4)]
         up[n * tiles + t] = jnp.concatenate([a[2][3:4], a[0][1:4]], axis=0)
         up[(n + 1) * tiles + t] = jnp.concatenate([b[1][2:4], a[1][2:4]], axis=0)
         up[(n + 2) * tiles + t] = jnp.concatenate([b[2][3:4], b[0][1:4]], axis=0)
         low, top = ends["n"]
-        a = [own[(low - k) % DIRS, t] for k in range(1, 4)]
-        b = [own[(top + k) % DIRS, t] for k in range(1, 4)]
+        a = [own[(low - k) % DIRS, at] for k in range(1, 4)]
+        b = [own[(top + k) % DIRS, at] for k in range(1, 4)]
         down[n * tiles + t] = jnp.concatenate([a[0][0:3], a[2][0:1]], axis=0)
         down[(n + 1) * tiles + t] = jnp.concatenate([a[1][0:2], b[1][0:2]], axis=0)
         down[(n + 2) * tiles + t] = jnp.concatenate([b[0][0:3], b[2][0:1]], axis=0)
@@ -161,12 +164,11 @@
 
 def step_kernel(chunk, first_call, group, coef, rfac, frsq, own, south, north, *refs):
     begin, count, tail = chunk
-    tiles, slots, made = tiles_of(chunk), slots_of(chunk), made_of(chunk)
+    tiles, slots, origin = tiles_of(chunk), slots_of(chunk), begin * BLOCKS
     if first_call:
-        maps, out, around, sums, st_a, st_b, ex_a, ex_b = refs
+        maps, out, around, st_a, st_b, ex_a, ex_b = refs
     else:
         around, given, out, st_a, st_b, ex_a, ex_b = refs
-        sums = None
     me = group[0]
     whole = count * BLOCKS
 
@@ -213,7 +215,7 @@
         n = len(SOUTH)
 
         def whole_tile(w, d, rows):
-            return jnp.concatenate([own[d, t], rows], axis=0) * seas[w]
+            return jnp.concatenate([own[d, origin + t], rows], axis=0) * seas[w]
 
         for i, d in enumerate(SOUTH):
             st_a[d, slot] = whole_tile("s", d, south[i * tiles + t])
@@ -241,26 +243,26 @@
 
     if first_call:
         for i in range(2 * BLOCKS):
-            sums[i] = jnp.zeros((4, LANES), jnp.float32)
+            out[0, SUMS_AT + i] = jnp.zeros((4, LANES), jnp.float32)
     else:
         for i in range(2 * BLOCKS):
-            out[0, made + i] = given[i]
+            out[0, SUMS_AT + i] = given[0, SUMS_AT + i]
+        for s in range(BLOCKS):
+            for d in range(3):
+                for i in range(origin):
+                    out[s, d * WHOLE + i] = given[s, d * WHOLE + i]
 
     def keep(t, d, new):
         if isinstance(t, int):
-            out[d // 3, 3 * whole + d % 3] = new[0:4]
+            out[d // 3, 3 * WHOLE + d % 3] = new[0:4]
         else:
-            out[d // 3, (d % 3) * whole + t] = new[0:4]
+            out[d // 3, (d % 3) * WHOLE + origin + t] = new[0:4]
 
     def add_up(t, f, total):
-        place = me if isinstance(t, int) else t % BLOCKS
+        place = SUMS_AT + (me if isinstance(t, int) else t % BLOCKS)
         total = total[0:4]
-        if first_call:
-            sums[place] += total
-            sums[BLOCKS + place] += total * frsq[f]
-        else:
-            out[0, made + place] += total
-            out[0, made + BLOCKS + place] += total * frsq[f]
+        out[0, place] += total
+        out[0, place + BLOCKS] += total * frsq[f]
 
     def make(step, src, src_ex, dst, dst_ex):
         def body(t, carry):
@@ -322,26 +324,25 @@
         (src, src_ex), (dst, dst_ex) = bufs[step % 2], bufs[(step + 1) % 2]
         body = make(step, src, src_ex, dst, dst_ex)
         if step < SUB - 1:
-            lax.fori_loop(0, tiles, body, 0)
+            lax.fori_loop(0, tiles, body, 0, unroll=4)
         else:
-            lax.fori_loop(0, whole, body, 0)
+            lax.fori_loop(0, whole, body, 0, unroll=4)
             if tail:
                 body(whole + 1, 0)
     if not first_call:
         for i in range(2 * BLOCKS):
-            value = out[0, made + i]
+            value = out[0, SUMS_AT + i]
             for s in range(1, BLOCKS):
-                out[s, made + i] = value
+                out[s, SUMS_AT + i] = value
 
 
 def step_call(chunk, first_call, group, own, south, north, rest):
-    slots, made = slots_of(chunk), made_of(chunk)
+    slots = slots_of(chunk)
     state = pltpu.VMEM((DIRS, slots, 8, LANES), jnp.float32)
     extra = pltpu.VMEM((len(EXTRAS), slots, 8, LANES), jnp.float32)
+    out = [(BLOCKS, MADE, 4, LANES)]
     if first_call:
-        out = [(BLOCKS, made, 4, LANES), (2, 2, BLOCKS + 2, 8, LANES), (2 * BLOCKS, 4, LANES)]
-    else:
-        out = [(BLOCKS, made + 2 * BLOCKS, 4, LANES)]
+        out.append((2, 2, BLOCKS + 2, 8, LANES))
     args = (group, COEF, RFAC, FR * FR, own, south, north, *rest)
     return call(
         functools.partial(step_kernel, chunk, first_call),
@@ -354,35 +355,27 @@
     )
 
 
-def source_kernel(cos, sin, *refs):
-    gots, (wind_u, wind_v, out) = refs[: len(CHUNKS)], refs[len(CHUNKS) :]
-    last = gots[-1]
-    at = made_of(CHUNKS[-1])
+def source_kernel(cos, sin, got, wind_u, wind_v, out):
     inverse = 1.0 / (DIRS * FREQS)
-
     for t in range(BLOCKS):
         cols = slice(t * LANES, (t + 1) * LANES)
-        m0 = last[0, at + t]
-        m2 = last[0, at + BLOCKS + t]
+        m0 = got[0, SUMS_AT + t]
+        m2 = got[0, SUMS_AT + BLOCKS + t]
         for j in range(1, BLOCKS):
-            m0 = m0 + last[j, at + t]
-            m2 = m2 + last[j, at + BLOCKS + t]
+            m0 = m0 + got[j, SUMS_AT + t]
+            m2 = m2 + got[j, SUMS_AT + BLOCKS + t]
         ratio = 0.5 * (m2 * inverse) / (1.0 + m0 * inverse)
         u, v = wind_u[:, cols], wind_v[:, cols]
         gain = [0.5 * jnp.maximum(u * cos[d] + v * sin[d], 0.0) for d in range(3)]
-        for (first, count, tail), got in zip(CHUNKS, gots):
-            where = [
-                (j * FULL + first + i, j, i * BLOCKS + t, count * BLOCKS)
-                for j in range(BLOCKS)
-                for i in range(count)
-            ]
-            if tail:
-                where.append((FREQS - 1, t, 3 * count * BLOCKS, 1))
-            for f, j, base, stride in where:
-                fr = float(FR[f])
-                shrink = 1.0 / (1.0 + ratio * (fr * fr))
-                for d in range(3):
-                    out[d, f, :, cols] = got[j, base + d * stride] * (1.0 + gain[d] * fr) * shrink
+        for f in range(FREQS):
+            fr = float(FR[f])
+            shrink = 1.0 / (1.0 + ratio * (fr * fr))
+            for d in range(3):
+                if f < BLOCKS * FULL:
+                    a = got[f // FULL, d * WHOLE + f % FULL * BLOCKS + t]
+                else:
+                    a = got[t, 3 * WHOLE + d]
+                out[d, f, :, cols] = a * (1.0 + gain[d] * fr) * shrink
 
 
 def on_device(spectrum, sea_mask, turning, wind_u, wind_v):
@@ -393,48 +386,43 @@
     down = [(j, i) for i, j in up]
 
     maps = jnp.stack([(sea_mask == 1).astype(jnp.float32), turning])
-    packs = call(
+    pack = pl.pallas_call(
         pack_kernel,
-        "pack",
-        [(BLOCKS, 3, tiles_of(c), 4, LANES) for c in CHUNKS],
-        (spectrum,),
-        0,
-    )
-    rows = []
-    hold = None
+        out_shape=jax.ShapeDtypeStruct((BLOCKS, 3, TILES, 4, LANES), jnp.float32),
+        in_specs=[pl.BlockSpec(memory_space=pltpu.HBM)],
+        out_specs=vmem(),
+        scratch_shapes=[pltpu.VMEM(spectrum.shape, jnp.float32), pltpu.SemaphoreType.DMA((3,))],
+        compiler_params=pltpu.CompilerParams(vmem_limit_bytes=VMEM_LIMIT),
+        interpret=INTERPRET,
+        name="pack",
+    )(spectrum)
+    own = lax.all_to_all(pack, "spec", 0, 0, tiled=True).reshape(DIRS, TILES, 4, LANES)
+    edges = []
     for i, chunk in enumerate(CHUNKS):
         tiles = tiles_of(chunk)
-        pack = packs[i]
-        if hold is not None:
-            pack, hold = lax.optimization_barrier((pack, hold))
-            rows[-1] = (rows[-1][0],) + tuple(hold)
-        own = lax.all_to_all(pack, "spec", 0, 0, tiled=True).reshape(DIRS, tiles, 4, LANES)
         size = PLANES * tiles + (2 * BLOCKS if i == 0 else 0)
-        args = (own, maps) if i == 0 else (own,)
-        edges = call(
-            functools.partial(halo_kernel, tiles, i == 0), "halo", [(size, 4, LANES)] * 2, args, 0
+        edges.append(
+            call(
+                functools.partial(halo_kernel, chunk[0] * BLOCKS, tiles, i == 0),
+                "halo",
+                [(size, 4, LANES)] * 2,
+                (own, maps) if i == 0 else (own,),
+                0,
+            )
         )
-        rows.append((own, edges[0], edges[1]))
-        hold = (edges[0], edges[1])
-    (own, u, d), (own_2, u_2, d_2) = rows
-    south, north = lax.ppermute(u, "space", up), lax.ppermute(d, "space", down)
-    south, north, _, _ = lax.optimization_barrier((south, north, u_2, d_2))
-    south_2, north_2 = lax.ppermute(u_2, "space", up), lax.ppermute(d_2, "space", down)
-    rows = [(own, south, north), (own_2, south_2, north_2)]
-
-    made, around, sums = step_call(CHUNKS[0], True, group, *rows[0], (maps,))
-    made, south_2, north_2 = lax.optimization_barrier((made, south_2, north_2))
-    gots = [lax.all_to_all(made, "spec", 0, 0, tiled=True)]
-    (made,) = step_call(CHUNKS[1], False, group, own_2, south_2, north_2, (around, sums))
-    made, gots = lax.optimization_barrier((made, gots))
-    gots.append(lax.all_to_all(made, "spec", 0, 0, tiled=True))
+    south, north = lax.ppermute(edges[0][0], "space", up), lax.ppermute(edges[0][1], "space", down)
+    south, north, _ = lax.optimization_barrier((south, north, edges[1]))
+    south_2, north_2 = lax.ppermute(edges[1][0], "space", up), lax.ppermute(edges[1][1], "space", down)
+    made, around = step_call(CHUNKS[0], True, group, own, south, north, (maps,))
+    (made,) = step_call(CHUNKS[1], False, group, own, south_2, north_2, (around, made))
+    got = lax.all_to_all(made, "spec", 0, 0, tiled=True)
     cos = lax.dynamic_slice_in_dim(jnp.asarray(COS), me * 3, 3)
     sin = lax.dynamic_slice_in_dim(jnp.asarray(SIN), me * 3, 3)
     return call(
         source_kernel,
         "source",
         (3, FREQS, 4, BLOCKS * LANES),
-        (cos, sin, *gots, wind_u, wind_v),
+        (cos, sin, got, wind_u, wind_v),
         2,
     )
 

time: 91.8 us -> 89.6 us (0.976)
  waiting for transfers between devices: 32.7 us -> 43.3 us
  starting transfers between devices: 34.9 us -> 27.2 us
  Pallas kernels: 21.4 us -> 16.5 us
    pallas_call x6 -> x5, Pallas kernels: 21.4 us -> 14.7 us  [call(): pl.pallas_call(kernel, out_shape=jax.tree.map(lambda s: jax.ShapeDtypeStr...]
    all_to_all x2 -> x1, waiting for transfers between devices: 13.1 us -> 17.7 us  [on_device(): lax.all_to_all(pack, 'spec', 0, 0, tiled=True)]
    all_to_all x2 -> x1, starting transfers between devices: 8.81 us -> 4.77 us  [on_device(): got = lax.all_to_all(made, 'spec', 0, 0, tiled=True)]
    all_to_all x2 -> x1, starting transfers between devices: 8.95 us -> 5.32 us  [on_device(): lax.all_to_all(pack, 'spec', 0, 0, tiled=True)]
    ppermute x4, waiting for transfers between devices: 1.91 us -> 4.96 us  [the longest x1 3.7 us: on_device(): lax.ppermute(edges[0][1], 'space', down)]
    all_to_all x2 -> x1, waiting for transfers between devices: 17.6 us -> 20.6 us  [on_device(): got = lax.all_to_all(made, 'spec', 0, 0, tiled=True)]
    pallas_call x0 -> x1, Pallas kernels: none -> 1.83 us  [on_device(): pl.pallas_call(pack_kernel, out_shape=jax.ShapeDtypeStruct((BLOCKS, 3, TI...]
  transfers between devices with their start and end apart: 8 -> 6, of which waited for: 5 -> 4; matrix products, arithmetic and copies ran while one was open for 0% -> 0% of each run, Pallas kernels for 19% -> 7%
where the time goes in v4:
time: 89.6 us; the launch traced here: 88.6 us
  waiting for transfers between devices  43.3 us (48%)
  starting transfers between devices  27.2 us (30%)
  Pallas kernels  16.5 us (18%)
  local copies, waits for them, and re-layouts  1.48 us (2%)
    all_to_all x1, waiting for transfers between devices, on_device(): got = lax.all_to_all(made, 'spec', 0, 0, tiled=True)  20.6 us
    all_to_all x1, waiting for transfers between devices, on_device(): lax.all_to_all(pack, 'spec', 0, 0, tiled=True)  17.7 us
    pallas_call x5, Pallas kernels, call(): pl.pallas_call(kernel, out_shape=jax.tree.map(lambda s: jax.ShapeDtypeStr...  14.7 us
    ppermute x1, starting transfers between devices, on_device(): lax.ppermute(edges[1][1], 'space', down)  6.65 us
    ppermute x1, starting transfers between devices, on_device(): lax.ppermute(edges[0][1], 'space', down)  6.65 us
    all_to_all x1, starting transfers between devices, on_device(): lax.all_to_all(pack, 'spec', 0, 0, tiled=True)  5.32 us
    all_to_all x1, starting transfers between devices, on_device(): got = lax.all_to_all(made, 'spec', 0, 0, tiled=True)  4.77 us
    ppermute x1, waiting for transfers between devices, on_device(): lax.ppermute(edges[0][1], 'space', down)  3.7 us
  transfers between devices with their start and end apart: 6, of which 4 were waited for; matrix products, arithmetic and copies ran while one was open for 0% of the time, Pallas kernels for 7%

profile of v4, /device:TPU:448, one launch (start us, length us, event | category | flops | bytes accessed | tf_op | source)
XLA Modules:
  0.0 88.6 jit_solution(4910779693301565392)
XLA Ops:
  0.0 0.0 copy-start
  0.0 1.3 %copy-done = f32[3,25,4,1024]{3,2,1,0:T(4,128)S(1)} copy-done((f32[3,25,4,1024]{3,2,1,0:T(4,128)S(1)}, f32[3,25,4,1024]{3,2,1,0:T(4,128)}, u32[]{:S(2)}) %copy-start) | copy-done | bytes 1228824
  1.3 1.8 %pack.1 = f32[8,3,27,4,128]{4,3,2,1,0:T(4,128)} custom-call(f32[3,25,4,1024]{3,2,1,0:T(4,128)S(1)} %copy-done), custom_call_target="tpu_custom_call" | custom-call | tf_op jit(solution)/shard_map/pack/pallas_call | solution.py:389
  3.1 0.0 copy-start.6
  3.1 0.0 copy-start.7
  3.1 5.3 %all-to-all-start = ((f32[8,3,27,4,128]{4,3,2,1,0:T(4,128)}), f32[8,3,27,4,128]{4,3,2,1,0:T(4,128)S(1)}, u32[]{:S(2)}, u32[]{:S(2)}) async-start(f32[8,3,27,4,128]{4,3,2,1,0:T(4,128)} %pack.1), calls=%async_computation | async-start | bytes 2654208 | tf_op jit(solution)/shard_map/all_to_all | solution.py:399
  8.5 0.0 copy-done.6
  8.5 0.0 copy-done.7
  8.5 17.7 %all-to-all-done = f32[8,3,27,4,128]{4,3,2,1,0:T(4,128)S(1)} async-done(((f32[8,3,27,4,128]{4,3,2,1,0:T(4,128)}), f32[8,3,27,4,128]{4,3,2,1,0:T(4,128)S(1)}, u32[]{:S(2)}, u32[]{:S(2)}) %all-to-all-start) | async-done | bytes 1327136 | tf_op jit(solution)/shard_map/all_to_all | solution.py:399
  26.3 0.0 copy-start.1
  26.3 0.0 copy-start.4
  26.3 0.0 copy-start.5
  26.3 1.3 %halo.3 = (f32[256,4,128]{2,1,0:T(4,128)}, f32[256,4,128]{2,1,0:T(4,128)}) custom-call(f32[24,27,4,128]{3,2,1,0:T(4,128)S(1)} %bitcast.5, f32[2,4,1024]{2,1,0:T(4,128)S(1)} %pad_maximum_fusion.refs_1_.refs_0_), custom_call_target="tpu_custom_call" | custom-call | flops 1000 | bytes 4000000 | tf_op jit(solution)/shard_map/halo/pallas_call | solution.py:94
  27.5 1.9 %collective-permute-start.2 = (f32[256,4,128]{2,1,0:T(4,128)}, f32[256,4,128]{2,1,0:T(4,128)S(1)}, u32[]{:S(2)}, u32[]{:S(2)}) collective-permute-start(f32[256,4,128]{2,1,0:T(4,128)} %get-tuple-element.15), channel_id=1, source_target_pairs={{0,8},{8,16},{16,24},{24,32},{32,40},{40,48},{48,56},{56,64},{64,7... | collective-permute-start | bytes 1572872 | tf_op jit(solution)/shard_map/ppermute | solution.py:413
  29.4 6.7 %collective-permute-start.3 = (f32[256,4,128]{2,1,0:T(4,128)}, f32[256,4,128]{2,1,0:T(4,128)S(1)}, u32[]{:S(2)}, u32[]{:S(2)}) collective-permute-start(f32[256,4,128]{2,1,0:T(4,128)} %get-tuple-element.16), channel_id=1, source_target_pairs={{8,0},{16,8},{24,16},{32,24},{40,32},{48,40},{56,48},{64,56},{72,6... | collective-permute-start | bytes 1572872 | tf_op jit(solution)/shard_map/ppermute | solution.py:413
  36.1 0.9 %halo.2 = (f32[165,4,128]{2,1,0:T(4,128)}, f32[165,4,128]{2,1,0:T(4,128)S(1)}) custom-call(f32[24,27,4,128]{3,2,1,0:T(4,128)S(1)} %bitcast.6), custom_call_target="tpu_custom_call" | custom-call | flops 1000 | bytes 4000000 | tf_op jit(solution)/shard_map/halo/pallas_call | solution.py:94
  37.0 1.9 %collective-permute-start = (f32[165,4,128]{2,1,0:T(4,128)}, f32[165,4,128]{2,1,0:T(4,128)S(1)}, u32[]{:S(2)}, u32[]{:S(2)}) collective-permute-start(f32[165,4,128]{2,1,0:T(4,128)} %get-tuple-element.13), channel_id=1, source_target_pairs={{0,8},{8,16},{16,24},{24,32},{32,40},{40,48},{48,56},{56,64},{64,7... | collective-permute-start | bytes 1013768 | tf_op jit(solution)/shard_map/ppermute | solution.py:415
  38.9 6.7 %collective-permute-start.1 = (f32[165,4,128]{2,1,0:T(4,128)S(1)}, f32[165,4,128]{2,1,0:T(4,128)S(1)}, u32[]{:S(2)}, u32[]{:S(2)}) collective-permute-start(f32[165,4,128]{2,1,0:T(4,128)S(1)} %get-tuple-element.14), channel_id=1, source_target_pairs={{8,0},{16,8},{24,16},{32,24},{40,32},{48,40},{56,48},{64,56},{72,6... | collective-permute-start | bytes 1013768 | tf_op jit(solution)/shard_map/ppermute | solution.py:415
  45.6 0.0 collective-permute-done.2.south
  45.6 3.7 %collective-permute-done.3.north = f32[256,4,128]{2,1,0:T(4,128)S(1)} collective-permute-done((f32[256,4,128]{2,1,0:T(4,128)}, f32[256,4,128]{2,1,0:T(4,128)S(1)}, u32[]{:S(2)}, u32[]{:S(2)}) %collective-permute-start.3) | collective-permute-done | bytes 524320 | tf_op jit(solution)/shard_map/ppermute | solution.py:413
  49.3 0.0 copy-done.1
  49.3 0.0 copy-done.4
  49.3 0.0 copy-done.5
  49.3 5.1 %steps.2 = (f32[8,91,4,128]{3,2,1,0:T(4,128)S(1)}, f32[2,2,10,8,128]{4,3,2,1,0:T(8,128)S(1)}) custom-call(s32[1]{0:T(128)} %bitcast.group, f32[25,18]{1,0:T(8,128)S(1)} %copy-done.1, f32[25]{0:T(128)S(1)} %copy-done.4, f32[25]{0:T(128)S(1)} %copy-done.5, f32[24,27,4,128]{3,2,1,0:T(4,128)S(1)} %bitcast.7, f32[256,4,128]{2,1,0:T(4,128)S(1)} %collective-permute-done.2.south, ...), custom_call_target="tpu_custom_call" | custom-call | flops 1000 | bytes 20000000 | tf_op jit(solution)/shard_map/steps/pallas_call | solution.py:94
  54.4 1.3 %collective-permute-done.south = f32[165,4,128]{2,1,0:T(4,128)S(1)} collective-permute-done((f32[165,4,128]{2,1,0:T(4,128)}, f32[165,4,128]{2,1,0:T(4,128)S(1)}, u32[]{:S(2)}, u32[]{:S(2)}) %collective-permute-start) | collective-permute-done | bytes 337952 | tf_op jit(solution)/shard_map/ppermute | solution.py:415
  55.6 0.0 collective-permute-done.1.north
  55.6 5.3 %steps.3 = f32[8,91,4,128]{3,2,1,0:T(4,128)} custom-call(s32[1]{0:T(128)} %bitcast.group, f32[25,18]{1,0:T(8,128)S(1)} %copy-done.1, f32[25]{0:T(128)S(1)} %copy-done.4, f32[25]{0:T(128)S(1)} %copy-done.5, f32[24,27,4,128]{3,2,1,0:T(4,128)S(1)} %bitcast.8, f32[165,4,128]{2,1,0:T(4,128)S(1)} %collective-permute-done.south, ...), custom_call_target="tpu_custom_call" | custom-call | flops 1000 | bytes 20000000 | tf_op jit(solution)/shard_map/steps/pallas_call | solution.py:94
  60.9 0.0 copy-start.9
  60.9 0.0 copy-start.8
  60.9 0.0 copy-start.2
  60.9 0.0 copy-start.3
  61.0 4.8 %all-to-all-start.1 = ((f32[8,91,4,128]{3,2,1,0:T(4,128)}), f32[8,91,4,128]{3,2,1,0:T(4,128)S(1)}, u32[]{:S(2)}, u32[]{:S(2)}) async-start(f32[8,91,4,128]{3,2,1,0:T(4,128)} %steps.3), calls=%async_computation.1 | async-start | bytes 2981888 | tf_op jit(solution)/shard_map/all_to_all | solution.py:418
  65.7 0.0 copy-done.9
  65.7 0.1 dynamic_slice.6.cos
  65.8 0.0 copy-done.8
  65.8 0.1 dynamic_slice.7.sin
  65.9 20.6 %all-to-all-done.1.got = f32[8,91,4,128]{3,2,1,0:T(4,128)S(1)} async-done(((f32[8,91,4,128]{3,2,1,0:T(4,128)}), f32[8,91,4,128]{3,2,1,0:T(4,128)S(1)}, u32[]{:S(2)}, u32[]{:S(2)}) %all-to-all-start.1) | async-done | bytes 1490976 | tf_op jit(solution)/shard_map/all_to_all | solution.py:418
  86.5 0.0 copy-done.2
  86.5 0.0 copy-done.3
  86.5 2.1 %source.1 = f32[3,25,4,1024]{3,2,1,0:T(4,128)} custom-call(f32[3]{0:T(128)S(1)} %dynamic_slice.6.cos, f32[3]{0:T(128)S(1)} %dynamic_slice.7.sin, f32[8,91,4,128]{3,2,1,0:T(4,128)S(1)} %all-to-all-done.1.got, f32[4,1024]{1,0:T(4,128)S(1)} %copy-done.2, f32[4,1024]{1,0:T(4,128)S(1)} %copy-done.3), custom_call_target="tpu_custom_call" | custom-call | flops 1000 | bytes 4000000 | tf_op jit(solution)/shard_map/source/pallas_call | solution.py:94
  (2 shorter events, 0.0 us)
Async XLA Ops:
  0.0 1.3 %copy-start = (f32[3,25,4,1024]{3,2,1,0:T(4,128)S(1)}, f32[3,25,4,1024]{3,2,1,0:T(4,128)}, u32[]{:S(2)}) copy-start(f32[3,25,4,1024]{3,2,1,0:T(4,128)} %spectrum.1) | copy-start | bytes 3686404
  3.1 5.4 %copy-start.6 = (s32[4,1024]{1,0:T(4,128)S(1)}, s32[4,1024]{1,0:T(4,128)}, u32[]{:S(2)}) copy-start(s32[4,1024]{1,0:T(4,128)} %param.12) | copy-start | bytes 49156
  3.1 5.4 %copy-start.7 = (f32[4,1024]{1,0:T(4,128)S(1)}, f32[4,1024]{1,0:T(4,128)}, u32[]{:S(2)}) copy-start(f32[4,1024]{1,0:T(4,128)} %param.13) | copy-start | bytes 49156
  3.1 23.1 %all-to-all-start = ((f32[8,3,27,4,128]{4,3,2,1,0:T(4,128)}), f32[8,3,27,4,128]{4,3,2,1,0:T(4,128)S(1)}, u32[]{:S(2)}, u32[]{:S(2)}) async-start(f32[8,3,27,4,128]{4,3,2,1,0:T(4,128)} %pack.1), calls=%async_computation | async-start | bytes 2654208 | tf_op jit(solution)/shard_map/all_to_all | solution.py:399
  26.3 23.0 %copy-start.1 = (f32[25,18]{1,0:T(8,128)S(1)}, f32[25,18]{1,0:T(8,128)}, u32[]{:S(2)}) copy-start(f32[25,18]{1,0:T(8,128)} %constant.22.clone.coef) | copy-start | bytes 5404
  26.3 23.0 %copy-start.4 = (f32[25]{0:T(128)S(1)}, f32[25]{0:T(128)}, u32[]{:S(2)}) copy-start(f32[25]{0:T(128)} %constant.23.clone.rfac) | copy-start | bytes 304
  26.3 23.0 %copy-start.5 = (f32[25]{0:T(128)S(1)}, f32[25]{0:T(128)}, u32[]{:S(2)}) copy-start(f32[25]{0:T(128)} %constant.24.clone.frsq) | copy-start | bytes 304
  27.5 18.0 %collective-permute-start.2 = (f32[256,4,128]{2,1,0:T(4,128)}, f32[256,4,128]{2,1,0:T(4,128)S(1)}, u32[]{:S(2)}, u32[]{:S(2)}) collective-permute-start(f32[256,4,128]{2,1,0:T(4,128)} %get-tuple-element.15), channel_id=1, source_target_pairs={{0,8},{8,16},{16,24},{24,32},{32,40},{40,48},{48,56},{56,64},{64,7... | collective-permute-start | bytes 1572872 | tf_op jit(solution)/shard_map/ppermute | solution.py:413
  29.4 19.8 %collective-permute-start.3 = (f32[256,4,128]{2,1,0:T(4,128)}, f32[256,4,128]{2,1,0:T(4,128)S(1)}, u32[]{:S(2)}, u32[]{:S(2)}) collective-permute-start(f32[256,4,128]{2,1,0:T(4,128)} %get-tuple-element.16), channel_id=1, source_target_pairs={{8,0},{16,8},{24,16},{32,24},{40,32},{48,40},{56,48},{64,56},{72,6... | collective-permute-start | bytes 1572872 | tf_op jit(solution)/shard_map/ppermute | solution.py:413
  37.0 18.6 %collective-permute-start = (f32[165,4,128]{2,1,0:T(4,128)}, f32[165,4,128]{2,1,0:T(4,128)S(1)}, u32[]{:S(2)}, u32[]{:S(2)}) collective-permute-start(f32[165,4,128]{2,1,0:T(4,128)} %get-tuple-element.13), channel_id=1, source_target_pairs={{0,8},{8,16},{16,24},{24,32},{32,40},{40,48},{48,56},{56,64},{64,7... | collective-permute-start | bytes 1013768 | tf_op jit(solution)/shard_map/ppermute | solution.py:415
  38.9 16.7 %collective-permute-start.1 = (f32[165,4,128]{2,1,0:T(4,128)S(1)}, f32[165,4,128]{2,1,0:T(4,128)S(1)}, u32[]{:S(2)}, u32[]{:S(2)}) collective-permute-start(f32[165,4,128]{2,1,0:T(4,128)S(1)} %get-tuple-element.14), channel_id=1, source_target_pairs={{8,0},{16,8},{24,16},{32,24},{40,32},{48,40},{56,48},{64,56},{72,6... | collective-permute-start | bytes 1013768 | tf_op jit(solution)/shard_map/ppermute | solution.py:415
  60.9 4.8 %copy-start.9 = (f32[24]{0:T(128)S(1)}, f32[24]{0:T(128)}, u32[]{:S(2)}) copy-start(f32[24]{0:T(128)} %constant.25.clone) | copy-start | bytes 292
  60.9 4.9 %copy-start.8 = (f32[24]{0:T(128)S(1)}, f32[24]{0:T(128)}, u32[]{:S(2)}) copy-start(f32[24]{0:T(128)} %constant.26.clone) | copy-start | bytes 292
  60.9 25.5 %copy-start.2 = (f32[4,1024]{1,0:T(4,128)S(1)}, f32[4,1024]{1,0:T(4,128)}, u32[]{:S(2)}) copy-start(f32[4,1024]{1,0:T(4,128)} %wind_u.1) | copy-start | bytes 49156
  60.9 25.5 %copy-start.3 = (f32[4,1024]{1,0:T(4,128)S(1)}, f32[4,1024]{1,0:T(4,128)}, u32[]{:S(2)}) copy-start(f32[4,1024]{1,0:T(4,128)} %wind_v.1) | copy-start | bytes 49156
  61.0 25.5 %all-to-all-start.1 = ((f32[8,91,4,128]{3,2,1,0:T(4,128)}), f32[8,91,4,128]{3,2,1,0:T(4,128)S(1)}, u32[]{:S(2)}, u32[]{:S(2)}) async-start(f32[8,91,4,128]{3,2,1,0:T(4,128)} %steps.3), calls=%async_computation.1 | async-start | bytes 2981888 | tf_op jit(solution)/shard_map/all_to_all | solution.py:418

commit v5 on v4

--- a/solution.py
+++ b/solution.py
@@ -104,26 +104,28 @@
     )(*args)
 
 
-def pack_kernel(spectrum, out, x, arrived):
+def pack_kernel(spectrum, *refs):
+    outs, (x, arrived) = refs[: len(CHUNKS)], refs[len(CHUNKS) :]
     copies = [pltpu.make_async_copy(spectrum.at[d], x.at[d], arrived.at[d]) for d in range(3)]
     for copy in copies:
         copy.start()
     zero = jnp.zeros((4, LANES), jnp.float32)
     for d in range(3):
         copies[d].wait()
-        for j in range(BLOCKS):
-            for i in range(FULL):
-                for l in range(BLOCKS):
-                    value = x[d, j * FULL + i, :, l * LANES : (l + 1) * LANES]
-                    out[j, d, i * BLOCKS + l] = value
-            for i in range(3):
-                l = j + i - 1
-                inside = 0 <= l < BLOCKS
-                value = x[d, FREQS - 1, :, l * LANES : (l + 1) * LANES] if inside else zero
-                out[j, d, WHOLE + i] = value
-
-
-def halo_kernel(origin, tiles, with_maps, *refs):
+        for (begin, count, tail), out in zip(CHUNKS, outs):
+            for j in range(BLOCKS):
+                for i in range(count):
+                    for l in range(BLOCKS):
+                        value = x[d, j * FULL + begin + i, :, l * LANES : (l + 1) * LANES]
+                        out[j, d, i * BLOCKS + l] = value
+                for i in range(3 if tail else 0):
+                    l = j + i - 1
+                    inside = 0 <= l < BLOCKS
+                    value = x[d, FREQS - 1, :, l * LANES : (l + 1) * LANES] if inside else zero
+                    out[j, d, count * BLOCKS + i] = value
+
+
+def halo_kernel(tiles, with_maps, *refs):
     if with_maps:
         own, maps, up, down = refs
         for k in range(2):
@@ -140,26 +142,25 @@
     n = len(SOUTH)
 
     def body(t, carry):
-        at = origin + t
         for i, d in enumerate(SOUTH):
-            up[i * tiles + t] = own[d, at]
+            up[i * tiles + t] = own[d, t]
         for i, d in enumerate(NORTH):
-            down[i * tiles + t] = own[d, at]
+            down[i * tiles + t] = own[d, t]
         top, low = ends["s"]
-        a = [own[(top + k) % DIRS, at] for k in range(1, 4)]
-        b = [own[(low - k) % DIRS, at] for k in range(1, 4)]
+        a = [own[(top + k) % DIRS, t] for k in range(1, 4)]
+        b = [own[(low - k) % DIRS, t] for k in range(1, 4)]
         up[n * tiles + t] = jnp.concatenate([a[2][3:4], a[0][1:4]], axis=0)
         up[(n + 1) * tiles + t] = jnp.concatenate([b[1][2:4], a[1][2:4]], axis=0)
         up[(n + 2) * tiles + t] = jnp.concatenate([b[2][3:4], b[0][1:4]], axis=0)
         low, top = ends["n"]
-        a = [own[(low - k) % DIRS, at] for k in range(1, 4)]
-        b = [own[(top + k) % DIRS, at] for k in range(1, 4)]
+        a = [own[(low - k) % DIRS, t] for k in range(1, 4)]
+        b = [own[(top + k) % DIRS, t] for k in range(1, 4)]
         down[n * tiles + t] = jnp.concatenate([a[0][0:3], a[2][0:1]], axis=0)
         down[(n + 1) * tiles + t] = jnp.concatenate([a[1][0:2], b[1][0:2]], axis=0)
         down[(n + 2) * tiles + t] = jnp.concatenate([b[0][0:3], b[2][0:1]], axis=0)
         return carry
 
-    lax.fori_loop(0, tiles, body, 0)
+    lax.fori_loop(0, tiles, body, 0, unroll=4)
 
 
 def step_kernel(chunk, first_call, group, coef, rfac, frsq, own, south, north, *refs):
@@ -215,7 +216,7 @@
         n = len(SOUTH)
 
         def whole_tile(w, d, rows):
-            return jnp.concatenate([own[d, origin + t], rows], axis=0) * seas[w]
+            return jnp.concatenate([own[d, t], rows], axis=0) * seas[w]
 
         for i, d in enumerate(SOUTH):
             st_a[d, slot] = whole_tile("s", d, south[i * tiles + t])
@@ -386,35 +387,39 @@
     down = [(j, i) for i, j in up]
 
     maps = jnp.stack([(sea_mask == 1).astype(jnp.float32), turning])
-    pack = pl.pallas_call(
+    packs = pl.pallas_call(
         pack_kernel,
-        out_shape=jax.ShapeDtypeStruct((BLOCKS, 3, TILES, 4, LANES), jnp.float32),
+        out_shape=[
+            jax.ShapeDtypeStruct((BLOCKS, 3, tiles_of(c), 4, LANES), jnp.float32) for c in CHUNKS
+        ],
         in_specs=[pl.BlockSpec(memory_space=pltpu.HBM)],
-        out_specs=vmem(),
+        out_specs=[vmem() for _ in CHUNKS],
         scratch_shapes=[pltpu.VMEM(spectrum.shape, jnp.float32), pltpu.SemaphoreType.DMA((3,))],
-        compiler_params=pltpu.CompilerParams(vmem_limit_bytes=VMEM_LIMIT),
+        compiler_params=pltpu.CompilerParams(vmem_limit_bytes=60 * 1024 * 1024),
         interpret=INTERPRET,
         name="pack",
     )(spectrum)
-    own = lax.all_to_all(pack, "spec", 0, 0, tiled=True).reshape(DIRS, TILES, 4, LANES)
-    edges = []
-    for i, chunk in enumerate(CHUNKS):
-        tiles = tiles_of(chunk)
+
+    def gather(i, pack):
+        tiles = tiles_of(CHUNKS[i])
+        own = lax.all_to_all(pack, "spec", 0, 0, tiled=True).reshape(DIRS, tiles, 4, LANES)
         size = PLANES * tiles + (2 * BLOCKS if i == 0 else 0)
-        edges.append(
-            call(
-                functools.partial(halo_kernel, chunk[0] * BLOCKS, tiles, i == 0),
-                "halo",
-                [(size, 4, LANES)] * 2,
-                (own, maps) if i == 0 else (own,),
-                0,
-            )
+        return own, call(
+            functools.partial(halo_kernel, tiles, i == 0),
+            "halo",
+            [(size, 4, LANES)] * 2,
+            (own, maps) if i == 0 else (own,),
+            0,
         )
-    south, north = lax.ppermute(edges[0][0], "space", up), lax.ppermute(edges[0][1], "space", down)
-    south, north, _ = lax.optimization_barrier((south, north, edges[1]))
-    south_2, north_2 = lax.ppermute(edges[1][0], "space", up), lax.ppermute(edges[1][1], "space", down)
+
+    own, (low, high) = gather(0, packs[0])
+    pack, low, high = lax.optimization_barrier((packs[1], low, high))
+    own_2, (low_2, high_2) = gather(1, pack)
+    south, north = lax.ppermute(low, "space", up), lax.ppermute(high, "space", down)
+    south, north, _, _ = lax.optimization_barrier((south, north, low_2, high_2))
+    south_2, north_2 = lax.ppermute(low_2, "space", up), lax.ppermute(high_2, "space", down)
     made, around = step_call(CHUNKS[0], True, group, own, south, north, (maps,))
-    (made,) = step_call(CHUNKS[1], False, group, own, south_2, north_2, (around, made))
+    (made,) = step_call(CHUNKS[1], False, group, own_2, south_2, north_2, (around, made))
     got = lax.all_to_all(made, "spec", 0, 0, tiled=True)
     cos = lax.dynamic_slice_in_dim(jnp.asarray(COS), me * 3, 3)
     sin = lax.dynamic_slice_in_dim(jnp.asarray(SIN), me * 3, 3)

time: 89.6 us -> 88.6 us (0.989)
  the two profiles are of different devices: /device:TPU:448 before, /device:TPU:256 now
where the time goes in v5:
time: 88.6 us; the launch traced here: 88.1 us
  waiting for transfers between devices  36.1 us (41%)
  starting transfers between devices  34.5 us (39%)
  Pallas kernels  17.1 us (19%)
    all_to_all x1, waiting for transfers between devices, on_device(): got = lax.all_to_all(made, 'spec', 0, 0, tiled=True)  20 us
    pallas_call x5, Pallas kernels, call(): pl.pallas_call(kernel, out_shape=jax.tree.map(lambda s: jax.ShapeDtypeStr...  14.8 us
    all_to_all x2, waiting for transfers between devices, gather(): lax.all_to_all(pack, 'spec', 0, 0, tiled=True)  11.9 us
    all_to_all x2, starting transfers between devices, gather(): lax.all_to_all(pack, 'spec', 0, 0, tiled=True)  8.96 us
    ppermute x1, starting transfers between devices, on_device(): lax.ppermute(high_2, 'space', down)  7.86 us
    ppermute x1, starting transfers between devices, on_device(): lax.ppermute(high, 'space', down)  7.86 us
    all_to_all x1, starting transfers between devices, on_device(): got = lax.all_to_all(made, 'spec', 0, 0, tiled=True)  6 us
    ppermute x1, waiting for transfers between devices, on_device(): lax.ppermute(low, 'space', up)  2.62 us
  transfers between devices with their start and end apart: 7, of which 4 were waited for; matrix products, arithmetic and copies ran while one was open for 0% of the time, Pallas kernels for 7%

profile of v5, /device:TPU:256, one launch (start us, length us, event | category | flops | bytes accessed | tf_op | source)
XLA Modules:
  0.0 88.1 jit_solution(14625096941875932374)
XLA Ops:
  0.0 0.0 copy-start.5
  0.0 0.0 copy-start.6
  0.0 2.4 %pack.1 = (f32[8,3,16,4,128]{4,3,2,1,0:T(4,128)}, f32[8,3,11,4,128]{4,3,2,1,0:T(4,128)}) custom-call(f32[3,25,4,1024]{3,2,1,0:T(4,128)} %spectrum.1), custom_call_target="tpu_custom_call" | custom-call | tf_op jit(solution)/shard_map/pack/pallas_call | solution.py:390
  2.4 5.3 %all-to-all-start = ((f32[8,3,16,4,128]{4,3,2,1,0:T(4,128)}), f32[8,3,16,4,128]{4,3,2,1,0:T(4,128)S(1)}, u32[]{:S(2)}, u32[]{:S(2)}) async-start(f32[8,3,16,4,128]{4,3,2,1,0:T(4,128)} %get-tuple-element.19), calls=%async_computation | async-start | bytes 1572864 | tf_op jit(solution)/shard_map/all_to_all | solution.py:405
  7.7 0.0 copy-done.5
  7.7 0.0 copy-start
  7.7 0.0 copy-start.3
  7.7 0.0 copy-start.4
  7.8 0.0 copy-done.6
  7.8 11.9 %all-to-all-done = f32[8,3,16,4,128]{4,3,2,1,0:T(4,128)S(1)} async-done(((f32[8,3,16,4,128]{4,3,2,1,0:T(4,128)}), f32[8,3,16,4,128]{4,3,2,1,0:T(4,128)S(1)}, u32[]{:S(2)}, u32[]{:S(2)}) %all-to-all-start) | async-done | bytes 786464 | tf_op jit(solution)/shard_map/all_to_all | solution.py:405
  19.7 1.1 %halo.2 = (f32[256,4,128]{2,1,0:T(4,128)}, f32[256,4,128]{2,1,0:T(4,128)}) custom-call(f32[24,16,4,128]{3,2,1,0:T(4,128)S(1)} %bitcast.6, f32[2,4,1024]{2,1,0:T(4,128)S(1)} %pad_maximum_fusion.refs_1_.refs_0_), custom_call_target="tpu_custom_call" | custom-call | flops 1000 | bytes 4000000 | tf_op jit(solution)/shard_map/halo/pallas_call | solution.py:94
  20.8 3.6 %all-to-all-start.1 = ((f32[8,3,11,4,128]{4,3,2,1,0:T(4,128)}), f32[8,3,11,4,128]{4,3,2,1,0:T(4,128)S(1)}, u32[]{:S(2)}, u32[]{:S(2)}) async-start(f32[8,3,11,4,128]{4,3,2,1,0:T(4,128)} %get-tuple-element.22), calls=%async_computation.1 | async-start | bytes 1081344 | tf_op jit(solution)/shard_map/all_to_all | solution.py:405
  24.5 1.9 %collective-permute-start.2 = (f32[256,4,128]{2,1,0:T(4,128)}, f32[256,4,128]{2,1,0:T(4,128)S(1)}, u32[]{:S(2)}, u32[]{:S(2)}) collective-permute-start(f32[256,4,128]{2,1,0:T(4,128)} %get-tuple-element.25), channel_id=1, source_target_pairs={{0,8},{8,16},{16,24},{24,32},{32,40},{40,48},{48,56},{56,64},{64,7... | collective-permute-start | bytes 1572872 | tf_op jit(solution)/shard_map/ppermute | solution.py:418
  26.4 7.9 %collective-permute-start.3 = (f32[256,4,128]{2,1,0:T(4,128)}, f32[256,4,128]{2,1,0:T(4,128)S(1)}, u32[]{:S(2)}, u32[]{:S(2)}) collective-permute-start(f32[256,4,128]{2,1,0:T(4,128)} %get-tuple-element.26), channel_id=1, source_target_pairs={{8,0},{16,8},{24,16},{32,24},{40,32},{48,40},{56,48},{64,56},{72,6... | collective-permute-start | bytes 1572872 | tf_op jit(solution)/shard_map/ppermute | solution.py:418
  34.3 0.0 all-to-all-done.1
  34.3 0.8 halo.3
  35.1 1.9 %collective-permute-start = (f32[165,4,128]{2,1,0:T(4,128)}, f32[165,4,128]{2,1,0:T(4,128)S(1)}, u32[]{:S(2)}, u32[]{:S(2)}) collective-permute-start(f32[165,4,128]{2,1,0:T(4,128)} %get-tuple-element.23), channel_id=1, source_target_pairs={{0,8},{8,16},{16,24},{24,32},{32,40},{40,48},{48,56},{56,64},{64,7... | collective-permute-start | bytes 1013768 | tf_op jit(solution)/shard_map/ppermute | solution.py:420
  37.0 7.9 %collective-permute-start.1 = (f32[165,4,128]{2,1,0:T(4,128)S(1)}, f32[165,4,128]{2,1,0:T(4,128)S(1)}, u32[]{:S(2)}, u32[]{:S(2)}) collective-permute-start(f32[165,4,128]{2,1,0:T(4,128)S(1)} %get-tuple-element.24), channel_id=1, source_target_pairs={{8,0},{16,8},{24,16},{32,24},{40,32},{48,40},{56,48},{64,56},{72,6... | collective-permute-start | bytes 1013768 | tf_op jit(solution)/shard_map/ppermute | solution.py:420
  44.9 2.6 %collective-permute-done.2.south = f32[256,4,128]{2,1,0:T(4,128)S(1)} collective-permute-done((f32[256,4,128]{2,1,0:T(4,128)}, f32[256,4,128]{2,1,0:T(4,128)S(1)}, u32[]{:S(2)}, u32[]{:S(2)}) %collective-permute-start.2) | collective-permute-done | bytes 524320 | tf_op jit(solution)/shard_map/ppermute | solution.py:418
  47.5 0.0 collective-permute-done.3.north
  47.5 0.0 copy-done
  47.5 0.0 copy-done.3
  47.5 0.0 copy-done.4
  47.5 5.3 %steps.2 = (f32[8,91,4,128]{3,2,1,0:T(4,128)S(1)}, f32[2,2,10,8,128]{4,3,2,1,0:T(8,128)S(1)}) custom-call(s32[1]{0:T(128)} %bitcast.group, f32[25,18]{1,0:T(8,128)S(1)} %copy-done, f32[25]{0:T(128)S(1)} %copy-done.3, f32[25]{0:T(128)S(1)} %copy-done.4, f32[24,16,4,128]{3,2,1,0:T(4,128)S(1)} %bitcast.7, f32[256,4,128]{2,1,0:T(4,128)S(1)} %collective-permute-done.2.south, ...), custom_call_target="tpu_custom_call" | custom-call | flops 1000 | bytes 20000000 | tf_op jit(solution)/shard_map/steps/pallas_call | solution.py:94
  52.9 0.0 collective-permute-done.south
  52.9 1.6 %collective-permute-done.1.north = f32[165,4,128]{2,1,0:T(4,128)S(1)} collective-permute-done((f32[165,4,128]{2,1,0:T(4,128)S(1)}, f32[165,4,128]{2,1,0:T(4,128)S(1)}, u32[]{:S(2)}, u32[]{:S(2)}) %collective-permute-start.1) | collective-permute-done | bytes 337952 | tf_op jit(solution)/shard_map/ppermute | solution.py:420
  54.5 5.4 %steps.3 = f32[8,91,4,128]{3,2,1,0:T(4,128)} custom-call(s32[1]{0:T(128)} %bitcast.group, f32[25,18]{1,0:T(8,128)S(1)} %copy-done, f32[25]{0:T(128)S(1)} %copy-done.3, f32[25]{0:T(128)S(1)} %copy-done.4, f32[24,11,4,128]{3,2,1,0:T(4,128)S(1)} %bitcast.9, f32[165,4,128]{2,1,0:T(4,128)S(1)} %collective-permute-done.south, ...), custom_call_target="tpu_custom_call" | custom-call | flops 1000 | bytes 20000000 | tf_op jit(solution)/shard_map/steps/pallas_call | solution.py:94
  59.9 0.0 copy-start.8
  59.9 0.0 copy-start.7
  59.9 0.0 copy-start.1
  59.9 0.0 copy-start.2
  59.9 6.0 %all-to-all-start.2 = ((f32[8,91,4,128]{3,2,1,0:T(4,128)}), f32[8,91,4,128]{3,2,1,0:T(4,128)S(1)}, u32[]{:S(2)}, u32[]{:S(2)}) async-start(f32[8,91,4,128]{3,2,1,0:T(4,128)} %steps.3), calls=%async_computation.2 | async-start | bytes 2981888 | tf_op jit(solution)/shard_map/all_to_all | solution.py:423
  65.9 0.0 copy-done.8
  65.9 0.1 dynamic_slice.6.cos
  66.0 0.0 copy-done.7
  66.0 0.1 dynamic_slice.7.sin
  66.0 20.0 %all-to-all-done.2.got = f32[8,91,4,128]{3,2,1,0:T(4,128)S(1)} async-done(((f32[8,91,4,128]{3,2,1,0:T(4,128)}), f32[8,91,4,128]{3,2,1,0:T(4,128)S(1)}, u32[]{:S(2)}, u32[]{:S(2)}) %all-to-all-start.2) | async-done | bytes 1490976 | tf_op jit(solution)/shard_map/all_to_all | solution.py:423
  86.0 0.0 copy-done.1
  86.0 0.0 copy-done.2
  86.0 2.1 %source.1 = f32[3,25,4,1024]{3,2,1,0:T(4,128)} custom-call(f32[3]{0:T(128)S(1)} %dynamic_slice.6.cos, f32[3]{0:T(128)S(1)} %dynamic_slice.7.sin, f32[8,91,4,128]{3,2,1,0:T(4,128)S(1)} %all-to-all-done.2.got, f32[4,1024]{1,0:T(4,128)S(1)} %copy-done.1, f32[4,1024]{1,0:T(4,128)S(1)} %copy-done.2), custom_call_target="tpu_custom_call" | custom-call | flops 1000 | bytes 4000000 | tf_op jit(solution)/shard_map/source/pallas_call | solution.py:94
  (2 shorter events, 0.0 us)
Async XLA Ops:
  0.0 7.7 %copy-start.5 = (s32[4,1024]{1,0:T(4,128)S(1)}, s32[4,1024]{1,0:T(4,128)}, u32[]{:S(2)}) copy-start(s32[4,1024]{1,0:T(4,128)} %param.12) | copy-start | bytes 49156
  0.0 7.8 %copy-start.6 = (f32[4,1024]{1,0:T(4,128)S(1)}, f32[4,1024]{1,0:T(4,128)}, u32[]{:S(2)}) copy-start(f32[4,1024]{1,0:T(4,128)} %param.13) | copy-start | bytes 49156
  2.4 17.3 %all-to-all-start = ((f32[8,3,16,4,128]{4,3,2,1,0:T(4,128)}), f32[8,3,16,4,128]{4,3,2,1,0:T(4,128)S(1)}, u32[]{:S(2)}, u32[]{:S(2)}) async-start(f32[8,3,16,4,128]{4,3,2,1,0:T(4,128)} %get-tuple-element.19), calls=%async_computation | async-start | bytes 1572864 | tf_op jit(solution)/shard_map/all_to_all | solution.py:405
  7.7 39.8 %copy-start = (f32[25,18]{1,0:T(8,128)S(1)}, f32[25,18]{1,0:T(8,128)}, u32[]{:S(2)}) copy-start(f32[25,18]{1,0:T(8,128)} %constant.22.clone.coef) | copy-start | bytes 5404
  7.7 39.8 %copy-start.3 = (f32[25]{0:T(128)S(1)}, f32[25]{0:T(128)}, u32[]{:S(2)}) copy-start(f32[25]{0:T(128)} %constant.23.clone.rfac) | copy-start | bytes 304
  7.7 39.8 %copy-start.4 = (f32[25]{0:T(128)S(1)}, f32[25]{0:T(128)}, u32[]{:S(2)}) copy-start(f32[25]{0:T(128)} %constant.24.clone.frsq) | copy-start | bytes 304
  20.8 13.4 %all-to-all-start.1 = ((f32[8,3,11,4,128]{4,3,2,1,0:T(4,128)}), f32[8,3,11,4,128]{4,3,2,1,0:T(4,128)S(1)}, u32[]{:S(2)}, u32[]{:S(2)}) async-start(f32[8,3,11,4,128]{4,3,2,1,0:T(4,128)} %get-tuple-element.22), calls=%async_computation.1 | async-start | bytes 1081344 | tf_op jit(solution)/shard_map/all_to_all | solution.py:405
  24.5 23.0 %collective-permute-start.2 = (f32[256,4,128]{2,1,0:T(4,128)}, f32[256,4,128]{2,1,0:T(4,128)S(1)}, u32[]{:S(2)}, u32[]{:S(2)}) collective-permute-start(f32[256,4,128]{2,1,0:T(4,128)} %get-tuple-element.25), channel_id=1, source_target_pairs={{0,8},{8,16},{16,24},{24,32},{32,40},{40,48},{48,56},{56,64},{64,7... | collective-permute-start | bytes 1572872 | tf_op jit(solution)/shard_map/ppermute | solution.py:418
  26.4 21.1 %collective-permute-start.3 = (f32[256,4,128]{2,1,0:T(4,128)}, f32[256,4,128]{2,1,0:T(4,128)S(1)}, u32[]{:S(2)}, u32[]{:S(2)}) collective-permute-start(f32[256,4,128]{2,1,0:T(4,128)} %get-tuple-element.26), channel_id=1, source_target_pairs={{8,0},{16,8},{24,16},{32,24},{40,32},{48,40},{56,48},{64,56},{72,6... | collective-permute-start | bytes 1572872 | tf_op jit(solution)/shard_map/ppermute | solution.py:418
  35.1 17.8 %collective-permute-start = (f32[165,4,128]{2,1,0:T(4,128)}, f32[165,4,128]{2,1,0:T(4,128)S(1)}, u32[]{:S(2)}, u32[]{:S(2)}) collective-permute-start(f32[165,4,128]{2,1,0:T(4,128)} %get-tuple-element.23), channel_id=1, source_target_pairs={{0,8},{8,16},{16,24},{24,32},{32,40},{40,48},{48,56},{56,64},{64,7... | collective-permute-start | bytes 1013768 | tf_op jit(solution)/shard_map/ppermute | solution.py:420
  37.0 17.5 %collective-permute-start.1 = (f32[165,4,128]{2,1,0:T(4,128)S(1)}, f32[165,4,128]{2,1,0:T(4,128)S(1)}, u32[]{:S(2)}, u32[]{:S(2)}) collective-permute-start(f32[165,4,128]{2,1,0:T(4,128)S(1)} %get-tuple-element.24), channel_id=1, source_target_pairs={{8,0},{16,8},{24,16},{32,24},{40,32},{48,40},{56,48},{64,56},{72,6... | collective-permute-start | bytes 1013768 | tf_op jit(solution)/shard_map/ppermute | solution.py:420
  59.9 6.0 %copy-start.8 = (f32[24]{0:T(128)S(1)}, f32[24]{0:T(128)}, u32[]{:S(2)}) copy-start(f32[24]{0:T(128)} %constant.25.clone) | copy-start | bytes 292
  59.9 6.1 %copy-start.7 = (f32[24]{0:T(128)S(1)}, f32[24]{0:T(128)}, u32[]{:S(2)}) copy-start(f32[24]{0:T(128)} %constant.26.clone) | copy-start | bytes 292
  59.9 26.2 %copy-start.1 = (f32[4,1024]{1,0:T(4,128)S(1)}, f32[4,1024]{1,0:T(4,128)}, u32[]{:S(2)}) copy-start(f32[4,1024]{1,0:T(4,128)} %wind_u.1) | copy-start | bytes 49156
  59.9 26.2 %copy-start.2 = (f32[4,1024]{1,0:T(4,128)S(1)}, f32[4,1024]{1,0:T(4,128)}, u32[]{:S(2)}) copy-start(f32[4,1024]{1,0:T(4,128)} %wind_v.1) | copy-start | bytes 49156
  59.9 26.1 %all-to-all-start.2 = ((f32[8,91,4,128]{3,2,1,0:T(4,128)}), f32[8,91,4,128]{3,2,1,0:T(4,128)S(1)}, u32[]{:S(2)}, u32[]{:S(2)}) async-start(f32[8,91,4,128]{3,2,1,0:T(4,128)} %steps.3), calls=%async_computation.2 | async-start | bytes 2981888 | tf_op jit(solution)/shard_map/all_to_all | solution.py:423

commit v6 on v5

--- a/solution.py
+++ b/solution.py
@@ -12,6 +12,7 @@
 FREQS = 25
 SUB = 4
 INTERPRET = False
+UNROLL = True
 LANES = 128
 BLOCKS = 8
 
@@ -50,7 +51,8 @@
 FULL = 3
 CHUNKS = ((0, 2, False), (2, 1, True))
 WHOLE = FULL * BLOCKS
-TILES = WHOLE + 3
+WINDOW = 2
+HALF = LANES // 2
 SUMS_AT = 3 * (WHOLE + 1)
 MADE = SUMS_AT + 2 * BLOCKS
 
@@ -75,7 +77,7 @@
 
 
 def tiles_of(chunk):
-    return chunk[1] * BLOCKS + (3 if chunk[2] else 0)
+    return chunk[1] * BLOCKS + (WINDOW if chunk[2] else 0)
 
 
 def slots_of(chunk):
@@ -104,63 +106,85 @@
     )(*args)
 
 
-def pack_kernel(spectrum, *refs):
-    outs, (x, arrived) = refs[: len(CHUNKS)], refs[len(CHUNKS) :]
+def first_pack_kernel(spectrum, out, done):
+    begin, count, _ = CHUNKS[0]
+    copies = [
+        pltpu.make_async_copy(
+            spectrum.at[d, pl.ds(j * FULL + begin, count)], out.at[j, d], done.at[j, d]
+        )
+        for d in range(3)
+        for j in range(BLOCKS)
+    ]
+    for copy in copies:
+        copy.start()
+    for copy in copies:
+        copy.wait()
+
+
+def last_pack_kernel(spectrum, out, x, arrived):
+    begin, count, _ = CHUNKS[1]
     copies = [pltpu.make_async_copy(spectrum.at[d], x.at[d], arrived.at[d]) for d in range(3)]
     for copy in copies:
         copy.start()
-    zero = jnp.zeros((4, LANES), jnp.float32)
+    zero = jnp.zeros((4, HALF), jnp.float32)
     for d in range(3):
         copies[d].wait()
-        for (begin, count, tail), out in zip(CHUNKS, outs):
-            for j in range(BLOCKS):
-                for i in range(count):
-                    for l in range(BLOCKS):
-                        value = x[d, j * FULL + begin + i, :, l * LANES : (l + 1) * LANES]
-                        out[j, d, i * BLOCKS + l] = value
-                for i in range(3 if tail else 0):
-                    l = j + i - 1
-                    inside = 0 <= l < BLOCKS
-                    value = x[d, FREQS - 1, :, l * LANES : (l + 1) * LANES] if inside else zero
-                    out[j, d, count * BLOCKS + i] = value
+        for j in range(BLOCKS):
+            for i in range(count):
+                for l in range(BLOCKS):
+                    value = x[d, j * FULL + begin + i, :, l * LANES : (l + 1) * LANES]
+                    out[j, d, i * BLOCKS + l] = value
+            left, right = j * LANES - HALF, (j + 1) * LANES + HALF
+            value = x[d, FREQS - 1, :, max(left, 0) : min(right, BLOCKS * LANES)]
+            if left < 0:
+                value = jnp.concatenate([zero, value], axis=1)
+            if right > BLOCKS * LANES:
+                value = jnp.concatenate([value, zero], axis=1)
+            for i in range(WINDOW):
+                out[j, d, count * BLOCKS + i] = value[:, i * LANES : (i + 1) * LANES]
 
 
 def halo_kernel(tiles, with_maps, *refs):
     if with_maps:
-        own, maps, up, down = refs
+        own, maps, up, down, done = refs
+    else:
+        own, up, down, done = refs
+    n = len(SOUTH)
+    copies = [
+        pltpu.make_async_copy(own.at[pl.ds(dirs[0], n)], ref.at[pl.ds(0, n)], done.at[i])
+        for i, (dirs, ref) in enumerate(((SOUTH, up), (NORTH, down)))
+    ]
+    for copy in copies:
+        copy.start()
+    if with_maps:
         for k in range(2):
             for l in range(BLOCKS):
                 value = maps[k, :, l * LANES : (l + 1) * LANES]
-                up[PLANES * tiles + k * BLOCKS + l] = value
-                down[PLANES * tiles + k * BLOCKS + l] = value
-    else:
-        own, up, down = refs
+                up[PLANES, k * BLOCKS + l] = value
+                down[PLANES, k * BLOCKS + l] = value
     ends = {
         "s": (SOUTH[-1], SOUTH[0]),
         "n": (NORTH[0], NORTH[-1]),
     }
-    n = len(SOUTH)
 
     def body(t, carry):
-        for i, d in enumerate(SOUTH):
-            up[i * tiles + t] = own[d, t]
-        for i, d in enumerate(NORTH):
-            down[i * tiles + t] = own[d, t]
         top, low = ends["s"]
         a = [own[(top + k) % DIRS, t] for k in range(1, 4)]
         b = [own[(low - k) % DIRS, t] for k in range(1, 4)]
-        up[n * tiles + t] = jnp.concatenate([a[2][3:4], a[0][1:4]], axis=0)
-        up[(n + 1) * tiles + t] = jnp.concatenate([b[1][2:4], a[1][2:4]], axis=0)
-        up[(n + 2) * tiles + t] = jnp.concatenate([b[2][3:4], b[0][1:4]], axis=0)
+        up[n, t] = jnp.concatenate([a[2][3:4], a[0][1:4]], axis=0)
+        up[n + 1, t] = jnp.concatenate([b[1][2:4], a[1][2:4]], axis=0)
+        up[n + 2, t] = jnp.concatenate([b[2][3:4], b[0][1:4]], axis=0)
         low, top = ends["n"]
         a = [own[(low - k) % DIRS, t] for k in range(1, 4)]
         b = [own[(top + k) % DIRS, t] for k in range(1, 4)]
-        down[n * tiles + t] = jnp.concatenate([a[0][0:3], a[2][0:1]], axis=0)
-        down[(n + 1) * tiles + t] = jnp.concatenate([a[1][0:2], b[1][0:2]], axis=0)
-        down[(n + 2) * tiles + t] = jnp.concatenate([b[0][0:3], b[2][0:1]], axis=0)
+        down[n, t] = jnp.concatenate([a[0][0:3], a[2][0:1]], axis=0)
+        down[n + 1, t] = jnp.concatenate([a[1][0:2], b[1][0:2]], axis=0)
+        down[n + 2, t] = jnp.concatenate([b[0][0:3], b[2][0:1]], axis=0)
         return carry
 
-    lax.fori_loop(0, tiles, body, 0, unroll=4)
+    lax.fori_loop(0, tiles, body, 0, unroll=2)
+    for copy in copies:
+        copy.wait()
 
 
 def step_kernel(chunk, first_call, group, coef, rfac, frsq, own, south, north, *refs):
@@ -181,16 +205,16 @@
 
     def map_of(t):
         if isinstance(t, int):
-            return me + t - whole
+            return BLOCKS + 2 + t - whole
         l = t % BLOCKS + 1
-        return jnp.where(t < whole, l, me + t - whole) if tail else l
+        return jnp.where(t < whole, l, BLOCKS + 2 + t - whole) if tail else l
 
     def slot_of(t):
         return t + t // BLOCKS + 1
 
     lane = lax.broadcasted_iota(jnp.int32, (8, LANES), 1)
     row = lax.broadcasted_iota(jnp.int32, (8, LANES), 0)
-    start, end, mine = lane == 0, lane == LANES - 1, row < 4
+    start, end, mine, half = lane == 0, lane == LANES - 1, row < 4, lane < HALF
     zero = jnp.zeros((8, LANES), jnp.float32)
     for p in [i * (BLOCKS + 1) for i in range(count + 1)] + ([slots - 1] if tail else []):
         for d in range(DIRS):
@@ -201,14 +225,16 @@
             ex_b[i, p] = zero
 
     if first_call:
-        at = PLANES * tiles
         for k in range(2):
             for w, ref in enumerate((south, north)):
                 around[k, w, 0] = zero
                 around[k, w, BLOCKS + 1] = zero
                 for l in range(BLOCKS):
                     mid = maps[k, :, l * LANES : (l + 1) * LANES]
-                    around[k, w, l + 1] = jnp.concatenate([mid, ref[at + k * BLOCKS + l]], axis=0)
+                    around[k, w, l + 1] = jnp.concatenate([mid, ref[PLANES, k * BLOCKS + l]], axis=0)
+                for i in range(WINDOW):
+                    left, right = around[k, w, me + i], around[k, w, me + i + 1]
+                    around[k, w, BLOCKS + 2 + i] = pltpu.roll(jnp.where(half, right, left), HALF, 1)
 
     def fill(t, carry):
         slot, m = slot_of(t), map_of(t)
@@ -219,11 +245,11 @@
             return jnp.concatenate([own[d, t], rows], axis=0) * seas[w]
 
         for i, d in enumerate(SOUTH):
-            st_a[d, slot] = whole_tile("s", d, south[i * tiles + t])
+            st_a[d, slot] = whole_tile("s", d, south[i, t])
         for i, d in enumerate(NORTH):
-            st_a[d, slot] = whole_tile("n", d, north[i * tiles + t])
+            st_a[d, slot] = whole_tile("n", d, north[i, t])
         for w, ref in (("s", south), ("n", north)):
-            a, b, c = (ref[(n + i) * tiles + t] for i in range(3))
+            a, b, c = (ref[n + i, t] for i in range(3))
             swap = jnp.concatenate([b[2:4], b[0:2]], axis=0)
             pick = slice(0, 1) if w == "s" else slice(3, 4)
             far_a = jnp.broadcast_to(a[pick], (4, LANES))
@@ -254,10 +280,7 @@
                     out[s, d * WHOLE + i] = given[s, d * WHOLE + i]
 
     def keep(t, d, new):
-        if isinstance(t, int):
-            out[d // 3, 3 * WHOLE + d % 3] = new[0:4]
-        else:
-            out[d // 3, (d % 3) * WHOLE + origin + t] = new[0:4]
+        out[d // 3, (d % 3) * WHOLE + origin + t] = new[0:4]
 
     def add_up(t, f, total):
         place = SUMS_AT + (me if isinstance(t, int) else t % BLOCKS)
@@ -305,7 +328,7 @@
             total = None
             for d in range(DIRS):
                 new = update(window(d), d)
-                if step < SUB - 1:
+                if step < SUB - 1 or isinstance(t, int):
                     fresh[d] = new
                     dst[d, slot] = new
                 else:
@@ -325,11 +348,19 @@
         (src, src_ex), (dst, dst_ex) = bufs[step % 2], bufs[(step + 1) % 2]
         body = make(step, src, src_ex, dst, dst_ex)
         if step < SUB - 1:
-            lax.fori_loop(0, tiles, body, 0, unroll=4)
+            lax.fori_loop(0, tiles, body, 0, unroll=(tiles if tail else BLOCKS) if UNROLL else 1)
         else:
-            lax.fori_loop(0, whole, body, 0, unroll=4)
-            if tail:
-                body(whole + 1, 0)
+            lax.fori_loop(0, whole, body, 0, unroll=BLOCKS if UNROLL else 1)
+    if tail:
+        for t in range(whole, tiles):
+            body(t, 0)
+        total = None
+        for d in range(DIRS):
+            left, right = dst[d, slot_of(whole)], dst[d, slot_of(whole + 1)]
+            new = pltpu.roll(jnp.where(half, right, left), HALF, 1)
+            out[d // 3, 3 * WHOLE + d % 3] = new[0:4]
+            total = new if total is None else total + new
+        add_up(whole, FREQS - 1, total)
     if not first_call:
         for i in range(2 * BLOCKS):
             value = out[0, SUMS_AT + i]
@@ -343,7 +374,7 @@
     extra = pltpu.VMEM((len(EXTRAS), slots, 8, LANES), jnp.float32)
     out = [(BLOCKS, MADE, 4, LANES)]
     if first_call:
-        out.append((2, 2, BLOCKS + 2, 8, LANES))
+        out.append((2, 2, BLOCKS + 2 + WINDOW, 8, LANES))
     args = (group, COEF, RFAC, FR * FR, own, south, north, *rest)
     return call(
         functools.partial(step_kernel, chunk, first_call),
@@ -356,27 +387,50 @@
     )
 
 
-def source_kernel(cos, sin, got, wind_u, wind_v, out):
+def source_kernel(cos, sin, got, wind_u, wind_v, out, made, shrink, done):
     inverse = 1.0 / (DIRS * FREQS)
-    for t in range(BLOCKS):
-        cols = slice(t * LANES, (t + 1) * LANES)
+    columns = [slice(t * LANES, (t + 1) * LANES) for t in range(BLOCKS)]
+    for t, cols in enumerate(columns):
         m0 = got[0, SUMS_AT + t]
         m2 = got[0, SUMS_AT + BLOCKS + t]
         for j in range(1, BLOCKS):
             m0 = m0 + got[j, SUMS_AT + t]
             m2 = m2 + got[j, SUMS_AT + BLOCKS + t]
         ratio = 0.5 * (m2 * inverse) / (1.0 + m0 * inverse)
-        u, v = wind_u[:, cols], wind_v[:, cols]
-        gain = [0.5 * jnp.maximum(u * cos[d] + v * sin[d], 0.0) for d in range(3)]
         for f in range(FREQS):
-            fr = float(FR[f])
-            shrink = 1.0 / (1.0 + ratio * (fr * fr))
-            for d in range(3):
+            shrink[f, :, cols] = 1.0 / (1.0 + ratio * float(FR[f] * FR[f]))
+    copies = []
+    for d in range(3):
+        for t, cols in enumerate(columns):
+            along = wind_u[:, cols] * cos[d] + wind_v[:, cols] * sin[d]
+            gain = 0.5 * jnp.maximum(along, 0.0)
+            for f in range(FREQS):
                 if f < BLOCKS * FULL:
                     a = got[f // FULL, d * WHOLE + f % FULL * BLOCKS + t]
                 else:
                     a = got[t, 3 * WHOLE + d]
-                out[d, f, :, cols] = a * (1.0 + gain[d] * fr) * shrink
+                made[d, f, :, cols] = a * (1.0 + gain * float(FR[f])) * shrink[f, :, cols]
+        copies.append(pltpu.make_async_copy(made.at[d], out.at[d], done.at[d]))
+        copies[-1].start()
+    for copy in copies:
+        copy.wait()
+
+
+def moving(kernel, name, out, ins, out_space, args, scratch):
+    return pl.pallas_call(
+        kernel,
+        out_shape=[jax.ShapeDtypeStruct(s, jnp.float32) for s in out],
+        in_specs=ins,
+        out_specs=[out_space for _ in out],
+        scratch_shapes=scratch,
+        compiler_params=pltpu.CompilerParams(vmem_limit_bytes=60 * 1024 * 1024 if "pack" in name else VMEM_LIMIT),
+        interpret=INTERPRET,
+        name=name,
+    )(*args)
+
+
+def tiled(rows):
+    return jnp.swapaxes(rows.reshape(rows.shape[:-1] + (BLOCKS, LANES)), -2, -3)
 
 
 def on_device(spectrum, sea_mask, turning, wind_u, wind_v):
@@ -387,34 +441,46 @@
     down = [(j, i) for i, j in up]
 
     maps = jnp.stack([(sea_mask == 1).astype(jnp.float32), turning])
-    packs = pl.pallas_call(
-        pack_kernel,
-        out_shape=[
-            jax.ShapeDtypeStruct((BLOCKS, 3, tiles_of(c), 4, LANES), jnp.float32) for c in CHUNKS
-        ],
-        in_specs=[pl.BlockSpec(memory_space=pltpu.HBM)],
-        out_specs=[vmem() for _ in CHUNKS],
-        scratch_shapes=[pltpu.VMEM(spectrum.shape, jnp.float32), pltpu.SemaphoreType.DMA((3,))],
-        compiler_params=pltpu.CompilerParams(vmem_limit_bytes=60 * 1024 * 1024),
-        interpret=INTERPRET,
-        name="pack",
-    )(spectrum)
-
-    def gather(i, pack):
-        tiles = tiles_of(CHUNKS[i])
-        own = lax.all_to_all(pack, "spec", 0, 0, tiled=True).reshape(DIRS, tiles, 4, LANES)
-        size = PLANES * tiles + (2 * BLOCKS if i == 0 else 0)
-        return own, call(
-            functools.partial(halo_kernel, tiles, i == 0),
+    hbm = pl.BlockSpec(memory_space=pltpu.HBM)
+    room = pltpu.VMEM(spectrum.shape, jnp.float32)
+    first, last = CHUNKS
+    (pack,) = moving(
+        first_pack_kernel,
+        "first_pack",
+        [(BLOCKS, 3, first[1]) + spectrum.shape[2:]],
+        [hbm],
+        hbm,
+        (spectrum,),
+        [pltpu.SemaphoreType.DMA((BLOCKS, 3))],
+    )
+    (pack_2,) = moving(
+        last_pack_kernel,
+        "last_pack",
+        [(BLOCKS, 3, tiles_of(last), 4, LANES)],
+        [hbm],
+        vmem(),
+        (spectrum,),
+        [room, pltpu.SemaphoreType.DMA((3,))],
+    )
+
+    def edges(tiles, planes, *args):
+        return moving(
+            functools.partial(halo_kernel, tiles, len(args) > 1),
             "halo",
-            [(size, 4, LANES)] * 2,
-            (own, maps) if i == 0 else (own,),
-            0,
+            [(planes, tiles, 4, LANES)] * 2,
+            [vmem() for _ in args],
+            vmem(),
+            args,
+            [pltpu.SemaphoreType.DMA((2,))],
         )
 
-    own, (low, high) = gather(0, packs[0])
-    pack, low, high = lax.optimization_barrier((packs[1], low, high))
-    own_2, (low_2, high_2) = gather(1, pack)
+    own = lax.all_to_all(pack, "spec", 0, 0, tiled=True)
+    own = tiled(own).reshape(DIRS, tiles_of(first), 4, LANES)
+    low, high = edges(tiles_of(first), PLANES + 1, own, maps)
+    pack_2, low, high = lax.optimization_barrier((pack_2, low, high))
+    own_2 = lax.all_to_all(pack_2, "spec", 0, 0, tiled=True)
+    own_2 = own_2.reshape(DIRS, tiles_of(last), 4, LANES)
+    low_2, high_2 = edges(tiles_of(last), PLANES, own_2)
     south, north = lax.ppermute(low, "space", up), lax.ppermute(high, "space", down)
     south, north, _, _ = lax.optimization_barrier((south, north, low_2, high_2))
     south_2, north_2 = lax.ppermute(low_2, "space", up), lax.ppermute(high_2, "space", down)
@@ -423,13 +489,16 @@
     got = lax.all_to_all(made, "spec", 0, 0, tiled=True)
     cos = lax.dynamic_slice_in_dim(jnp.asarray(COS), me * 3, 3)
     sin = lax.dynamic_slice_in_dim(jnp.asarray(SIN), me * 3, 3)
-    return call(
+    (result,) = moving(
         source_kernel,
         "source",
-        (3, FREQS, 4, BLOCKS * LANES),
+        [spectrum.shape],
+        [smem(), smem(), vmem(), vmem(), vmem()],
+        hbm,
         (cos, sin, got, wind_u, wind_v),
-        2,
+        [room, pltpu.VMEM(spectrum.shape[1:], jnp.float32), pltpu.SemaphoreType.DMA((3,))],
     )
+    return result
 
 
 def solution(mesh):

time: 88.6 us -> 108 us (1.22)
  the two profiles are of different devices: /device:TPU:256 before, /device:TPU:448 now
where the time goes in v6:
time: 108 us; the launch traced here: 107 us
  Pallas kernels  41.9 us (39%)
  waiting for transfers between devices  33.5 us (31%)
  starting transfers between devices  31.6 us (29%)
    pallas_call x5, Pallas kernels, moving(): pl.pallas_call(kernel, out_shape=[jax.ShapeDtypeStruct(s, jnp.float32) fo...  32.1 us
    all_to_all x1, waiting for transfers between devices, on_device(): got = lax.all_to_all(made, 'spec', 0, 0, tiled=True)  20.4 us
    pallas_call x2, Pallas kernels, call(): pl.pallas_call(kernel, out_shape=jax.tree.map(lambda s: jax.ShapeDtypeStr...  9.83 us
    all_to_all x1, waiting for transfers between devices, on_device(): own = lax.all_to_all(pack, 'spec', 0, 0, tiled=True)  9.74 us
    ppermute x1, starting transfers between devices, on_device(): lax.ppermute(high, 'space', down)  6.65 us
    ppermute x1, starting transfers between devices, on_device(): lax.ppermute(high_2, 'space', down)  6.65 us
    all_to_all x1, starting transfers between devices, on_device(): got = lax.all_to_all(made, 'spec', 0, 0, tiled=True)  5.45 us
    all_to_all x1, starting transfers between devices, on_device(): own = lax.all_to_all(pack, 'spec', 0, 0, tiled=True)  5.32 us
  transfers between devices with their start and end apart: 7, of which 5 were waited for; matrix products, arithmetic and copies ran while one was open for 0% of the time, Pallas kernels for 9%

profile of v6, /device:TPU:448, one launch (start us, length us, event | category | flops | bytes accessed | tf_op | source)
XLA Modules:
  0.0 107.3 jit_solution(16552447384256050209)
XLA Ops:
  0.0 25.1 %first_pack.1 = f32[8,3,2,4,1024]{4,3,2,1,0:T(4,128)} custom-call(f32[3,25,4,1024]{3,2,1,0:T(4,128)} %spectrum.3), custom_call_target="tpu_custom_call" | custom-call | tf_op jit(solution)/shard_map/first_pack/pallas_call | solution.py:420
  25.1 0.0 copy-start.5
  25.2 0.0 copy-start.6
  25.2 5.3 %all-to-all-start = ((f32[8,3,2,4,1024]{4,3,2,1,0:T(4,128)}), f32[8,3,2,4,1024]{4,3,2,1,0:T(4,128)S(1)}, u32[]{:S(2)}, u32[]{:S(2)}) async-start(f32[8,3,2,4,1024]{4,3,2,1,0:T(4,128)} %first_pack.1), calls=%async_computation | async-start | bytes 1572864 | tf_op jit(solution)/shard_map/all_to_all | solution.py:477
  30.5 2.1 %last_pack.1 = f32[8,3,10,4,128]{4,3,2,1,0:T(4,128)} custom-call(f32[3,25,4,1024]{3,2,1,0:T(4,128)} %spectrum.3), custom_call_target="tpu_custom_call" | custom-call | tf_op jit(solution)/shard_map/last_pack/pallas_call | solution.py:420
  32.7 0.0 copy-done.5
  32.7 0.0 copy-start
  32.7 0.0 copy-start.3
  32.7 0.0 copy-start.4
  32.7 0.0 copy-done.6
  32.7 9.7 %all-to-all-done = f32[8,3,2,4,1024]{4,3,2,1,0:T(4,128)S(1)} async-done(((f32[8,3,2,4,1024]{4,3,2,1,0:T(4,128)}), f32[8,3,2,4,1024]{4,3,2,1,0:T(4,128)S(1)}, u32[]{:S(2)}, u32[]{:S(2)}) %all-to-all-start) | async-done | bytes 786464 | tf_op jit(solution)/shard_map/all_to_all | solution.py:477
  42.5 1.3 %halo.2 = (f32[16,16,4,128]{3,2,1,0:T(4,128)}, f32[16,16,4,128]{3,2,1,0:T(4,128)S(1)}) custom-call(f32[24,16,4,128]{3,2,1,0:T(4,128)S(1)} %bitcast.10, f32[2,4,1024]{2,1,0:T(4,128)S(1)} %pad_maximum_fusion.refs_1_.refs_0_), custom_call_target="tpu_custom_call" | custom-call | tf_op jit(solution)/shard_map/halo/pallas_call | solution.py:420
  43.8 3.6 %all-to-all-start.1 = ((f32[8,3,10,4,128]{4,3,2,1,0:T(4,128)}), f32[8,3,10,4,128]{4,3,2,1,0:T(4,128)S(1)}, u32[]{:S(2)}, u32[]{:S(2)}) async-start(f32[8,3,10,4,128]{4,3,2,1,0:T(4,128)} %last_pack.1), calls=%async_computation.1 | async-start | bytes 983040 | tf_op jit(solution)/shard_map/all_to_all | solution.py:481
  47.4 1.9 %collective-permute-start.2 = (f32[16,16,4,128]{3,2,1,0:T(4,128)}, f32[16,16,4,128]{3,2,1,0:T(4,128)S(1)}, u32[]{:S(2)}, u32[]{:S(2)}) collective-permute-start(f32[16,16,4,128]{3,2,1,0:T(4,128)} %get-tuple-element.21), channel_id=1, source_target_pairs={{0,8},{8,16},{16,24},{24,32},{32,40},{40,48},{48,56},{56,64},{64,7... | collective-permute-start | bytes 1572872 | tf_op jit(solution)/shard_map/ppermute | solution.py:484
  49.3 6.7 %collective-permute-start.3 = (f32[16,16,4,128]{3,2,1,0:T(4,128)S(1)}, f32[16,16,4,128]{3,2,1,0:T(4,128)S(1)}, u32[]{:S(2)}, u32[]{:S(2)}) collective-permute-start(f32[16,16,4,128]{3,2,1,0:T(4,128)S(1)} %get-tuple-element.22), channel_id=1, source_target_pairs={{8,0},{16,8},{24,16},{32,24},{40,32},{48,40},{56,48},{64,56},{72,6... | collective-permute-start | bytes 1572872 | tf_op jit(solution)/shard_map/ppermute | solution.py:484
  56.0 0.8 all-to-all-done.1
  56.8 1.5 %halo.3 = (f32[15,10,4,128]{3,2,1,0:T(4,128)}, f32[15,10,4,128]{3,2,1,0:T(4,128)}) custom-call(f32[24,10,4,128]{3,2,1,0:T(4,128)S(1)} %bitcast.12), custom_call_target="tpu_custom_call" | custom-call | tf_op jit(solution)/shard_map/halo/pallas_call | solution.py:420
  58.3 1.9 %collective-permute-start = (f32[15,10,4,128]{3,2,1,0:T(4,128)}, f32[15,10,4,128]{3,2,1,0:T(4,128)S(1)}, u32[]{:S(2)}, u32[]{:S(2)}) collective-permute-start(f32[15,10,4,128]{3,2,1,0:T(4,128)} %get-tuple-element.19), channel_id=1, source_target_pairs={{0,8},{8,16},{16,24},{24,32},{32,40},{40,48},{48,56},{56,64},{64,7... | collective-permute-start | bytes 921608 | tf_op jit(solution)/shard_map/ppermute | solution.py:486
  60.2 6.7 %collective-permute-start.1 = (f32[15,10,4,128]{3,2,1,0:T(4,128)}, f32[15,10,4,128]{3,2,1,0:T(4,128)S(1)}, u32[]{:S(2)}, u32[]{:S(2)}) collective-permute-start(f32[15,10,4,128]{3,2,1,0:T(4,128)} %get-tuple-element.20), channel_id=1, source_target_pairs={{8,0},{16,8},{24,16},{32,24},{40,32},{48,40},{56,48},{64,56},{72,6... | collective-permute-start | bytes 921608 | tf_op jit(solution)/shard_map/ppermute | solution.py:486
  66.9 2.4 %collective-permute-done.2.south = f32[16,16,4,128]{3,2,1,0:T(4,128)S(1)} collective-permute-done((f32[16,16,4,128]{3,2,1,0:T(4,128)}, f32[16,16,4,128]{3,2,1,0:T(4,128)S(1)}, u32[]{:S(2)}, u32[]{:S(2)}) %collective-permute-start.2) | collective-permute-done | bytes 524320 | tf_op jit(solution)/shard_map/ppermute | solution.py:484
  69.3 0.0 collective-permute-done.3.north
  69.3 0.0 copy-done
  69.3 0.0 copy-done.3
  69.3 0.0 copy-done.4
  69.3 5.5 %steps.2 = (f32[8,91,4,128]{3,2,1,0:T(4,128)S(1)}, f32[2,2,12,8,128]{4,3,2,1,0:T(8,128)S(1)}) custom-call(s32[1]{0:T(128)} %bitcast.group, f32[25,18]{1,0:T(8,128)S(1)} %copy-done, f32[25]{0:T(128)S(1)} %copy-done.3, f32[25]{0:T(128)S(1)} %copy-done.4, f32[24,16,4,128]{3,2,1,0:T(4,128)S(1)} %bitcast.11, f32[16,16,4,128]{3,2,1,0:T(4,128)S(1)} %collective-permute-done.2.south, ...), custom_call_target="tpu_custom_call" | custom-call | flops 1000 | bytes 20000000 | tf_op jit(solution)/shard_map/steps/pallas_call | solution.py:96
  74.9 0.0 collective-permute-done.south
  74.9 0.1 collective-permute-done.1.north
  75.0 4.3 %steps.3 = f32[8,91,4,128]{3,2,1,0:T(4,128)} custom-call(s32[1]{0:T(128)} %bitcast.group, f32[25,18]{1,0:T(8,128)S(1)} %copy-done, f32[25]{0:T(128)S(1)} %copy-done.3, f32[25]{0:T(128)S(1)} %copy-done.4, f32[24,10,4,128]{3,2,1,0:T(4,128)S(1)} %bitcast.13, f32[15,10,4,128]{3,2,1,0:T(4,128)S(1)} %collective-permute-done.south, ...), custom_call_target="tpu_custom_call" | custom-call | flops 1000 | bytes 20000000 | tf_op jit(solution)/shard_map/steps/pallas_call | solution.py:96
  79.3 0.0 copy-start.8
  79.3 0.0 copy-start.7
  79.3 0.0 copy-start.1
  79.3 0.0 copy-start.2
  79.3 5.5 %all-to-all-start.2 = ((f32[8,91,4,128]{3,2,1,0:T(4,128)}), f32[8,91,4,128]{3,2,1,0:T(4,128)S(1)}, u32[]{:S(2)}, u32[]{:S(2)}) async-start(f32[8,91,4,128]{3,2,1,0:T(4,128)} %steps.3), calls=%async_computation.2 | async-start | bytes 2981888 | tf_op jit(solution)/shard_map/all_to_all | solution.py:489
  84.8 0.0 copy-done.8
  84.8 0.1 dynamic_slice.6.cos
  84.8 0.0 copy-done.7
  84.8 0.1 dynamic_slice.7.sin
  84.9 20.4 %all-to-all-done.2.got = f32[8,91,4,128]{3,2,1,0:T(4,128)S(1)} async-done(((f32[8,91,4,128]{3,2,1,0:T(4,128)}), f32[8,91,4,128]{3,2,1,0:T(4,128)S(1)}, u32[]{:S(2)}, u32[]{:S(2)}) %all-to-all-start.2) | async-done | bytes 1490976 | tf_op jit(solution)/shard_map/all_to_all | solution.py:489
  105.3 0.0 copy-done.1
  105.3 0.0 copy-done.2
  105.3 2.0 %source.1 = f32[3,25,4,1024]{3,2,1,0:T(4,128)} custom-call(f32[3]{0:T(128)S(1)} %dynamic_slice.6.cos, f32[3]{0:T(128)S(1)} %dynamic_slice.7.sin, f32[8,91,4,128]{3,2,1,0:T(4,128)S(1)} %all-to-all-done.2.got, f32[4,1024]{1,0:T(4,128)S(1)} %copy-done.1, f32[4,1024]{1,0:T(4,128)S(1)} %copy-done.2), custom_call_target="tpu_custom_call" | custom-call | tf_op jit(solution)/shard_map/source/pallas_call | solution.py:420
  (2 shorter events, 0.0 us)
Async XLA Ops:
  25.1 7.5 %copy-start.5 = (s32[4,1024]{1,0:T(4,128)S(1)}, s32[4,1024]{1,0:T(4,128)}, u32[]{:S(2)}) copy-start(s32[4,1024]{1,0:T(4,128)} %param.12) | copy-start | bytes 49156
  25.2 7.6 %copy-start.6 = (f32[4,1024]{1,0:T(4,128)S(1)}, f32[4,1024]{1,0:T(4,128)}, u32[]{:S(2)}) copy-start(f32[4,1024]{1,0:T(4,128)} %param.13) | copy-start | bytes 49156
  25.2 17.3 %all-to-all-start = ((f32[8,3,2,4,1024]{4,3,2,1,0:T(4,128)}), f32[8,3,2,4,1024]{4,3,2,1,0:T(4,128)S(1)}, u32[]{:S(2)}, u32[]{:S(2)}) async-start(f32[8,3,2,4,1024]{4,3,2,1,0:T(4,128)} %first_pack.1), calls=%async_computation | async-start | bytes 1572864 | tf_op jit(solution)/shard_map/all_to_all | solution.py:477
  32.7 36.6 %copy-start = (f32[25,18]{1,0:T(8,128)S(1)}, f32[25,18]{1,0:T(8,128)}, u32[]{:S(2)}) copy-start(f32[25,18]{1,0:T(8,128)} %constant.22.clone.coef) | copy-start | bytes 5404
  32.7 36.6 %copy-start.3 = (f32[25]{0:T(128)S(1)}, f32[25]{0:T(128)}, u32[]{:S(2)}) copy-start(f32[25]{0:T(128)} %constant.23.clone.rfac) | copy-start | bytes 304
  32.7 36.6 %copy-start.4 = (f32[25]{0:T(128)S(1)}, f32[25]{0:T(128)}, u32[]{:S(2)}) copy-start(f32[25]{0:T(128)} %constant.24.clone.frsq) | copy-start | bytes 304
  43.8 13.0 %all-to-all-start.1 = ((f32[8,3,10,4,128]{4,3,2,1,0:T(4,128)}), f32[8,3,10,4,128]{4,3,2,1,0:T(4,128)S(1)}, u32[]{:S(2)}, u32[]{:S(2)}) async-start(f32[8,3,10,4,128]{4,3,2,1,0:T(4,128)} %last_pack.1), calls=%async_computation.1 | async-start | bytes 983040 | tf_op jit(solution)/shard_map/all_to_all | solution.py:481
  47.4 21.9 %collective-permute-start.2 = (f32[16,16,4,128]{3,2,1,0:T(4,128)}, f32[16,16,4,128]{3,2,1,0:T(4,128)S(1)}, u32[]{:S(2)}, u32[]{:S(2)}) collective-permute-start(f32[16,16,4,128]{3,2,1,0:T(4,128)} %get-tuple-element.21), channel_id=1, source_target_pairs={{0,8},{8,16},{16,24},{24,32},{32,40},{40,48},{48,56},{56,64},{64,7... | collective-permute-start | bytes 1572872 | tf_op jit(solution)/shard_map/ppermute | solution.py:484
  49.3 20.0 %collective-permute-start.3 = (f32[16,16,4,128]{3,2,1,0:T(4,128)S(1)}, f32[16,16,4,128]{3,2,1,0:T(4,128)S(1)}, u32[]{:S(2)}, u32[]{:S(2)}) collective-permute-start(f32[16,16,4,128]{3,2,1,0:T(4,128)S(1)} %get-tuple-element.22), channel_id=1, source_target_pairs={{8,0},{16,8},{24,16},{32,24},{40,32},{48,40},{56,48},{64,56},{72,6... | collective-permute-start | bytes 1572872 | tf_op jit(solution)/shard_map/ppermute | solution.py:484
  58.3 16.5 %collective-permute-start = (f32[15,10,4,128]{3,2,1,0:T(4,128)}, f32[15,10,4,128]{3,2,1,0:T(4,128)S(1)}, u32[]{:S(2)}, u32[]{:S(2)}) collective-permute-start(f32[15,10,4,128]{3,2,1,0:T(4,128)} %get-tuple-element.19), channel_id=1, source_target_pairs={{0,8},{8,16},{16,24},{24,32},{32,40},{40,48},{48,56},{56,64},{64,7... | collective-permute-start | bytes 921608 | tf_op jit(solution)/shard_map/ppermute | solution.py:486
  60.2 14.8 %collective-permute-start.1 = (f32[15,10,4,128]{3,2,1,0:T(4,128)}, f32[15,10,4,128]{3,2,1,0:T(4,128)S(1)}, u32[]{:S(2)}, u32[]{:S(2)}) collective-permute-start(f32[15,10,4,128]{3,2,1,0:T(4,128)} %get-tuple-element.20), channel_id=1, source_target_pairs={{8,0},{16,8},{24,16},{32,24},{40,32},{48,40},{56,48},{64,56},{72,6... | collective-permute-start | bytes 921608 | tf_op jit(solution)/shard_map/ppermute | solution.py:486
  79.3 5.5 %copy-start.8 = (f32[24]{0:T(128)S(1)}, f32[24]{0:T(128)}, u32[]{:S(2)}) copy-start(f32[24]{0:T(128)} %constant.25.clone) | copy-start | bytes 292
  79.3 5.5 %copy-start.7 = (f32[24]{0:T(128)S(1)}, f32[24]{0:T(128)}, u32[]{:S(2)}) copy-start(f32[24]{0:T(128)} %constant.26.clone) | copy-start | bytes 292
  79.3 26.0 %copy-start.1 = (f32[4,1024]{1,0:T(4,128)S(1)}, f32[4,1024]{1,0:T(4,128)}, u32[]{:S(2)}) copy-start(f32[4,1024]{1,0:T(4,128)} %wind_u.1) | copy-start | bytes 49156
  79.3 26.0 %copy-start.2 = (f32[4,1024]{1,0:T(4,128)S(1)}, f32[4,1024]{1,0:T(4,128)}, u32[]{:S(2)}) copy-start(f32[4,1024]{1,0:T(4,128)} %wind_v.1) | copy-start | bytes 49156
  79.3 26.0 %all-to-all-start.2 = ((f32[8,91,4,128]{3,2,1,0:T(4,128)}), f32[8,91,4,128]{3,2,1,0:T(4,128)S(1)}, u32[]{:S(2)}, u32[]{:S(2)}) async-start(f32[8,91,4,128]{3,2,1,0:T(4,128)} %steps.3), calls=%async_computation.2 | async-start | bytes 2981888 | tf_op jit(solution)/shard_map/all_to_all | solution.py:489

commit v7 on v6

--- a/solution.py
+++ b/solution.py
@@ -106,19 +106,27 @@
     )(*args)
 
 
-def first_pack_kernel(spectrum, out, done):
+def first_pack_kernel(spectrum, out, x, arrived, done):
     begin, count, _ = CHUNKS[0]
-    copies = [
-        pltpu.make_async_copy(
-            spectrum.at[d, pl.ds(j * FULL + begin, count)], out.at[j, d], done.at[j, d]
-        )
+    ins = [
+        [
+            pltpu.make_async_copy(
+                spectrum.at[d, pl.ds(j * FULL + begin, count)], x.at[d, j], arrived.at[d, j]
+            )
+            for j in range(BLOCKS)
+        ]
         for d in range(3)
-        for j in range(BLOCKS)
     ]
-    for copy in copies:
-        copy.start()
-    for copy in copies:
-        copy.wait()
+    outs = [pltpu.make_async_copy(x.at[d], out.at[:, d], done.at[d]) for d in range(3)]
+    for copies in ins:
+        for copy in copies:
+            copy.start()
+    for copies, leave in zip(ins, outs):
+        for copy in copies:
+            copy.wait()
+        leave.start()
+    for leave in outs:
+        leave.wait()
 
 
 def last_pack_kernel(spectrum, out, x, arrived):
@@ -146,16 +154,10 @@
 
 def halo_kernel(tiles, with_maps, *refs):
     if with_maps:
-        own, maps, up, down, done = refs
+        own, maps, up, down = refs
     else:
-        own, up, down, done = refs
+        own, up, down = refs
     n = len(SOUTH)
-    copies = [
-        pltpu.make_async_copy(own.at[pl.ds(dirs[0], n)], ref.at[pl.ds(0, n)], done.at[i])
-        for i, (dirs, ref) in enumerate(((SOUTH, up), (NORTH, down)))
-    ]
-    for copy in copies:
-        copy.start()
     if with_maps:
         for k in range(2):
             for l in range(BLOCKS):
@@ -168,6 +170,10 @@
     }
 
     def body(t, carry):
+        for i, d in enumerate(SOUTH):
+            up[i, t] = own[d, t]
+        for i, d in enumerate(NORTH):
+            down[i, t] = own[d, t]
         top, low = ends["s"]
         a = [own[(top + k) % DIRS, t] for k in range(1, 4)]
         b = [own[(low - k) % DIRS, t] for k in range(1, 4)]
@@ -182,9 +188,7 @@
         down[n + 2, t] = jnp.concatenate([b[0][0:3], b[2][0:1]], axis=0)
         return carry
 
-    lax.fori_loop(0, tiles, body, 0, unroll=2)
-    for copy in copies:
-        copy.wait()
+    lax.fori_loop(0, tiles, body, 0, unroll=4)
 
 
 def step_kernel(chunk, first_call, group, coef, rfac, frsq, own, south, north, *refs):
@@ -451,7 +455,11 @@
         [hbm],
         hbm,
         (spectrum,),
-        [pltpu.SemaphoreType.DMA((BLOCKS, 3))],
+        [
+            pltpu.VMEM((3, BLOCKS, first[1]) + spectrum.shape[2:], jnp.float32),
+            pltpu.SemaphoreType.DMA((3, BLOCKS)),
+            pltpu.SemaphoreType.DMA((3,)),
+        ],
     )
     (pack_2,) = moving(
         last_pack_kernel,
@@ -464,15 +472,8 @@
     )
 
     def edges(tiles, planes, *args):
-        return moving(
-            functools.partial(halo_kernel, tiles, len(args) > 1),
-            "halo",
-            [(planes, tiles, 4, LANES)] * 2,
-            [vmem() for _ in args],
-            vmem(),
-            args,
-            [pltpu.SemaphoreType.DMA((2,))],
-        )
+        kernel = functools.partial(halo_kernel, tiles, len(args) > 1)
+        return call(kernel, "halo", [(planes, tiles, 4, LANES)] * 2, args, 0)
 
     own = lax.all_to_all(pack, "spec", 0, 0, tiled=True)
     own = tiled(own).reshape(DIRS, tiles_of(first), 4, LANES)

time: 108 us -> 85.1 us (0.79)
  Pallas kernels: 41.9 us -> 17.9 us
    pallas_call x5 -> x3, Pallas kernels: 32.1 us -> 6.13 us  [moving(): pl.pallas_call(kernel, out_shape=[jax.ShapeDtypeStruct(s, jnp.float32) fo...]
    pallas_call x2 -> x4, Pallas kernels: 9.83 us -> 11.7 us  [call(): pl.pallas_call(kernel, out_shape=jax.tree.map(lambda s: jax.ShapeDtypeStr...]
  transfers between devices with their start and end apart: 7 -> 7, of which waited for: 5 -> 4; matrix products, arithmetic and copies ran while one was open for 0% -> 0% of each run, Pallas kernels for 9% -> 10%
where the time goes in v7:
time: 85.1 us; the launch traced here: 84.2 us
  waiting for transfers between devices  34 us (40%)
  starting transfers between devices  32 us (38%)
  Pallas kernels  17.9 us (21%)
    all_to_all x1, waiting for transfers between devices, on_device(): got = lax.all_to_all(made, 'spec', 0, 0, tiled=True)  20.4 us
    pallas_call x4, Pallas kernels, call(): pl.pallas_call(kernel, out_shape=jax.tree.map(lambda s: jax.ShapeDtypeStr...  11.7 us
    all_to_all x1, waiting for transfers between devices, on_device(): own = lax.all_to_all(pack, 'spec', 0, 0, tiled=True)  9.74 us
    ppermute x1, starting transfers between devices, on_device(): lax.ppermute(high, 'space', down)  6.65 us
    ppermute x1, starting transfers between devices, on_device(): lax.ppermute(high_2, 'space', down)  6.65 us
    pallas_call x3, Pallas kernels, moving(): pl.pallas_call(kernel, out_shape=[jax.ShapeDtypeStruct(s, jnp.float32) fo...  6.13 us
    all_to_all x1, starting transfers between devices, on_device(): got = lax.all_to_all(made, 'spec', 0, 0, tiled=True)  5.88 us
    all_to_all x1, starting transfers between devices, on_device(): own = lax.all_to_all(pack, 'spec', 0, 0, tiled=True)  5.32 us
  transfers between devices with their start and end apart: 7, of which 4 were waited for; matrix products, arithmetic and copies ran while one was open for 0% of the time, Pallas kernels for 10%

profile of v7, /device:TPU:448, one launch (start us, length us, event | category | flops | bytes accessed | tf_op | source)
XLA Modules:
  0.0 84.2 jit_solution(3501456151536148396)
XLA Ops:
  0.0 2.0 %first_pack.1 = f32[8,3,2,4,1024]{4,3,2,1,0:T(4,128)} custom-call(f32[3,25,4,1024]{3,2,1,0:T(4,128)} %spectrum.3), custom_call_target="tpu_custom_call" | custom-call | tf_op jit(solution)/shard_map/first_pack/pallas_call | solution.py:424
  2.0 0.0 copy-start.5
  2.0 0.0 copy-start.6
  2.1 5.3 %all-to-all-start = ((f32[8,3,2,4,1024]{4,3,2,1,0:T(4,128)}), f32[8,3,2,4,1024]{4,3,2,1,0:T(4,128)S(1)}, u32[]{:S(2)}, u32[]{:S(2)}) async-start(f32[8,3,2,4,1024]{4,3,2,1,0:T(4,128)} %first_pack.1), calls=%async_computation | async-start | bytes 1572864 | tf_op jit(solution)/shard_map/all_to_all | solution.py:478
  7.4 2.1 %last_pack.1 = f32[8,3,10,4,128]{4,3,2,1,0:T(4,128)} custom-call(f32[3,25,4,1024]{3,2,1,0:T(4,128)} %spectrum.3), custom_call_target="tpu_custom_call" | custom-call | tf_op jit(solution)/shard_map/last_pack/pallas_call | solution.py:424
  9.5 0.0 copy-done.5
  9.5 0.0 copy-start
  9.6 0.0 copy-start.3
  9.6 0.0 copy-start.4
  9.6 0.0 copy-done.6
  9.6 9.7 %all-to-all-done = f32[8,3,2,4,1024]{4,3,2,1,0:T(4,128)S(1)} async-done(((f32[8,3,2,4,1024]{4,3,2,1,0:T(4,128)}), f32[8,3,2,4,1024]{4,3,2,1,0:T(4,128)S(1)}, u32[]{:S(2)}, u32[]{:S(2)}) %all-to-all-start) | async-done | bytes 786464 | tf_op jit(solution)/shard_map/all_to_all | solution.py:478
  19.4 1.0 %halo.2 = (f32[16,16,4,128]{3,2,1,0:T(4,128)}, f32[16,16,4,128]{3,2,1,0:T(4,128)S(1)}) custom-call(f32[24,16,4,128]{3,2,1,0:T(4,128)S(1)} %bitcast.10, f32[2,4,1024]{2,1,0:T(4,128)S(1)} %pad_maximum_fusion.refs_1_.refs_0_), custom_call_target="tpu_custom_call" | custom-call | flops 1000 | bytes 4000000 | tf_op jit(solution)/shard_map/halo/pallas_call | solution.py:96
  20.3 3.6 %all-to-all-start.1 = ((f32[8,3,10,4,128]{4,3,2,1,0:T(4,128)}), f32[8,3,10,4,128]{4,3,2,1,0:T(4,128)S(1)}, u32[]{:S(2)}, u32[]{:S(2)}) async-start(f32[8,3,10,4,128]{4,3,2,1,0:T(4,128)} %last_pack.1), calls=%async_computation.1 | async-start | bytes 983040 | tf_op jit(solution)/shard_map/all_to_all | solution.py:482
  24.0 1.9 %collective-permute-start.2 = (f32[16,16,4,128]{3,2,1,0:T(4,128)}, f32[16,16,4,128]{3,2,1,0:T(4,128)S(1)}, u32[]{:S(2)}, u32[]{:S(2)}) collective-permute-start(f32[16,16,4,128]{3,2,1,0:T(4,128)} %get-tuple-element.21), channel_id=1, source_target_pairs={{0,8},{8,16},{16,24},{24,32},{32,40},{40,48},{48,56},{56,64},{64,7... | collective-permute-start | bytes 1572872 | tf_op jit(solution)/shard_map/ppermute | solution.py:485
  25.9 6.7 %collective-permute-start.3 = (f32[16,16,4,128]{3,2,1,0:T(4,128)S(1)}, f32[16,16,4,128]{3,2,1,0:T(4,128)S(1)}, u32[]{:S(2)}, u32[]{:S(2)}) collective-permute-start(f32[16,16,4,128]{3,2,1,0:T(4,128)S(1)} %get-tuple-element.22), channel_id=1, source_target_pairs={{8,0},{16,8},{24,16},{32,24},{40,32},{48,40},{56,48},{64,56},{72,6... | collective-permute-start | bytes 1572872 | tf_op jit(solution)/shard_map/ppermute | solution.py:485
  32.6 0.8 all-to-all-done.1
  33.3 0.9 %halo.3 = (f32[15,10,4,128]{3,2,1,0:T(4,128)}, f32[15,10,4,128]{3,2,1,0:T(4,128)}) custom-call(f32[24,10,4,128]{3,2,1,0:T(4,128)S(1)} %bitcast.12), custom_call_target="tpu_custom_call" | custom-call | flops 1000 | bytes 4000000 | tf_op jit(solution)/shard_map/halo/pallas_call | solution.py:96
  34.3 1.9 %collective-permute-start = (f32[15,10,4,128]{3,2,1,0:T(4,128)}, f32[15,10,4,128]{3,2,1,0:T(4,128)S(1)}, u32[]{:S(2)}, u32[]{:S(2)}) collective-permute-start(f32[15,10,4,128]{3,2,1,0:T(4,128)} %get-tuple-element.19), channel_id=1, source_target_pairs={{0,8},{8,16},{16,24},{24,32},{32,40},{40,48},{48,56},{56,64},{64,7... | collective-permute-start | bytes 921608 | tf_op jit(solution)/shard_map/ppermute | solution.py:487
  36.2 6.7 %collective-permute-start.1 = (f32[15,10,4,128]{3,2,1,0:T(4,128)}, f32[15,10,4,128]{3,2,1,0:T(4,128)S(1)}, u32[]{:S(2)}, u32[]{:S(2)}) collective-permute-start(f32[15,10,4,128]{3,2,1,0:T(4,128)} %get-tuple-element.20), channel_id=1, source_target_pairs={{8,0},{16,8},{24,16},{32,24},{40,32},{48,40},{56,48},{64,56},{72,6... | collective-permute-start | bytes 921608 | tf_op jit(solution)/shard_map/ppermute | solution.py:487
  42.8 3.0 %collective-permute-done.2.south = f32[16,16,4,128]{3,2,1,0:T(4,128)S(1)} collective-permute-done((f32[16,16,4,128]{3,2,1,0:T(4,128)}, f32[16,16,4,128]{3,2,1,0:T(4,128)S(1)}, u32[]{:S(2)}, u32[]{:S(2)}) %collective-permute-start.2) | collective-permute-done | bytes 524320 | tf_op jit(solution)/shard_map/ppermute | solution.py:485
  45.8 0.0 collective-permute-done.3.north
  45.9 0.0 copy-done
  45.9 0.0 copy-done.3
  45.9 0.0 copy-done.4
  45.9 5.5 %steps.2 = (f32[8,91,4,128]{3,2,1,0:T(4,128)S(1)}, f32[2,2,12,8,128]{4,3,2,1,0:T(8,128)S(1)}) custom-call(s32[1]{0:T(128)} %bitcast.group, f32[25,18]{1,0:T(8,128)S(1)} %copy-done, f32[25]{0:T(128)S(1)} %copy-done.3, f32[25]{0:T(128)S(1)} %copy-done.4, f32[24,16,4,128]{3,2,1,0:T(4,128)S(1)} %bitcast.11, f32[16,16,4,128]{3,2,1,0:T(4,128)S(1)} %collective-permute-done.2.south, ...), custom_call_target="tpu_custom_call" | custom-call | flops 1000 | bytes 20000000 | tf_op jit(solution)/shard_map/steps/pallas_call | solution.py:96
  51.4 0.0 collective-permute-done.south
  51.4 0.0 collective-permute-done.1.north
  51.4 4.3 %steps.3 = f32[8,91,4,128]{3,2,1,0:T(4,128)} custom-call(s32[1]{0:T(128)} %bitcast.group, f32[25,18]{1,0:T(8,128)S(1)} %copy-done, f32[25]{0:T(128)S(1)} %copy-done.3, f32[25]{0:T(128)S(1)} %copy-done.4, f32[24,10,4,128]{3,2,1,0:T(4,128)S(1)} %bitcast.13, f32[15,10,4,128]{3,2,1,0:T(4,128)S(1)} %collective-permute-done.south, ...), custom_call_target="tpu_custom_call" | custom-call | flops 1000 | bytes 20000000 | tf_op jit(solution)/shard_map/steps/pallas_call | solution.py:96
  55.7 0.0 copy-start.8
  55.7 0.0 copy-start.7
  55.7 0.0 copy-start.1
  55.7 0.0 copy-start.2
  55.7 5.9 %all-to-all-start.2 = ((f32[8,91,4,128]{3,2,1,0:T(4,128)}), f32[8,91,4,128]{3,2,1,0:T(4,128)S(1)}, u32[]{:S(2)}, u32[]{:S(2)}) async-start(f32[8,91,4,128]{3,2,1,0:T(4,128)} %steps.3), calls=%async_computation.2 | async-start | bytes 2981888 | tf_op jit(solution)/shard_map/all_to_all | solution.py:490
  61.6 0.0 copy-done.8
  61.6 0.1 dynamic_slice.6.cos
  61.7 0.0 copy-done.7
  61.7 0.1 dynamic_slice.7.sin
  61.8 20.4 %all-to-all-done.2.got = f32[8,91,4,128]{3,2,1,0:T(4,128)S(1)} async-done(((f32[8,91,4,128]{3,2,1,0:T(4,128)}), f32[8,91,4,128]{3,2,1,0:T(4,128)S(1)}, u32[]{:S(2)}, u32[]{:S(2)}) %all-to-all-start.2) | async-done | bytes 1490976 | tf_op jit(solution)/shard_map/all_to_all | solution.py:490
  82.2 0.0 copy-done.1
  82.2 0.0 copy-done.2
  82.2 2.0 %source.1 = f32[3,25,4,1024]{3,2,1,0:T(4,128)} custom-call(f32[3]{0:T(128)S(1)} %dynamic_slice.6.cos, f32[3]{0:T(128)S(1)} %dynamic_slice.7.sin, f32[8,91,4,128]{3,2,1,0:T(4,128)S(1)} %all-to-all-done.2.got, f32[4,1024]{1,0:T(4,128)S(1)} %copy-done.1, f32[4,1024]{1,0:T(4,128)S(1)} %copy-done.2), custom_call_target="tpu_custom_call" | custom-call | tf_op jit(solution)/shard_map/source/pallas_call | solution.py:424
  (2 shorter events, 0.0 us)
Async XLA Ops:
  2.0 7.5 %copy-start.5 = (s32[4,1024]{1,0:T(4,128)S(1)}, s32[4,1024]{1,0:T(4,128)}, u32[]{:S(2)}) copy-start(s32[4,1024]{1,0:T(4,128)} %param.12) | copy-start | bytes 49156
  2.0 7.6 %copy-start.6 = (f32[4,1024]{1,0:T(4,128)S(1)}, f32[4,1024]{1,0:T(4,128)}, u32[]{:S(2)}) copy-start(f32[4,1024]{1,0:T(4,128)} %param.13) | copy-start | bytes 49156
  2.1 17.3 %all-to-all-start = ((f32[8,3,2,4,1024]{4,3,2,1,0:T(4,128)}), f32[8,3,2,4,1024]{4,3,2,1,0:T(4,128)S(1)}, u32[]{:S(2)}, u32[]{:S(2)}) async-start(f32[8,3,2,4,1024]{4,3,2,1,0:T(4,128)} %first_pack.1), calls=%async_computation | async-start | bytes 1572864 | tf_op jit(solution)/shard_map/all_to_all | solution.py:478
  9.5 36.3 %copy-start = (f32[25,18]{1,0:T(8,128)S(1)}, f32[25,18]{1,0:T(8,128)}, u32[]{:S(2)}) copy-start(f32[25,18]{1,0:T(8,128)} %constant.22.clone.coef) | copy-start | bytes 5404
  9.6 36.3 %copy-start.3 = (f32[25]{0:T(128)S(1)}, f32[25]{0:T(128)}, u32[]{:S(2)}) copy-start(f32[25]{0:T(128)} %constant.23.clone.rfac) | copy-start | bytes 304
  9.6 36.3 %copy-start.4 = (f32[25]{0:T(128)S(1)}, f32[25]{0:T(128)}, u32[]{:S(2)}) copy-start(f32[25]{0:T(128)} %constant.24.clone.frsq) | copy-start | bytes 304
  20.3 13.0 %all-to-all-start.1 = ((f32[8,3,10,4,128]{4,3,2,1,0:T(4,128)}), f32[8,3,10,4,128]{4,3,2,1,0:T(4,128)S(1)}, u32[]{:S(2)}, u32[]{:S(2)}) async-start(f32[8,3,10,4,128]{4,3,2,1,0:T(4,128)} %last_pack.1), calls=%async_computation.1 | async-start | bytes 983040 | tf_op jit(solution)/shard_map/all_to_all | solution.py:482
  24.0 21.9 %collective-permute-start.2 = (f32[16,16,4,128]{3,2,1,0:T(4,128)}, f32[16,16,4,128]{3,2,1,0:T(4,128)S(1)}, u32[]{:S(2)}, u32[]{:S(2)}) collective-permute-start(f32[16,16,4,128]{3,2,1,0:T(4,128)} %get-tuple-element.21), channel_id=1, source_target_pairs={{0,8},{8,16},{16,24},{24,32},{32,40},{40,48},{48,56},{56,64},{64,7... | collective-permute-start | bytes 1572872 | tf_op jit(solution)/shard_map/ppermute | solution.py:485
  25.9 20.0 %collective-permute-start.3 = (f32[16,16,4,128]{3,2,1,0:T(4,128)S(1)}, f32[16,16,4,128]{3,2,1,0:T(4,128)S(1)}, u32[]{:S(2)}, u32[]{:S(2)}) collective-permute-start(f32[16,16,4,128]{3,2,1,0:T(4,128)S(1)} %get-tuple-element.22), channel_id=1, source_target_pairs={{8,0},{16,8},{24,16},{32,24},{40,32},{48,40},{56,48},{64,56},{72,6... | collective-permute-start | bytes 1572872 | tf_op jit(solution)/shard_map/ppermute | solution.py:485
  34.3 17.2 %collective-permute-start = (f32[15,10,4,128]{3,2,1,0:T(4,128)}, f32[15,10,4,128]{3,2,1,0:T(4,128)S(1)}, u32[]{:S(2)}, u32[]{:S(2)}) collective-permute-start(f32[15,10,4,128]{3,2,1,0:T(4,128)} %get-tuple-element.19), channel_id=1, source_target_pairs={{0,8},{8,16},{16,24},{24,32},{32,40},{40,48},{48,56},{56,64},{64,7... | collective-permute-start | bytes 921608 | tf_op jit(solution)/shard_map/ppermute | solution.py:487
  36.2 15.2 %collective-permute-start.1 = (f32[15,10,4,128]{3,2,1,0:T(4,128)}, f32[15,10,4,128]{3,2,1,0:T(4,128)S(1)}, u32[]{:S(2)}, u32[]{:S(2)}) collective-permute-start(f32[15,10,4,128]{3,2,1,0:T(4,128)} %get-tuple-element.20), channel_id=1, source_target_pairs={{8,0},{16,8},{24,16},{32,24},{40,32},{48,40},{56,48},{64,56},{72,6... | collective-permute-start | bytes 921608 | tf_op jit(solution)/shard_map/ppermute | solution.py:487
  55.7 5.9 %copy-start.8 = (f32[24]{0:T(128)S(1)}, f32[24]{0:T(128)}, u32[]{:S(2)}) copy-start(f32[24]{0:T(128)} %constant.25.clone) | copy-start | bytes 292
  55.7 6.0 %copy-start.7 = (f32[24]{0:T(128)S(1)}, f32[24]{0:T(128)}, u32[]{:S(2)}) copy-start(f32[24]{0:T(128)} %constant.26.clone) | copy-start | bytes 292
  55.7 26.5 %copy-start.1 = (f32[4,1024]{1,0:T(4,128)S(1)}, f32[4,1024]{1,0:T(4,128)}, u32[]{:S(2)}) copy-start(f32[4,1024]{1,0:T(4,128)} %wind_u.1) | copy-start | bytes 49156
  55.7 26.5 %copy-start.2 = (f32[4,1024]{1,0:T(4,128)S(1)}, f32[4,1024]{1,0:T(4,128)}, u32[]{:S(2)}) copy-start(f32[4,1024]{1,0:T(4,128)} %wind_v.1) | copy-start | bytes 49156
  55.7 26.5 %all-to-all-start.2 = ((f32[8,91,4,128]{3,2,1,0:T(4,128)}), f32[8,91,4,128]{3,2,1,0:T(4,128)S(1)}, u32[]{:S(2)}, u32[]{:S(2)}) async-start(f32[8,91,4,128]{3,2,1,0:T(4,128)} %steps.3), calls=%async_computation.2 | async-start | bytes 2981888 | tf_op jit(solution)/shard_map/all_to_all | solution.py:490

commit v8 on v7

--- a/solution.py
+++ b/solution.py
@@ -53,6 +53,7 @@
 WHOLE = FULL * BLOCKS
 WINDOW = 2
 HALF = LANES // 2
+FIRST_MADE = 3 * CHUNKS[0][1] * BLOCKS
 SUMS_AT = 3 * (WHOLE + 1)
 MADE = SUMS_AT + 2 * BLOCKS
 
@@ -193,11 +194,16 @@
 
 def step_kernel(chunk, first_call, group, coef, rfac, frsq, own, south, north, *refs):
     begin, count, tail = chunk
-    tiles, slots, origin = tiles_of(chunk), slots_of(chunk), begin * BLOCKS
+    tiles, slots = tiles_of(chunk), slots_of(chunk)
     if first_call:
-        maps, out, around, st_a, st_b, ex_a, ex_b = refs
+        maps, out, around, sums, st_a, st_b, ex_a, ex_b = refs
+        base = 0
     else:
-        around, given, out, st_a, st_b, ex_a, ex_b = refs
+        around, given, given_sums, result, st_a, st_b, ex_a, ex_b, out, sums, done = refs
+        base = FIRST_MADE
+        early = pltpu.make_async_copy(given, result.at[:, pl.ds(0, base)], done.at[0])
+        late = pltpu.make_async_copy(out, result.at[:, pl.ds(base, MADE - base)], done.at[1])
+        early.start()
     me = group[0]
     whole = count * BLOCKS
 
@@ -272,25 +278,17 @@
 
     lax.fori_loop(0, tiles, fill, 0)
 
-    if first_call:
-        for i in range(2 * BLOCKS):
-            out[0, SUMS_AT + i] = jnp.zeros((4, LANES), jnp.float32)
-    else:
-        for i in range(2 * BLOCKS):
-            out[0, SUMS_AT + i] = given[0, SUMS_AT + i]
-        for s in range(BLOCKS):
-            for d in range(3):
-                for i in range(origin):
-                    out[s, d * WHOLE + i] = given[s, d * WHOLE + i]
+    for i in range(2 * BLOCKS):
+        sums[i] = jnp.zeros((4, LANES), jnp.float32) if first_call else given_sums[i]
 
     def keep(t, d, new):
-        out[d // 3, (d % 3) * WHOLE + origin + t] = new[0:4]
+        out[d // 3, (d % 3) * whole + t] = new[0:4]
 
     def add_up(t, f, total):
-        place = SUMS_AT + (me if isinstance(t, int) else t % BLOCKS)
+        place = me if isinstance(t, int) else t % BLOCKS
         total = total[0:4]
-        out[0, place] += total
-        out[0, place + BLOCKS] += total * frsq[f]
+        sums[place] += total
+        sums[BLOCKS + place] += total * frsq[f]
 
     def make(step, src, src_ex, dst, dst_ex):
         def body(t, carry):
@@ -362,36 +360,56 @@
         for d in range(DIRS):
             left, right = dst[d, slot_of(whole)], dst[d, slot_of(whole + 1)]
             new = pltpu.roll(jnp.where(half, right, left), HALF, 1)
-            out[d // 3, 3 * WHOLE + d % 3] = new[0:4]
+            out[d // 3, 3 * whole + d % 3] = new[0:4]
             total = new if total is None else total + new
         add_up(whole, FREQS - 1, total)
     if not first_call:
         for i in range(2 * BLOCKS):
-            value = out[0, SUMS_AT + i]
-            for s in range(1, BLOCKS):
-                out[s, SUMS_AT + i] = value
+            value = sums[i]
+            for s in range(BLOCKS):
+                out[s, SUMS_AT - base + i] = value
+        late.start()
+        early.wait()
+        late.wait()
 
 
 def step_call(chunk, first_call, group, own, south, north, rest):
     slots = slots_of(chunk)
     state = pltpu.VMEM((DIRS, slots, 8, LANES), jnp.float32)
     extra = pltpu.VMEM((len(EXTRAS), slots, 8, LANES), jnp.float32)
-    out = [(BLOCKS, MADE, 4, LANES)]
+    args = (group, COEF, RFAC, FR * FR, own, south, north, *rest)
+    scratch = [state, state, extra, extra]
     if first_call:
-        out.append((2, 2, BLOCKS + 2 + WINDOW, 8, LANES))
-    args = (group, COEF, RFAC, FR * FR, own, south, north, *rest)
-    return call(
+        out = [
+            (BLOCKS, FIRST_MADE, 4, LANES),
+            (2, 2, BLOCKS + 2 + WINDOW, 8, LANES),
+            (2 * BLOCKS, 4, LANES),
+        ]
+        space = vmem()
+    else:
+        out = [(BLOCKS, MADE, 4, LANES)]
+        space = pl.BlockSpec(memory_space=pltpu.HBM)
+        scratch += [
+            pltpu.VMEM((BLOCKS, MADE - FIRST_MADE, 4, LANES), jnp.float32),
+            pltpu.VMEM((2 * BLOCKS, 4, LANES), jnp.float32),
+            pltpu.SemaphoreType.DMA((2,)),
+        ]
+    return moving(
         functools.partial(step_kernel, chunk, first_call),
         "steps",
         out,
+        [smem()] * 4 + [vmem()] * (len(args) - 4),
+        space,
         args,
-        4,
-        [state, state, extra, extra],
+        scratch,
         20_000_000,
     )
 
 
-def source_kernel(cos, sin, got, wind_u, wind_v, out, made, shrink, done):
+SPAN = 5
+
+
+def source_kernel(cos, sin, got, wind_u, wind_v, out, made, shrink, gains, done):
     inverse = 1.0 / (DIRS * FREQS)
     columns = [slice(t * LANES, (t + 1) * LANES) for t in range(BLOCKS)]
     for t, cols in enumerate(columns):
@@ -400,34 +418,47 @@
         for j in range(1, BLOCKS):
             m0 = m0 + got[j, SUMS_AT + t]
             m2 = m2 + got[j, SUMS_AT + BLOCKS + t]
-        ratio = 0.5 * (m2 * inverse) / (1.0 + m0 * inverse)
-        for f in range(FREQS):
-            shrink[f, :, cols] = 1.0 / (1.0 + ratio * float(FR[f] * FR[f]))
+        shrink[t] = 0.5 * (m2 * inverse) / (1.0 + m0 * inverse)
+        for d in range(3):
+            along = wind_u[:, cols] * cos[d] + wind_v[:, cols] * sin[d]
+            gains[d, t] = 0.5 * jnp.maximum(along, 0.0)
     copies = []
-    for d in range(3):
+    for part in range(FREQS // SPAN):
+        span = range(part * SPAN, (part + 1) * SPAN)
         for t, cols in enumerate(columns):
-            along = wind_u[:, cols] * cos[d] + wind_v[:, cols] * sin[d]
-            gain = 0.5 * jnp.maximum(along, 0.0)
-            for f in range(FREQS):
-                if f < BLOCKS * FULL:
-                    a = got[f // FULL, d * WHOLE + f % FULL * BLOCKS + t]
-                else:
-                    a = got[t, 3 * WHOLE + d]
-                made[d, f, :, cols] = a * (1.0 + gain * float(FR[f])) * shrink[f, :, cols]
-        copies.append(pltpu.make_async_copy(made.at[d], out.at[d], done.at[d]))
-        copies[-1].start()
+            ratio = shrink[t]
+            gain = [gains[d, t] for d in range(3)]
+            for f in span:
+                less = 1.0 / (1.0 + ratio * float(FR[f] * FR[f]))
+                j, i = f // FULL, f % FULL
+                for d in range(3):
+                    if f == FREQS - 1:
+                        a = got[t, 3 * WHOLE + d]
+                    elif i < CHUNKS[0][1]:
+                        a = got[j, (d * CHUNKS[0][1] + i) * BLOCKS + t]
+                    else:
+                        a = got[j, FIRST_MADE + d * BLOCKS + t]
+                    made[d, f, :, cols] = a * (1.0 + gain[d] * float(FR[f])) * less
+        for d in range(3):
+            rows = pl.ds(part * SPAN, SPAN)
+            copies.append(
+                pltpu.make_async_copy(made.at[d, rows], out.at[d, rows], done.at[part, d])
+            )
+            copies[-1].start()
     for copy in copies:
         copy.wait()
 
 
-def moving(kernel, name, out, ins, out_space, args, scratch):
+def moving(kernel, name, out, ins, out_space, args, scratch, cost=4_000_000):
+    limit = 60 * 1024 * 1024 if "pack" in name else VMEM_LIMIT
     return pl.pallas_call(
         kernel,
         out_shape=[jax.ShapeDtypeStruct(s, jnp.float32) for s in out],
         in_specs=ins,
         out_specs=[out_space for _ in out],
         scratch_shapes=scratch,
-        compiler_params=pltpu.CompilerParams(vmem_limit_bytes=60 * 1024 * 1024 if "pack" in name else VMEM_LIMIT),
+        compiler_params=pltpu.CompilerParams(vmem_limit_bytes=limit),
+        cost_estimate=pl.CostEstimate(flops=1000, bytes_accessed=cost, transcendentals=0),
         interpret=INTERPRET,
         name=name,
     )(*args)
@@ -485,8 +516,8 @@
     south, north = lax.ppermute(low, "space", up), lax.ppermute(high, "space", down)
     south, north, _, _ = lax.optimization_barrier((south, north, low_2, high_2))
     south_2, north_2 = lax.ppermute(low_2, "space", up), lax.ppermute(high_2, "space", down)
-    made, around = step_call(CHUNKS[0], True, group, own, south, north, (maps,))
-    (made,) = step_call(CHUNKS[1], False, group, own_2, south_2, north_2, (around, made))
+    made, around, sums = step_call(CHUNKS[0], True, group, own, south, north, (maps,))
+    (made,) = step_call(CHUNKS[1], False, group, own_2, south_2, north_2, (around, made, sums))
     got = lax.all_to_all(made, "spec", 0, 0, tiled=True)
     cos = lax.dynamic_slice_in_dim(jnp.asarray(COS), me * 3, 3)
     sin = lax.dynamic_slice_in_dim(jnp.asarray(SIN), me * 3, 3)
@@ -497,7 +528,12 @@
         [smem(), smem(), vmem(), vmem(), vmem()],
         hbm,
         (cos, sin, got, wind_u, wind_v),
-        [room, pltpu.VMEM(spectrum.shape[1:], jnp.float32), pltpu.SemaphoreType.DMA((3,))],
+        [
+            room,
+            pltpu.VMEM((BLOCKS, 4, LANES), jnp.float32),
+            pltpu.VMEM((3, BLOCKS, 4, LANES), jnp.float32),
+            pltpu.SemaphoreType.DMA((FREQS // SPAN, 3)),
+        ],
     )
     return result
 

time: 85.1 us -> 84.8 us (level)
    pallas_call x4 -> x2, Pallas kernels: 11.7 us -> 1.9 us  [call(): pl.pallas_call(kernel, out_shape=jax.tree.map(lambda s: jax.ShapeDtypeStr...]
    pallas_call x3 -> x5, Pallas kernels: 6.13 us -> 15.6 us  [moving(): pl.pallas_call(kernel, out_shape=[jax.ShapeDtypeStruct(s, jnp.float32) fo...]
where the time goes in v8:
time: 84.8 us; the launch traced here: 83.9 us
  waiting for transfers between devices  34 us (40%)
  starting transfers between devices  32 us (38%)
  Pallas kernels  17.5 us (21%)
    all_to_all x1, waiting for transfers between devices, on_device(): got = lax.all_to_all(made, 'spec', 0, 0, tiled=True)  20.4 us
    pallas_call x5, Pallas kernels, moving(): pl.pallas_call(kernel, out_shape=[jax.ShapeDtypeStruct(s, jnp.float32) fo...  15.6 us
    all_to_all x1, waiting for transfers between devices, on_device(): own = lax.all_to_all(pack, 'spec', 0, 0, tiled=True)  9.74 us
    ppermute x1, starting transfers between devices, on_device(): lax.ppermute(high, 'space', down)  6.65 us
    ppermute x1, starting transfers between devices, on_device(): lax.ppermute(high_2, 'space', down)  6.65 us
    all_to_all x1, starting transfers between devices, on_device(): got = lax.all_to_all(made, 'spec', 0, 0, tiled=True)  5.89 us
    all_to_all x1, starting transfers between devices, on_device(): own = lax.all_to_all(pack, 'spec', 0, 0, tiled=True)  5.32 us
    all_to_all x1, starting transfers between devices, on_device(): own_2 = lax.all_to_all(pack_2, 'spec', 0, 0, tiled=True)  3.63 us
  transfers between devices with their start and end apart: 7, of which 4 were waited for; matrix products, arithmetic and copies ran while one was open for 0% of the time, Pallas kernels for 10%

profile of v8, /device:TPU:448, one launch (start us, length us, event | category | flops | bytes accessed | tf_op | source)
XLA Modules:
  0.0 83.9 jit_solution(12285838219148996873)
XLA Ops:
  0.0 2.0 %first_pack.1 = f32[8,3,2,4,1024]{4,3,2,1,0:T(4,128)} custom-call(f32[3,25,4,1024]{3,2,1,0:T(4,128)} %spectrum.3), custom_call_target="tpu_custom_call" | custom-call | flops 1000 | bytes 4000000 | tf_op jit(solution)/shard_map/first_pack/pallas_call | solution.py:454
  2.0 0.0 copy-start.5
  2.0 0.0 copy-start.6
  2.1 5.3 %all-to-all-start = ((f32[8,3,2,4,1024]{4,3,2,1,0:T(4,128)}), f32[8,3,2,4,1024]{4,3,2,1,0:T(4,128)S(1)}, u32[]{:S(2)}, u32[]{:S(2)}) async-start(f32[8,3,2,4,1024]{4,3,2,1,0:T(4,128)} %first_pack.1), calls=%async_computation | async-start | bytes 1572864 | tf_op jit(solution)/shard_map/all_to_all | solution.py:509
  7.4 2.1 %last_pack.1 = f32[8,3,10,4,128]{4,3,2,1,0:T(4,128)} custom-call(f32[3,25,4,1024]{3,2,1,0:T(4,128)} %spectrum.3), custom_call_target="tpu_custom_call" | custom-call | flops 1000 | bytes 4000000 | tf_op jit(solution)/shard_map/last_pack/pallas_call | solution.py:454
  9.5 0.0 copy-done.5
  9.5 0.0 copy-start
  9.6 0.0 copy-start.3
  9.6 0.0 copy-start.4
  9.6 0.0 copy-done.6
  9.6 9.7 %all-to-all-done = f32[8,3,2,4,1024]{4,3,2,1,0:T(4,128)S(1)} async-done(((f32[8,3,2,4,1024]{4,3,2,1,0:T(4,128)}), f32[8,3,2,4,1024]{4,3,2,1,0:T(4,128)S(1)}, u32[]{:S(2)}, u32[]{:S(2)}) %all-to-all-start) | async-done | bytes 786464 | tf_op jit(solution)/shard_map/all_to_all | solution.py:509
  19.4 1.0 %halo.2 = (f32[16,16,4,128]{3,2,1,0:T(4,128)}, f32[16,16,4,128]{3,2,1,0:T(4,128)S(1)}) custom-call(f32[24,16,4,128]{3,2,1,0:T(4,128)S(1)} %bitcast.10, f32[2,4,1024]{2,1,0:T(4,128)S(1)} %pad_maximum_fusion.refs_1_.refs_0_), custom_call_target="tpu_custom_call" | custom-call | flops 1000 | bytes 4000000 | tf_op jit(solution)/shard_map/halo/pallas_call | solution.py:97
  20.3 3.6 %all-to-all-start.1 = ((f32[8,3,10,4,128]{4,3,2,1,0:T(4,128)}), f32[8,3,10,4,128]{4,3,2,1,0:T(4,128)S(1)}, u32[]{:S(2)}, u32[]{:S(2)}) async-start(f32[8,3,10,4,128]{4,3,2,1,0:T(4,128)} %last_pack.1), calls=%async_computation.1 | async-start | bytes 983040 | tf_op jit(solution)/shard_map/all_to_all | solution.py:513
  24.0 1.9 %collective-permute-start.2 = (f32[16,16,4,128]{3,2,1,0:T(4,128)}, f32[16,16,4,128]{3,2,1,0:T(4,128)S(1)}, u32[]{:S(2)}, u32[]{:S(2)}) collective-permute-start(f32[16,16,4,128]{3,2,1,0:T(4,128)} %get-tuple-element.22), channel_id=1, source_target_pairs={{0,8},{8,16},{16,24},{24,32},{32,40},{40,48},{48,56},{56,64},{64,7... | collective-permute-start | bytes 1572872 | tf_op jit(solution)/shard_map/ppermute | solution.py:516
  25.9 6.7 %collective-permute-start.3 = (f32[16,16,4,128]{3,2,1,0:T(4,128)S(1)}, f32[16,16,4,128]{3,2,1,0:T(4,128)S(1)}, u32[]{:S(2)}, u32[]{:S(2)}) collective-permute-start(f32[16,16,4,128]{3,2,1,0:T(4,128)S(1)} %get-tuple-element.23), channel_id=1, source_target_pairs={{8,0},{16,8},{24,16},{32,24},{40,32},{48,40},{56,48},{64,56},{72,6... | collective-permute-start | bytes 1572872 | tf_op jit(solution)/shard_map/ppermute | solution.py:516
  32.6 0.8 all-to-all-done.1
  33.3 0.9 %halo.3 = (f32[15,10,4,128]{3,2,1,0:T(4,128)}, f32[15,10,4,128]{3,2,1,0:T(4,128)}) custom-call(f32[24,10,4,128]{3,2,1,0:T(4,128)S(1)} %bitcast.12), custom_call_target="tpu_custom_call" | custom-call | flops 1000 | bytes 4000000 | tf_op jit(solution)/shard_map/halo/pallas_call | solution.py:97
  34.3 1.9 %collective-permute-start = (f32[15,10,4,128]{3,2,1,0:T(4,128)}, f32[15,10,4,128]{3,2,1,0:T(4,128)S(1)}, u32[]{:S(2)}, u32[]{:S(2)}) collective-permute-start(f32[15,10,4,128]{3,2,1,0:T(4,128)} %get-tuple-element.20), channel_id=1, source_target_pairs={{0,8},{8,16},{16,24},{24,32},{32,40},{40,48},{48,56},{56,64},{64,7... | collective-permute-start | bytes 921608 | tf_op jit(solution)/shard_map/ppermute | solution.py:518
  36.2 6.7 %collective-permute-start.1 = (f32[15,10,4,128]{3,2,1,0:T(4,128)}, f32[15,10,4,128]{3,2,1,0:T(4,128)S(1)}, u32[]{:S(2)}, u32[]{:S(2)}) collective-permute-start(f32[15,10,4,128]{3,2,1,0:T(4,128)} %get-tuple-element.21), channel_id=1, source_target_pairs={{8,0},{16,8},{24,16},{32,24},{40,32},{48,40},{56,48},{64,56},{72,6... | collective-permute-start | bytes 921608 | tf_op jit(solution)/shard_map/ppermute | solution.py:518
  42.8 3.0 %collective-permute-done.2.south = f32[16,16,4,128]{3,2,1,0:T(4,128)S(1)} collective-permute-done((f32[16,16,4,128]{3,2,1,0:T(4,128)}, f32[16,16,4,128]{3,2,1,0:T(4,128)S(1)}, u32[]{:S(2)}, u32[]{:S(2)}) %collective-permute-start.2) | collective-permute-done | bytes 524320 | tf_op jit(solution)/shard_map/ppermute | solution.py:516
  45.8 0.0 collective-permute-done.3.north
  45.9 0.0 copy-done
  45.9 0.0 copy-done.3
  45.9 0.0 copy-done.4
  45.9 5.5 %steps.2 = (f32[8,48,4,128]{3,2,1,0:T(4,128)S(1)}, f32[2,2,12,8,128]{4,3,2,1,0:T(8,128)S(1)}, f32[16,4,128]{2,1,0:T(4,128)S(1)}) custom-call(s32[1]{0:T(128)} %bitcast.group, f32[25,18]{1,0:T(8,128)S(1)} %copy-done, f32[25]{0:T(128)S(1)} %copy-done.3, f32[25]{0:T(128)S(1)} %copy-done.4, f32[24,16,4,128]{3,2,1,0:T(4,128)S(1)} %bitcast.11, ...), custom_call_target="tpu_custom_call" | custom-call | flops 1000 | bytes 20000000 | tf_op jit(solution)/shard_map/steps/pallas_call | solution.py:454
  51.4 0.0 collective-permute-done.south
  51.4 0.0 collective-permute-done.1.north
  51.4 4.1 %steps.3 = f32[8,91,4,128]{3,2,1,0:T(4,128)} custom-call(s32[1]{0:T(128)} %bitcast.group, f32[25,18]{1,0:T(8,128)S(1)} %copy-done, f32[25]{0:T(128)S(1)} %copy-done.3, f32[25]{0:T(128)S(1)} %copy-done.4, f32[24,10,4,128]{3,2,1,0:T(4,128)S(1)} %bitcast.13, f32[15,10,4,128]{3,2,1,0:T(4,128)S(1)} %collective-permute-done.south, ...), custom_call_target="tpu_custom_call" | custom-call | flops 1000 | bytes 20000000 | tf_op jit(solution)/shard_map/steps/pallas_call | solution.py:454
  55.5 0.0 copy-start.8
  55.5 0.0 copy-start.7
  55.5 0.0 copy-start.1
  55.5 0.0 copy-start.2
  55.5 5.9 %all-to-all-start.2 = ((f32[8,91,4,128]{3,2,1,0:T(4,128)}), f32[8,91,4,128]{3,2,1,0:T(4,128)S(1)}, u32[]{:S(2)}, u32[]{:S(2)}) async-start(f32[8,91,4,128]{3,2,1,0:T(4,128)} %steps.3), calls=%async_computation.2 | async-start | bytes 2981888 | tf_op jit(solution)/shard_map/all_to_all | solution.py:521
  61.4 0.0 copy-done.8
  61.4 0.1 dynamic_slice.6.cos
  61.5 0.0 copy-done.7
  61.5 0.1 dynamic_slice.7.sin
  61.6 20.4 %all-to-all-done.2.got = f32[8,91,4,128]{3,2,1,0:T(4,128)S(1)} async-done(((f32[8,91,4,128]{3,2,1,0:T(4,128)}), f32[8,91,4,128]{3,2,1,0:T(4,128)S(1)}, u32[]{:S(2)}, u32[]{:S(2)}) %all-to-all-start.2) | async-done | bytes 1490976 | tf_op jit(solution)/shard_map/all_to_all | solution.py:521
  82.0 0.0 copy-done.1
  82.0 0.0 copy-done.2
  82.0 1.9 %source.1 = f32[3,25,4,1024]{3,2,1,0:T(4,128)} custom-call(f32[3]{0:T(128)S(1)} %dynamic_slice.6.cos, f32[3]{0:T(128)S(1)} %dynamic_slice.7.sin, f32[8,91,4,128]{3,2,1,0:T(4,128)S(1)} %all-to-all-done.2.got, f32[4,1024]{1,0:T(4,128)S(1)} %copy-done.1, f32[4,1024]{1,0:T(4,128)S(1)} %copy-done.2), custom_call_target="tpu_custom_call" | custom-call | flops 1000 | bytes 4000000 | tf_op jit(solution)/shard_map/source/pallas_call | solution.py:454
  (2 shorter events, 0.0 us)
Async XLA Ops:
  2.0 7.5 %copy-start.5 = (s32[4,1024]{1,0:T(4,128)S(1)}, s32[4,1024]{1,0:T(4,128)}, u32[]{:S(2)}) copy-start(s32[4,1024]{1,0:T(4,128)} %param.12) | copy-start | bytes 49156
  2.0 7.6 %copy-start.6 = (f32[4,1024]{1,0:T(4,128)S(1)}, f32[4,1024]{1,0:T(4,128)}, u32[]{:S(2)}) copy-start(f32[4,1024]{1,0:T(4,128)} %param.13) | copy-start | bytes 49156
  2.1 17.3 %all-to-all-start = ((f32[8,3,2,4,1024]{4,3,2,1,0:T(4,128)}), f32[8,3,2,4,1024]{4,3,2,1,0:T(4,128)S(1)}, u32[]{:S(2)}, u32[]{:S(2)}) async-start(f32[8,3,2,4,1024]{4,3,2,1,0:T(4,128)} %first_pack.1), calls=%async_computation | async-start | bytes 1572864 | tf_op jit(solution)/shard_map/all_to_all | solution.py:509
  9.5 36.3 %copy-start = (f32[25,18]{1,0:T(8,128)S(1)}, f32[25,18]{1,0:T(8,128)}, u32[]{:S(2)}) copy-start(f32[25,18]{1,0:T(8,128)} %constant.22.clone.coef) | copy-start | bytes 5404
  9.6 36.3 %copy-start.3 = (f32[25]{0:T(128)S(1)}, f32[25]{0:T(128)}, u32[]{:S(2)}) copy-start(f32[25]{0:T(128)} %constant.23.clone.rfac) | copy-start | bytes 304
  9.6 36.3 %copy-start.4 = (f32[25]{0:T(128)S(1)}, f32[25]{0:T(128)}, u32[]{:S(2)}) copy-start(f32[25]{0:T(128)} %constant.24.clone.frsq) | copy-start | bytes 304
  20.3 13.0 %all-to-all-start.1 = ((f32[8,3,10,4,128]{4,3,2,1,0:T(4,128)}), f32[8,3,10,4,128]{4,3,2,1,0:T(4,128)S(1)}, u32[]{:S(2)}, u32[]{:S(2)}) async-start(f32[8,3,10,4,128]{4,3,2,1,0:T(4,128)} %last_pack.1), calls=%async_computation.1 | async-start | bytes 983040 | tf_op jit(solution)/shard_map/all_to_all | solution.py:513
  24.0 21.9 %collective-permute-start.2 = (f32[16,16,4,128]{3,2,1,0:T(4,128)}, f32[16,16,4,128]{3,2,1,0:T(4,128)S(1)}, u32[]{:S(2)}, u32[]{:S(2)}) collective-permute-start(f32[16,16,4,128]{3,2,1,0:T(4,128)} %get-tuple-element.22), channel_id=1, source_target_pairs={{0,8},{8,16},{16,24},{24,32},{32,40},{40,48},{48,56},{56,64},{64,7... | collective-permute-start | bytes 1572872 | tf_op jit(solution)/shard_map/ppermute | solution.py:516
  25.9 20.0 %collective-permute-start.3 = (f32[16,16,4,128]{3,2,1,0:T(4,128)S(1)}, f32[16,16,4,128]{3,2,1,0:T(4,128)S(1)}, u32[]{:S(2)}, u32[]{:S(2)}) collective-permute-start(f32[16,16,4,128]{3,2,1,0:T(4,128)S(1)} %get-tuple-element.23), channel_id=1, source_target_pairs={{8,0},{16,8},{24,16},{32,24},{40,32},{48,40},{56,48},{64,56},{72,6... | collective-permute-start | bytes 1572872 | tf_op jit(solution)/shard_map/ppermute | solution.py:516
  34.3 17.1 %collective-permute-start = (f32[15,10,4,128]{3,2,1,0:T(4,128)}, f32[15,10,4,128]{3,2,1,0:T(4,128)S(1)}, u32[]{:S(2)}, u32[]{:S(2)}) collective-permute-start(f32[15,10,4,128]{3,2,1,0:T(4,128)} %get-tuple-element.20), channel_id=1, source_target_pairs={{0,8},{8,16},{16,24},{24,32},{32,40},{40,48},{48,56},{56,64},{64,7... | collective-permute-start | bytes 921608 | tf_op jit(solution)/shard_map/ppermute | solution.py:518
  36.2 15.2 %collective-permute-start.1 = (f32[15,10,4,128]{3,2,1,0:T(4,128)}, f32[15,10,4,128]{3,2,1,0:T(4,128)S(1)}, u32[]{:S(2)}, u32[]{:S(2)}) collective-permute-start(f32[15,10,4,128]{3,2,1,0:T(4,128)} %get-tuple-element.21), channel_id=1, source_target_pairs={{8,0},{16,8},{24,16},{32,24},{40,32},{48,40},{56,48},{64,56},{72,6... | collective-permute-start | bytes 921608 | tf_op jit(solution)/shard_map/ppermute | solution.py:518
  55.5 5.9 %copy-start.8 = (f32[24]{0:T(128)S(1)}, f32[24]{0:T(128)}, u32[]{:S(2)}) copy-start(f32[24]{0:T(128)} %constant.25.clone) | copy-start | bytes 292
  55.5 6.0 %copy-start.7 = (f32[24]{0:T(128)S(1)}, f32[24]{0:T(128)}, u32[]{:S(2)}) copy-start(f32[24]{0:T(128)} %constant.26.clone) | copy-start | bytes 292
  55.5 26.5 %copy-start.1 = (f32[4,1024]{1,0:T(4,128)S(1)}, f32[4,1024]{1,0:T(4,128)}, u32[]{:S(2)}) copy-start(f32[4,1024]{1,0:T(4,128)} %wind_u.1) | copy-start | bytes 49156
  55.5 26.5 %copy-start.2 = (f32[4,1024]{1,0:T(4,128)S(1)}, f32[4,1024]{1,0:T(4,128)}, u32[]{:S(2)}) copy-start(f32[4,1024]{1,0:T(4,128)} %wind_v.1) | copy-start | bytes 49156
  55.5 26.5 %all-to-all-start.2 = ((f32[8,91,4,128]{3,2,1,0:T(4,128)}), f32[8,91,4,128]{3,2,1,0:T(4,128)S(1)}, u32[]{:S(2)}, u32[]{:S(2)}) async-start(f32[8,91,4,128]{3,2,1,0:T(4,128)} %steps.3), calls=%async_computation.2 | async-start | bytes 2981888 | tf_op jit(solution)/shard_map/all_to_all | solution.py:521

commit v9 on v8

--- a/solution.py
+++ b/solution.py
@@ -153,46 +153,49 @@
                 out[j, d, count * BLOCKS + i] = value[:, i * LANES : (i + 1) * LANES]
 
 
-def halo_kernel(tiles, with_maps, *refs):
-    if with_maps:
-        own, maps, up, down = refs
-    else:
-        own, up, down = refs
+def halo_kernel(tiles, with_maps, group, *refs):
+    own, far, near = refs[0], refs[-2], refs[-1]
+    maps = refs[1] if with_maps else None
     n = len(SOUTH)
-    if with_maps:
-        for k in range(2):
-            for l in range(BLOCKS):
-                value = maps[k, :, l * LANES : (l + 1) * LANES]
-                up[PLANES, k * BLOCKS + l] = value
-                down[PLANES, k * BLOCKS + l] = value
-    ends = {
-        "s": (SOUTH[-1], SOUTH[0]),
-        "n": (NORTH[0], NORTH[-1]),
-    }
-
-    def body(t, carry):
-        for i, d in enumerate(SOUTH):
-            up[i, t] = own[d, t]
-        for i, d in enumerate(NORTH):
-            down[i, t] = own[d, t]
-        top, low = ends["s"]
-        a = [own[(top + k) % DIRS, t] for k in range(1, 4)]
-        b = [own[(low - k) % DIRS, t] for k in range(1, 4)]
-        up[n, t] = jnp.concatenate([a[2][3:4], a[0][1:4]], axis=0)
-        up[n + 1, t] = jnp.concatenate([b[1][2:4], a[1][2:4]], axis=0)
-        up[n + 2, t] = jnp.concatenate([b[2][3:4], b[0][1:4]], axis=0)
-        low, top = ends["n"]
-        a = [own[(low - k) % DIRS, t] for k in range(1, 4)]
-        b = [own[(top + k) % DIRS, t] for k in range(1, 4)]
-        down[n, t] = jnp.concatenate([a[0][0:3], a[2][0:1]], axis=0)
-        down[n + 1, t] = jnp.concatenate([a[1][0:2], b[1][0:2]], axis=0)
-        down[n + 2, t] = jnp.concatenate([b[0][0:3], b[2][0:1]], axis=0)
-        return carry
-
-    lax.fori_loop(0, tiles, body, 0, unroll=4)
-
-
-def step_kernel(chunk, first_call, group, coef, rfac, frsq, own, south, north, *refs):
+
+    def write(up, down):
+        if with_maps:
+            for k in range(2):
+                for l in range(BLOCKS):
+                    value = maps[k, :, l * LANES : (l + 1) * LANES]
+                    up[PLANES, k * BLOCKS + l] = value
+                    down[PLANES, k * BLOCKS + l] = value
+        ends = {
+            "s": (SOUTH[-1], SOUTH[0]),
+            "n": (NORTH[0], NORTH[-1]),
+        }
+
+        def body(t, carry):
+            for i, d in enumerate(SOUTH):
+                up[i, t] = own[d, t]
+            for i, d in enumerate(NORTH):
+                down[i, t] = own[d, t]
+            top, low = ends["s"]
+            a = [own[(top + k) % DIRS, t] for k in range(1, 4)]
+            b = [own[(low - k) % DIRS, t] for k in range(1, 4)]
+            up[n, t] = jnp.concatenate([a[2][3:4], a[0][1:4]], axis=0)
+            up[n + 1, t] = jnp.concatenate([b[1][2:4], a[1][2:4]], axis=0)
+            up[n + 2, t] = jnp.concatenate([b[2][3:4], b[0][1:4]], axis=0)
+            low, top = ends["n"]
+            a = [own[(low - k) % DIRS, t] for k in range(1, 4)]
+            b = [own[(top + k) % DIRS, t] for k in range(1, 4)]
+            down[n, t] = jnp.concatenate([a[0][0:3], a[2][0:1]], axis=0)
+            down[n + 1, t] = jnp.concatenate([a[1][0:2], b[1][0:2]], axis=0)
+            down[n + 2, t] = jnp.concatenate([b[0][0:3], b[2][0:1]], axis=0)
+            return carry
+
+        lax.fori_loop(0, tiles, body, 0, unroll=4)
+
+    pl.when(group[1] == 1)(lambda: write(far, near))
+    pl.when(group[1] == 0)(lambda: write(near, far))
+
+
+def step_kernel(chunk, first_call, group, coef, rfac, frsq, own, far, near, *refs):
     begin, count, tail = chunk
     tiles, slots = tiles_of(chunk), slots_of(chunk)
     if first_call:
@@ -234,49 +237,53 @@
             ex_a[i, p] = zero
             ex_b[i, p] = zero
 
-    if first_call:
-        for k in range(2):
-            for w, ref in enumerate((south, north)):
-                around[k, w, 0] = zero
-                around[k, w, BLOCKS + 1] = zero
-                for l in range(BLOCKS):
-                    mid = maps[k, :, l * LANES : (l + 1) * LANES]
-                    around[k, w, l + 1] = jnp.concatenate([mid, ref[PLANES, k * BLOCKS + l]], axis=0)
-                for i in range(WINDOW):
-                    left, right = around[k, w, me + i], around[k, w, me + i + 1]
-                    around[k, w, BLOCKS + 2 + i] = pltpu.roll(jnp.where(half, right, left), HALF, 1)
-
-    def fill(t, carry):
-        slot, m = slot_of(t), map_of(t)
-        seas = {"s": around[0, 0, m], "n": around[0, 1, m]}
-        n = len(SOUTH)
-
-        def whole_tile(w, d, rows):
-            return jnp.concatenate([own[d, t], rows], axis=0) * seas[w]
-
-        for i, d in enumerate(SOUTH):
-            st_a[d, slot] = whole_tile("s", d, south[i, t])
-        for i, d in enumerate(NORTH):
-            st_a[d, slot] = whole_tile("n", d, north[i, t])
-        for w, ref in (("s", south), ("n", north)):
-            a, b, c = (ref[n + i, t] for i in range(3))
-            swap = jnp.concatenate([b[2:4], b[0:2]], axis=0)
-            pick = slice(0, 1) if w == "s" else slice(3, 4)
-            far_a = jnp.broadcast_to(a[pick], (4, LANES))
-            far_c = jnp.broadcast_to(c[pick], (4, LANES))
-            if w == "s":
-                top, low = SOUTH[-1], SOUTH[0]
-                line = [(top + 1, a), (top + 2, b), (top + 3, far_a)]
-                line += [(low - 1, c), (low - 2, swap), (low - 3, far_c)]
-            else:
-                low, top = NORTH[0], NORTH[-1]
-                line = [(low - 1, a), (low - 2, b), (low - 3, far_a)]
-                line += [(top + 1, c), (top + 2, swap), (top + 3, far_c)]
-            for d, rows in line:
-                ex_a[EXTRA_AT[w, d % DIRS], slot] = whole_tile(w, d % DIRS, rows)
-        return carry
-
-    lax.fori_loop(0, tiles, fill, 0)
+    def load(south, north):
+        if first_call:
+            for k in range(2):
+                for w, ref in enumerate((south, north)):
+                    around[k, w, 0] = zero
+                    around[k, w, BLOCKS + 1] = zero
+                    for l in range(BLOCKS):
+                        mid = maps[k, :, l * LANES : (l + 1) * LANES]
+                        around[k, w, l + 1] = jnp.concatenate([mid, ref[PLANES, k * BLOCKS + l]], axis=0)
+                    for i in range(WINDOW):
+                        left, right = around[k, w, me + i], around[k, w, me + i + 1]
+                        around[k, w, BLOCKS + 2 + i] = pltpu.roll(jnp.where(half, right, left), HALF, 1)
+
+        def fill(t, carry):
+            slot, m = slot_of(t), map_of(t)
+            seas = {"s": around[0, 0, m], "n": around[0, 1, m]}
+            n = len(SOUTH)
+
+            def whole_tile(w, d, rows):
+                return jnp.concatenate([own[d, t], rows], axis=0) * seas[w]
+
+            for i, d in enumerate(SOUTH):
+                st_a[d, slot] = whole_tile("s", d, south[i, t])
+            for i, d in enumerate(NORTH):
+                st_a[d, slot] = whole_tile("n", d, north[i, t])
+            for w, ref in (("s", south), ("n", north)):
+                a, b, c = (ref[n + i, t] for i in range(3))
+                swap = jnp.concatenate([b[2:4], b[0:2]], axis=0)
+                pick = slice(0, 1) if w == "s" else slice(3, 4)
+                far_a = jnp.broadcast_to(a[pick], (4, LANES))
+                far_c = jnp.broadcast_to(c[pick], (4, LANES))
+                if w == "s":
+                    top, low = SOUTH[-1], SOUTH[0]
+                    line = [(top + 1, a), (top + 2, b), (top + 3, far_a)]
+                    line += [(low - 1, c), (low - 2, swap), (low - 3, far_c)]
+                else:
+                    low, top = NORTH[0], NORTH[-1]
+                    line = [(low - 1, a), (low - 2, b), (low - 3, far_a)]
+                    line += [(top + 1, c), (top + 2, swap), (top + 3, far_c)]
+                for d, rows in line:
+                    ex_a[EXTRA_AT[w, d % DIRS], slot] = whole_tile(w, d % DIRS, rows)
+            return carry
+
+        lax.fori_loop(0, tiles, fill, 0)
+
+    pl.when(group[1] == 1)(lambda: load(near, far))
+    pl.when(group[1] == 0)(lambda: load(far, near))
 
     for i in range(2 * BLOCKS):
         sums[i] = jnp.zeros((4, LANES), jnp.float32) if first_call else given_sums[i]
@@ -373,11 +380,11 @@
         late.wait()
 
 
-def step_call(chunk, first_call, group, own, south, north, rest):
+def step_call(chunk, first_call, group, own, far, near, rest):
     slots = slots_of(chunk)
     state = pltpu.VMEM((DIRS, slots, 8, LANES), jnp.float32)
     extra = pltpu.VMEM((len(EXTRAS), slots, 8, LANES), jnp.float32)
-    args = (group, COEF, RFAC, FR * FR, own, south, north, *rest)
+    args = (group, COEF, RFAC, FR * FR, own, far, near, *rest)
     scratch = [state, state, extra, extra]
     if first_call:
         out = [
@@ -470,10 +477,10 @@
 
 def on_device(spectrum, sea_mask, turning, wind_u, wind_v):
     me = lax.axis_index("spec")
-    group = me.reshape(1)
+    group = jnp.stack([me, lax.axis_index("space") % 2])
     count = lax.axis_size("space")
-    up = [(i, i + 1) for i in range(count - 1)]
-    down = [(j, i) for i, j in up]
+    swaps = [[(i, i + 1) for i in range(first, count - 1, 2)] for first in (1, 0)]
+    over, within = ([*pairs, *((j, i) for i, j in pairs)] for pairs in swaps)
 
     maps = jnp.stack([(sea_mask == 1).astype(jnp.float32), turning])
     hbm = pl.BlockSpec(memory_space=pltpu.HBM)
@@ -504,20 +511,20 @@
 
     def edges(tiles, planes, *args):
         kernel = functools.partial(halo_kernel, tiles, len(args) > 1)
-        return call(kernel, "halo", [(planes, tiles, 4, LANES)] * 2, args, 0)
+        return call(kernel, "halo", [(planes, tiles, 4, LANES)] * 2, (group, *args), 1)
 
     own = lax.all_to_all(pack, "spec", 0, 0, tiled=True)
     own = tiled(own).reshape(DIRS, tiles_of(first), 4, LANES)
-    low, high = edges(tiles_of(first), PLANES + 1, own, maps)
-    pack_2, low, high = lax.optimization_barrier((pack_2, low, high))
+    far, near = edges(tiles_of(first), PLANES + 1, own, maps)
+    pack_2, far, near = lax.optimization_barrier((pack_2, far, near))
     own_2 = lax.all_to_all(pack_2, "spec", 0, 0, tiled=True)
     own_2 = own_2.reshape(DIRS, tiles_of(last), 4, LANES)
-    low_2, high_2 = edges(tiles_of(last), PLANES, own_2)
-    south, north = lax.ppermute(low, "space", up), lax.ppermute(high, "space", down)
-    south, north, _, _ = lax.optimization_barrier((south, north, low_2, high_2))
-    south_2, north_2 = lax.ppermute(low_2, "space", up), lax.ppermute(high_2, "space", down)
-    made, around, sums = step_call(CHUNKS[0], True, group, own, south, north, (maps,))
-    (made,) = step_call(CHUNKS[1], False, group, own_2, south_2, north_2, (around, made, sums))
+    far_2, near_2 = edges(tiles_of(last), PLANES, own_2)
+    far, near = lax.ppermute(far, "space", over), lax.ppermute(near, "space", within)
+    far, near, _, _ = lax.optimization_barrier((far, near, far_2, near_2))
+    far_2, near_2 = lax.ppermute(far_2, "space", over), lax.ppermute(near_2, "space", within)
+    made, around, sums = step_call(CHUNKS[0], True, group, own, far, near, (maps,))
+    (made,) = step_call(CHUNKS[1], False, group, own_2, far_2, near_2, (around, made, sums))
     got = lax.all_to_all(made, "spec", 0, 0, tiled=True)
     cos = lax.dynamic_slice_in_dim(jnp.asarray(COS), me * 3, 3)
     sin = lax.dynamic_slice_in_dim(jnp.asarray(SIN), me * 3, 3)

time: 84.8 us -> 83 us (0.979)
  starting transfers between devices: 32 us -> 24.2 us
  waiting for transfers between devices: 34 us -> 39.9 us
    all_to_all x1, waiting for transfers between devices: 0.78 us -> 8.39 us  [on_device(): own_2 = lax.all_to_all(pack_2, 'spec', 0, 0, tiled=True)]
    ppermute x4, starting transfers between devices: 17.1 us -> 11.5 us  [the longest x1 4.58 us: on_device(): lax.ppermute(far, 'space', over)]
    all_to_all x1, starting transfers between devices: 5.89 us -> 3.72 us  [on_device(): got = lax.all_to_all(made, 'spec', 0, 0, tiled=True)]
    all_to_all x1, waiting for transfers between devices: 20.4 us -> 18.4 us  [on_device(): got = lax.all_to_all(made, 'spec', 0, 0, tiled=True)]
  transfers between devices with their start and end apart: 7 -> 7, of which waited for: 4 -> 5; matrix products, arithmetic and copies ran while one was open for 0% -> 0% of each run, Pallas kernels for 10% -> 10%
where the time goes in v9:
time: 83 us; the launch traced here: 81.6 us
  waiting for transfers between devices  39.9 us (48%)
  starting transfers between devices  24.2 us (29%)
  Pallas kernels  16.9 us (20%)
    all_to_all x1, waiting for transfers between devices, on_device(): got = lax.all_to_all(made, 'spec', 0, 0, tiled=True)  18.4 us
    pallas_call x5, Pallas kernels, moving(): pl.pallas_call(kernel, out_shape=[jax.ShapeDtypeStruct(s, jnp.float32) fo...  15.6 us
    all_to_all x1, waiting for transfers between devices, on_device(): own = lax.all_to_all(pack, 'spec', 0, 0, tiled=True)  9.67 us
    all_to_all x1, waiting for transfers between devices, on_device(): own_2 = lax.all_to_all(pack_2, 'spec', 0, 0, tiled=True)  8.39 us
    all_to_all x1, starting transfers between devices, on_device(): own = lax.all_to_all(pack, 'spec', 0, 0, tiled=True)  5.32 us
    ppermute x1, starting transfers between devices, on_device(): lax.ppermute(far, 'space', over)  4.58 us
    all_to_all x1, starting transfers between devices, on_device(): got = lax.all_to_all(made, 'spec', 0, 0, tiled=True)  3.72 us
    all_to_all x1, starting transfers between devices, on_device(): own_2 = lax.all_to_all(pack_2, 'spec', 0, 0, tiled=True)  3.65 us
  transfers between devices with their start and end apart: 7, of which 5 were waited for; matrix products, arithmetic and copies ran while one was open for 0% of the time, Pallas kernels for 10%

profile of v9, /device:TPU:448, one launch (start us, length us, event | category | flops | bytes accessed | tf_op | source)
XLA Modules:
  0.0 81.6 jit_solution(15332302684751478209)
XLA Ops:
  0.0 2.0 %first_pack.1 = f32[8,3,2,4,1024]{4,3,2,1,0:T(4,128)} custom-call(f32[3,25,4,1024]{3,2,1,0:T(4,128)} %spectrum.3), custom_call_target="tpu_custom_call" | custom-call | flops 1000 | bytes 4000000 | tf_op jit(solution)/shard_map/first_pack/pallas_call | solution.py:461
  2.0 0.0 copy-start.5
  2.0 0.0 copy-start.6
  2.1 5.3 %all-to-all-start = ((f32[8,3,2,4,1024]{4,3,2,1,0:T(4,128)}), f32[8,3,2,4,1024]{4,3,2,1,0:T(4,128)S(1)}, u32[]{:S(2)}, u32[]{:S(2)}) async-start(f32[8,3,2,4,1024]{4,3,2,1,0:T(4,128)} %first_pack.1), calls=%async_computation | async-start | bytes 1572864 | tf_op jit(solution)/shard_map/all_to_all | solution.py:516
  7.4 2.1 %last_pack.1 = f32[8,3,10,4,128]{4,3,2,1,0:T(4,128)} custom-call(f32[3,25,4,1024]{3,2,1,0:T(4,128)} %spectrum.3), custom_call_target="tpu_custom_call" | custom-call | flops 1000 | bytes 4000000 | tf_op jit(solution)/shard_map/last_pack/pallas_call | solution.py:461
  9.5 0.0 copy-start
  9.5 0.0 copy-start.3
  9.6 0.0 copy-start.4
  9.6 0.1 pad_add_fusion.group
  9.7 0.0 copy-done.5
  9.7 0.0 copy-done.6
  9.7 9.7 %all-to-all-done = f32[8,3,2,4,1024]{4,3,2,1,0:T(4,128)S(1)} async-done(((f32[8,3,2,4,1024]{4,3,2,1,0:T(4,128)}), f32[8,3,2,4,1024]{4,3,2,1,0:T(4,128)S(1)}, u32[]{:S(2)}, u32[]{:S(2)}) %all-to-all-start) | async-done | bytes 786464 | tf_op jit(solution)/shard_map/all_to_all | solution.py:516
  19.4 0.7 halo.2
  20.1 3.6 %all-to-all-start.1 = ((f32[8,3,10,4,128]{4,3,2,1,0:T(4,128)}), f32[8,3,10,4,128]{4,3,2,1,0:T(4,128)S(1)}, u32[]{:S(2)}, u32[]{:S(2)}) async-start(f32[8,3,10,4,128]{4,3,2,1,0:T(4,128)} %last_pack.1), calls=%async_computation.1 | async-start | bytes 983040 | tf_op jit(solution)/shard_map/all_to_all | solution.py:520
  23.7 4.6 %collective-permute-start.2 = (f32[16,16,4,128]{3,2,1,0:T(4,128)S(1)}, f32[16,16,4,128]{3,2,1,0:T(4,128)S(1)}, u32[]{:S(2)}, u32[]{:S(2)}) collective-permute-start(f32[16,16,4,128]{3,2,1,0:T(4,128)S(1)} %get-tuple-element.22), channel_id=1, source_target_pairs={{8,16},{24,32},{40,48},{56,64},{72,80},{88,96},{104,112},{120,128}... | collective-permute-start | bytes 1572872 | tf_op jit(solution)/shard_map/ppermute | solution.py:523
  28.3 1.9 %collective-permute-start.3 = (f32[16,16,4,128]{3,2,1,0:T(4,128)S(1)}, f32[16,16,4,128]{3,2,1,0:T(4,128)S(1)}, u32[]{:S(2)}, u32[]{:S(2)}) collective-permute-start(f32[16,16,4,128]{3,2,1,0:T(4,128)S(1)} %get-tuple-element.23), channel_id=1, source_target_pairs={{0,8},{16,24},{32,40},{48,56},{64,72},{80,88},{96,104},{112,120},{... | collective-permute-start | bytes 1572872 | tf_op jit(solution)/shard_map/ppermute | solution.py:523
  30.3 8.4 %all-to-all-done.1 = f32[8,3,10,4,128]{4,3,2,1,0:T(4,128)S(1)} async-done(((f32[8,3,10,4,128]{4,3,2,1,0:T(4,128)}), f32[8,3,10,4,128]{4,3,2,1,0:T(4,128)S(1)}, u32[]{:S(2)}, u32[]{:S(2)}) %all-to-all-start.1) | async-done | bytes 491552 | tf_op jit(solution)/shard_map/all_to_all | solution.py:520
  38.7 0.6 halo.3
  39.3 1.9 %collective-permute-start = (f32[15,10,4,128]{3,2,1,0:T(4,128)S(1)}, f32[15,10,4,128]{3,2,1,0:T(4,128)S(1)}, u32[]{:S(2)}, u32[]{:S(2)}) collective-permute-start(f32[15,10,4,128]{3,2,1,0:T(4,128)S(1)} %get-tuple-element.20), channel_id=1, source_target_pairs={{8,16},{24,32},{40,48},{56,64},{72,80},{88,96},{104,112},{120,128}... | collective-permute-start | bytes 921608 | tf_op jit(solution)/shard_map/ppermute | solution.py:525
  41.2 3.1 %collective-permute-start.1 = (f32[15,10,4,128]{3,2,1,0:T(4,128)S(1)}, f32[15,10,4,128]{3,2,1,0:T(4,128)S(1)}, u32[]{:S(2)}, u32[]{:S(2)}) collective-permute-start(f32[15,10,4,128]{3,2,1,0:T(4,128)S(1)} %get-tuple-element.21), channel_id=1, source_target_pairs={{0,8},{16,24},{32,40},{48,56},{64,72},{80,88},{96,104},{112,120},{... | collective-permute-start | bytes 921608 | tf_op jit(solution)/shard_map/ppermute | solution.py:525
  44.3 0.1 collective-permute-done.2.far
  44.4 0.0 collective-permute-done.3.near
  44.4 0.0 copy-done
  44.4 0.0 copy-done.3
  44.4 0.0 copy-done.4
  44.4 5.5 %steps.2 = (f32[8,48,4,128]{3,2,1,0:T(4,128)S(1)}, f32[2,2,12,8,128]{4,3,2,1,0:T(8,128)S(1)}, f32[16,4,128]{2,1,0:T(4,128)S(1)}) custom-call(s32[2]{0:T(128)S(1)} %pad_add_fusion.group, f32[25,18]{1,0:T(8,128)S(1)} %copy-done, f32[25]{0:T(128)S(1)} %copy-done.3, f32[25]{0:T(128)S(1)} %copy-done.4, f32[24,16,4,128]{3,2,1,0:T(4,128)S(1)} %bitcast.12, ...), custom_call_target="tpu_custom_call" | custom-call | flops 1000 | bytes 20000000 | tf_op jit(solution)/shard_map/steps/pallas_call | solution.py:461
  49.9 3.4 %collective-permute-done.far = f32[15,10,4,128]{3,2,1,0:T(4,128)S(1)} collective-permute-done((f32[15,10,4,128]{3,2,1,0:T(4,128)S(1)}, f32[15,10,4,128]{3,2,1,0:T(4,128)S(1)}, u32[]{:S(2)}, u32[]{:S(2)}) %collective-permute-start) | collective-permute-done | bytes 307232 | tf_op jit(solution)/shard_map/ppermute | solution.py:525
  53.3 0.0 collective-permute-done.1.near
  53.3 4.1 %steps.3 = f32[8,91,4,128]{3,2,1,0:T(4,128)} custom-call(s32[2]{0:T(128)S(1)} %pad_add_fusion.group, f32[25,18]{1,0:T(8,128)S(1)} %copy-done, f32[25]{0:T(128)S(1)} %copy-done.3, f32[25]{0:T(128)S(1)} %copy-done.4, f32[24,10,4,128]{3,2,1,0:T(4,128)S(1)} %bitcast.14, f32[15,10,4,128]{3,2,1,0:T(4,128)S(1)} %collective-permute-done.far, ...), custom_call_target="tpu_custom_call" | custom-call | flops 1000 | bytes 20000000 | tf_op jit(solution)/shard_map/steps/pallas_call | solution.py:461
  57.3 0.0 copy-start.8
  57.4 0.0 copy-start.7
  57.4 0.0 copy-start.1
  57.4 0.0 copy-start.2
  57.4 3.7 %all-to-all-start.2 = ((f32[8,91,4,128]{3,2,1,0:T(4,128)}), f32[8,91,4,128]{3,2,1,0:T(4,128)S(1)}, u32[]{:S(2)}, u32[]{:S(2)}) async-start(f32[8,91,4,128]{3,2,1,0:T(4,128)} %steps.3), calls=%async_computation.2 | async-start | bytes 2981888 | tf_op jit(solution)/shard_map/all_to_all | solution.py:528
  61.1 0.0 copy-done.8
  61.1 0.1 dynamic_slice.6.cos
  61.2 0.0 copy-done.7
  61.2 0.1 dynamic_slice.7.sin
  61.3 18.4 %all-to-all-done.2.got = f32[8,91,4,128]{3,2,1,0:T(4,128)S(1)} async-done(((f32[8,91,4,128]{3,2,1,0:T(4,128)}), f32[8,91,4,128]{3,2,1,0:T(4,128)S(1)}, u32[]{:S(2)}, u32[]{:S(2)}) %all-to-all-start.2) | async-done | bytes 1490976 | tf_op jit(solution)/shard_map/all_to_all | solution.py:528
  79.7 0.0 copy-done.1
  79.7 0.0 copy-done.2
  79.7 1.9 %source.1 = f32[3,25,4,1024]{3,2,1,0:T(4,128)} custom-call(f32[3]{0:T(128)S(1)} %dynamic_slice.6.cos, f32[3]{0:T(128)S(1)} %dynamic_slice.7.sin, f32[8,91,4,128]{3,2,1,0:T(4,128)S(1)} %all-to-all-done.2.got, f32[4,1024]{1,0:T(4,128)S(1)} %copy-done.1, f32[4,1024]{1,0:T(4,128)S(1)} %copy-done.2), custom_call_target="tpu_custom_call" | custom-call | flops 1000 | bytes 4000000 | tf_op jit(solution)/shard_map/source/pallas_call | solution.py:461
  (2 shorter events, 0.0 us)
Async XLA Ops:
  2.0 7.6 %copy-start.5 = (s32[4,1024]{1,0:T(4,128)S(1)}, s32[4,1024]{1,0:T(4,128)}, u32[]{:S(2)}) copy-start(s32[4,1024]{1,0:T(4,128)} %param.12) | copy-start | bytes 49156
  2.0 7.6 %copy-start.6 = (f32[4,1024]{1,0:T(4,128)S(1)}, f32[4,1024]{1,0:T(4,128)}, u32[]{:S(2)}) copy-start(f32[4,1024]{1,0:T(4,128)} %param.13) | copy-start | bytes 49156
  2.1 17.3 %all-to-all-start = ((f32[8,3,2,4,1024]{4,3,2,1,0:T(4,128)}), f32[8,3,2,4,1024]{4,3,2,1,0:T(4,128)S(1)}, u32[]{:S(2)}, u32[]{:S(2)}) async-start(f32[8,3,2,4,1024]{4,3,2,1,0:T(4,128)} %first_pack.1), calls=%async_computation | async-start | bytes 1572864 | tf_op jit(solution)/shard_map/all_to_all | solution.py:516
  9.5 34.9 %copy-start = (f32[25,18]{1,0:T(8,128)S(1)}, f32[25,18]{1,0:T(8,128)}, u32[]{:S(2)}) copy-start(f32[25,18]{1,0:T(8,128)} %constant.38.clone.coef) | copy-start | bytes 5404
  9.5 34.9 %copy-start.3 = (f32[25]{0:T(128)S(1)}, f32[25]{0:T(128)}, u32[]{:S(2)}) copy-start(f32[25]{0:T(128)} %constant.39.clone.rfac) | copy-start | bytes 304
  9.6 34.9 %copy-start.4 = (f32[25]{0:T(128)S(1)}, f32[25]{0:T(128)}, u32[]{:S(2)}) copy-start(f32[25]{0:T(128)} %constant.40.clone.frsq) | copy-start | bytes 304
  20.1 18.6 %all-to-all-start.1 = ((f32[8,3,10,4,128]{4,3,2,1,0:T(4,128)}), f32[8,3,10,4,128]{4,3,2,1,0:T(4,128)S(1)}, u32[]{:S(2)}, u32[]{:S(2)}) async-start(f32[8,3,10,4,128]{4,3,2,1,0:T(4,128)} %last_pack.1), calls=%async_computation.1 | async-start | bytes 983040 | tf_op jit(solution)/shard_map/all_to_all | solution.py:520
  23.7 20.7 %collective-permute-start.2 = (f32[16,16,4,128]{3,2,1,0:T(4,128)S(1)}, f32[16,16,4,128]{3,2,1,0:T(4,128)S(1)}, u32[]{:S(2)}, u32[]{:S(2)}) collective-permute-start(f32[16,16,4,128]{3,2,1,0:T(4,128)S(1)} %get-tuple-element.22), channel_id=1, source_target_pairs={{8,16},{24,32},{40,48},{56,64},{72,80},{88,96},{104,112},{120,128}... | collective-permute-start | bytes 1572872 | tf_op jit(solution)/shard_map/ppermute | solution.py:523
  28.3 16.1 %collective-permute-start.3 = (f32[16,16,4,128]{3,2,1,0:T(4,128)S(1)}, f32[16,16,4,128]{3,2,1,0:T(4,128)S(1)}, u32[]{:S(2)}, u32[]{:S(2)}) collective-permute-start(f32[16,16,4,128]{3,2,1,0:T(4,128)S(1)} %get-tuple-element.23), channel_id=1, source_target_pairs={{0,8},{16,24},{32,40},{48,56},{64,72},{80,88},{96,104},{112,120},{... | collective-permute-start | bytes 1572872 | tf_op jit(solution)/shard_map/ppermute | solution.py:523
  39.3 14.0 %collective-permute-start = (f32[15,10,4,128]{3,2,1,0:T(4,128)S(1)}, f32[15,10,4,128]{3,2,1,0:T(4,128)S(1)}, u32[]{:S(2)}, u32[]{:S(2)}) collective-permute-start(f32[15,10,4,128]{3,2,1,0:T(4,128)S(1)} %get-tuple-element.20), channel_id=1, source_target_pairs={{8,16},{24,32},{40,48},{56,64},{72,80},{88,96},{104,112},{120,128}... | collective-permute-start | bytes 921608 | tf_op jit(solution)/shard_map/ppermute | solution.py:525
  41.2 12.0 %collective-permute-start.1 = (f32[15,10,4,128]{3,2,1,0:T(4,128)S(1)}, f32[15,10,4,128]{3,2,1,0:T(4,128)S(1)}, u32[]{:S(2)}, u32[]{:S(2)}) collective-permute-start(f32[15,10,4,128]{3,2,1,0:T(4,128)S(1)} %get-tuple-element.21), channel_id=1, source_target_pairs={{0,8},{16,24},{32,40},{48,56},{64,72},{80,88},{96,104},{112,120},{... | collective-permute-start | bytes 921608 | tf_op jit(solution)/shard_map/ppermute | solution.py:525
  57.3 3.8 %copy-start.8 = (f32[24]{0:T(128)S(1)}, f32[24]{0:T(128)}, u32[]{:S(2)}) copy-start(f32[24]{0:T(128)} %constant.41.clone) | copy-start | bytes 292
  57.4 3.9 %copy-start.7 = (f32[24]{0:T(128)S(1)}, f32[24]{0:T(128)}, u32[]{:S(2)}) copy-start(f32[24]{0:T(128)} %constant.42.clone) | copy-start | bytes 292
  57.4 22.4 %copy-start.1 = (f32[4,1024]{1,0:T(4,128)S(1)}, f32[4,1024]{1,0:T(4,128)}, u32[]{:S(2)}) copy-start(f32[4,1024]{1,0:T(4,128)} %wind_u.1) | copy-start | bytes 49156
  57.4 22.3 %copy-start.2 = (f32[4,1024]{1,0:T(4,128)S(1)}, f32[4,1024]{1,0:T(4,128)}, u32[]{:S(2)}) copy-start(f32[4,1024]{1,0:T(4,128)} %wind_v.1) | copy-start | bytes 49156
  57.4 22.3 %all-to-all-start.2 = ((f32[8,91,4,128]{3,2,1,0:T(4,128)}), f32[8,91,4,128]{3,2,1,0:T(4,128)S(1)}, u32[]{:S(2)}, u32[]{:S(2)}) async-start(f32[8,91,4,128]{3,2,1,0:T(4,128)} %steps.3), calls=%async_computation.2 | async-start | bytes 2981888 | tf_op jit(solution)/shard_map/all_to_all | solution.py:528

commit v10 on v9

--- a/solution.py
+++ b/solution.py
@@ -70,6 +70,7 @@
         ("n", (NORTH[0] - k) % DIRS, k),
     ]
 EXTRA_AT = {(w, d): i for i, (w, d, _) in enumerate(EXTRAS)}
+NEAR_AT = (PLANES + 1) * CHUNKS[0][1] * BLOCKS
 VMEM_LIMIT = 40 * 1024 * 1024
 
 
@@ -154,17 +155,21 @@
 
 
 def halo_kernel(tiles, with_maps, group, *refs):
-    own, far, near = refs[0], refs[-2], refs[-1]
-    maps = refs[1] if with_maps else None
+    own, more, far, near = refs
+    skip = 0 if with_maps else NEAR_AT
+    maps = more
+    if skip:
+        for i in range(skip):
+            near[i] = more[i]
     n = len(SOUTH)
 
-    def write(up, down):
+    def write(up, down, up_at, down_at):
         if with_maps:
             for k in range(2):
                 for l in range(BLOCKS):
                     value = maps[k, :, l * LANES : (l + 1) * LANES]
-                    up[PLANES, k * BLOCKS + l] = value
-                    down[PLANES, k * BLOCKS + l] = value
+                    up[up_at + PLANES * tiles + k * BLOCKS + l] = value
+                    down[down_at + PLANES * tiles + k * BLOCKS + l] = value
         ends = {
             "s": (SOUTH[-1], SOUTH[0]),
             "n": (NORTH[0], NORTH[-1]),
@@ -172,27 +177,27 @@
 
         def body(t, carry):
             for i, d in enumerate(SOUTH):
-                up[i, t] = own[d, t]
+                up[up_at + i * tiles + t] = own[d, t]
             for i, d in enumerate(NORTH):
-                down[i, t] = own[d, t]
+                down[down_at + i * tiles + t] = own[d, t]
             top, low = ends["s"]
             a = [own[(top + k) % DIRS, t] for k in range(1, 4)]
             b = [own[(low - k) % DIRS, t] for k in range(1, 4)]
-            up[n, t] = jnp.concatenate([a[2][3:4], a[0][1:4]], axis=0)
-            up[n + 1, t] = jnp.concatenate([b[1][2:4], a[1][2:4]], axis=0)
-            up[n + 2, t] = jnp.concatenate([b[2][3:4], b[0][1:4]], axis=0)
+            up[up_at + (n) * tiles + t] = jnp.concatenate([a[2][3:4], a[0][1:4]], axis=0)
+            up[up_at + (n + 1) * tiles + t] = jnp.concatenate([b[1][2:4], a[1][2:4]], axis=0)
+            up[up_at + (n + 2) * tiles + t] = jnp.concatenate([b[2][3:4], b[0][1:4]], axis=0)
             low, top = ends["n"]
             a = [own[(low - k) % DIRS, t] for k in range(1, 4)]
             b = [own[(top + k) % DIRS, t] for k in range(1, 4)]
-            down[n, t] = jnp.concatenate([a[0][0:3], a[2][0:1]], axis=0)
-            down[n + 1, t] = jnp.concatenate([a[1][0:2], b[1][0:2]], axis=0)
-            down[n + 2, t] = jnp.concatenate([b[0][0:3], b[2][0:1]], axis=0)
+            down[down_at + (n) * tiles + t] = jnp.concatenate([a[0][0:3], a[2][0:1]], axis=0)
+            down[down_at + (n + 1) * tiles + t] = jnp.concatenate([a[1][0:2], b[1][0:2]], axis=0)
+            down[down_at + (n + 2) * tiles + t] = jnp.concatenate([b[0][0:3], b[2][0:1]], axis=0)
             return carry
 
         lax.fori_loop(0, tiles, body, 0, unroll=4)
 
-    pl.when(group[1] == 1)(lambda: write(far, near))
-    pl.when(group[1] == 0)(lambda: write(near, far))
+    pl.when(group[1] == 1)(lambda: write(far, near, 0, skip))
+    pl.when(group[1] == 0)(lambda: write(near, far, skip, 0))
 
 
 def step_kernel(chunk, first_call, group, coef, rfac, frsq, own, far, near, *refs):
@@ -237,15 +242,17 @@
             ex_a[i, p] = zero
             ex_b[i, p] = zero
 
-    def load(south, north):
+    skip = 0 if first_call else NEAR_AT
+
+    def load(south, north, south_at, north_at):
         if first_call:
             for k in range(2):
-                for w, ref in enumerate((south, north)):
+                for w, (ref, at) in enumerate(((south, south_at), (north, north_at))):
                     around[k, w, 0] = zero
                     around[k, w, BLOCKS + 1] = zero
                     for l in range(BLOCKS):
                         mid = maps[k, :, l * LANES : (l + 1) * LANES]
-                        around[k, w, l + 1] = jnp.concatenate([mid, ref[PLANES, k * BLOCKS + l]], axis=0)
+                        around[k, w, l + 1] = jnp.concatenate([mid, ref[at + PLANES * tiles + k * BLOCKS + l]], axis=0)
                     for i in range(WINDOW):
                         left, right = around[k, w, me + i], around[k, w, me + i + 1]
                         around[k, w, BLOCKS + 2 + i] = pltpu.roll(jnp.where(half, right, left), HALF, 1)
@@ -259,11 +266,11 @@
                 return jnp.concatenate([own[d, t], rows], axis=0) * seas[w]
 
             for i, d in enumerate(SOUTH):
-                st_a[d, slot] = whole_tile("s", d, south[i, t])
+                st_a[d, slot] = whole_tile("s", d, south[south_at + i * tiles + t])
             for i, d in enumerate(NORTH):
-                st_a[d, slot] = whole_tile("n", d, north[i, t])
-            for w, ref in (("s", south), ("n", north)):
-                a, b, c = (ref[n + i, t] for i in range(3))
+                st_a[d, slot] = whole_tile("n", d, north[north_at + i * tiles + t])
+            for w, ref, at in (("s", south, south_at), ("n", north, north_at)):
+                a, b, c = (ref[at + (n + i) * tiles + t] for i in range(3))
                 swap = jnp.concatenate([b[2:4], b[0:2]], axis=0)
                 pick = slice(0, 1) if w == "s" else slice(3, 4)
                 far_a = jnp.broadcast_to(a[pick], (4, LANES))
@@ -282,8 +289,8 @@
 
         lax.fori_loop(0, tiles, fill, 0)
 
-    pl.when(group[1] == 1)(lambda: load(near, far))
-    pl.when(group[1] == 0)(lambda: load(far, near))
+    pl.when(group[1] == 1)(lambda: load(near, far, skip, 0))
+    pl.when(group[1] == 0)(lambda: load(far, near, 0, skip))
 
     for i in range(2 * BLOCKS):
         sums[i] = jnp.zeros((4, LANES), jnp.float32) if first_call else given_sums[i]
@@ -509,22 +516,23 @@
         [room, pltpu.SemaphoreType.DMA((3,))],
     )
 
-    def edges(tiles, planes, *args):
-        kernel = functools.partial(halo_kernel, tiles, len(args) > 1)
-        return call(kernel, "halo", [(planes, tiles, 4, LANES)] * 2, (group, *args), 1)
+    def edges(tiles, sizes, with_maps, *args):
+        kernel = functools.partial(halo_kernel, tiles, with_maps)
+        return call(kernel, "halo", [(n, 4, LANES) for n in sizes], (group, *args), 1)
 
     own = lax.all_to_all(pack, "spec", 0, 0, tiled=True)
     own = tiled(own).reshape(DIRS, tiles_of(first), 4, LANES)
-    far, near = edges(tiles_of(first), PLANES + 1, own, maps)
+    far, near = edges(tiles_of(first), [NEAR_AT] * 2, True, own, maps)
     pack_2, far, near = lax.optimization_barrier((pack_2, far, near))
     own_2 = lax.all_to_all(pack_2, "spec", 0, 0, tiled=True)
     own_2 = own_2.reshape(DIRS, tiles_of(last), 4, LANES)
-    far_2, near_2 = edges(tiles_of(last), PLANES, own_2)
+    extra = PLANES * tiles_of(last)
+    far_2, near = edges(tiles_of(last), [extra, NEAR_AT + extra], False, own_2, near)
     far, near = lax.ppermute(far, "space", over), lax.ppermute(near, "space", within)
-    far, near, _, _ = lax.optimization_barrier((far, near, far_2, near_2))
-    far_2, near_2 = lax.ppermute(far_2, "space", over), lax.ppermute(near_2, "space", within)
+    far, near, _ = lax.optimization_barrier((far, near, far_2))
+    far_2 = lax.ppermute(far_2, "space", over)
     made, around, sums = step_call(CHUNKS[0], True, group, own, far, near, (maps,))
-    (made,) = step_call(CHUNKS[1], False, group, own_2, far_2, near_2, (around, made, sums))
+    (made,) = step_call(CHUNKS[1], False, group, own_2, far_2, near, (around, made, sums))
     got = lax.all_to_all(made, "spec", 0, 0, tiled=True)
     cos = lax.dynamic_slice_in_dim(jnp.asarray(COS), me * 3, 3)
     sin = lax.dynamic_slice_in_dim(jnp.asarray(SIN), me * 3, 3)

time: 83 us -> 93.3 us (1.12)
  blocking collectives: 0 us -> 13.6 us
  starting transfers between devices: 24.2 us -> 21 us
    all_to_all x0 -> x1, blocking collectives: none -> 13.6 us  [on_device(): own_2 = lax.all_to_all(pack_2, 'spec', 0, 0, tiled=True)]
    ppermute x1, waiting for transfers between devices: 0.06 us -> 11.5 us  [on_device(): lax.ppermute(far, 'space', over)]
    all_to_all x1 -> x0, waiting for transfers between devices: 8.39 us -> none  [on_device(): own_2 = lax.all_to_all(pack_2, 'spec', 0, 0, tiled=True)]
    all_to_all x1 -> x0, starting transfers between devices: 3.65 us -> none  [on_device(): own_2 = lax.all_to_all(pack_2, 'spec', 0, 0, tiled=True)]
    ppermute x2 -> x1, waiting for transfers between devices: 3.36 us -> 0.01 us  [on_device(): far_2 = lax.ppermute(far_2, 'space', over)]
    ppermute x2 -> x1, starting transfers between devices: 5.02 us -> 3.22 us  [on_device(): far_2 = lax.ppermute(far_2, 'space', over)]
    all_to_all x1, starting transfers between devices: 3.72 us -> 5.16 us  [on_device(): got = lax.all_to_all(made, 'spec', 0, 0, tiled=True)]
  transfers between devices with their start and end apart: 7 -> 5, of which waited for: 5 -> 3; matrix products, arithmetic and copies ran while one was open for 0% -> 0% of each run, Pallas kernels for 10% -> 8%
where the time goes in v10:
time: 93.3 us; the launch traced here: 92.7 us
  waiting for transfers between devices  40.5 us (43%)
  starting transfers between devices  21 us (23%)
  Pallas kernels  17.1 us (18%)
  blocking collectives  13.6 us (15%)
    all_to_all x1, waiting for transfers between devices, on_device(): got = lax.all_to_all(made, 'spec', 0, 0, tiled=True)  19.3 us
    pallas_call x5, Pallas kernels, moving(): pl.pallas_call(kernel, out_shape=[jax.ShapeDtypeStruct(s, jnp.float32) fo...  15.7 us
    all_to_all x1, blocking collectives, on_device(): own_2 = lax.all_to_all(pack_2, 'spec', 0, 0, tiled=True)  13.6 us
    ppermute x1, waiting for transfers between devices, on_device(): lax.ppermute(far, 'space', over)  11.5 us
    all_to_all x1, waiting for transfers between devices, on_device(): own = lax.all_to_all(pack, 'spec', 0, 0, tiled=True)  9.67 us
    ppermute x1, starting transfers between devices, on_device(): lax.ppermute(far, 'space', over)  5.36 us
    all_to_all x1, starting transfers between devices, on_device(): own = lax.all_to_all(pack, 'spec', 0, 0, tiled=True)  5.32 us
    all_to_all x1, starting transfers between devices, on_device(): got = lax.all_to_all(made, 'spec', 0, 0, tiled=True)  5.16 us
  transfers between devices with their start and end apart: 5, of which 3 were waited for; matrix products, arithmetic and copies ran while one was open for 0% of the time, Pallas kernels for 8%

profile of v10, /device:TPU:448, one launch (start us, length us, event | category | flops | bytes accessed | tf_op | source)
XLA Modules:
  0.0 92.7 jit_solution(6183536070611204825)
XLA Ops:
  0.0 2.0 %first_pack.1 = f32[8,3,2,4,1024]{4,3,2,1,0:T(4,128)} custom-call(f32[3,25,4,1024]{3,2,1,0:T(4,128)} %spectrum.3), custom_call_target="tpu_custom_call" | custom-call | flops 1000 | bytes 4000000 | tf_op jit(solution)/shard_map/first_pack/pallas_call | solution.py:468
  2.0 0.0 copy-start.5
  2.0 0.0 copy-start.6
  2.1 5.3 %all-to-all-start = ((f32[8,3,2,4,1024]{4,3,2,1,0:T(4,128)}), f32[8,3,2,4,1024]{4,3,2,1,0:T(4,128)S(1)}, u32[]{:S(2)}, u32[]{:S(2)}) async-start(f32[8,3,2,4,1024]{4,3,2,1,0:T(4,128)} %first_pack.1), calls=%async_computation | async-start | bytes 1572864 | tf_op jit(solution)/shard_map/all_to_all | solution.py:523
  7.4 2.1 %last_pack.1 = f32[8,3,10,4,128]{4,3,2,1,0:T(4,128)} custom-call(f32[3,25,4,1024]{3,2,1,0:T(4,128)} %spectrum.3), custom_call_target="tpu_custom_call" | custom-call | flops 1000 | bytes 4000000 | tf_op jit(solution)/shard_map/last_pack/pallas_call | solution.py:468
  9.5 0.0 copy-start
  9.5 0.0 copy-start.3
  9.6 0.0 copy-start.4
  9.6 0.1 pad_add_fusion.group
  9.7 0.0 copy-done.5
  9.7 0.0 copy-done.6
  9.7 9.7 %all-to-all-done = f32[8,3,2,4,1024]{4,3,2,1,0:T(4,128)S(1)} async-done(((f32[8,3,2,4,1024]{4,3,2,1,0:T(4,128)}), f32[8,3,2,4,1024]{4,3,2,1,0:T(4,128)S(1)}, u32[]{:S(2)}, u32[]{:S(2)}) %all-to-all-start) | async-done | bytes 786464 | tf_op jit(solution)/shard_map/all_to_all | solution.py:523
  19.4 0.7 halo.2
  20.1 13.6 %all_to_all.15 = f32[8,3,10,4,128]{4,3,2,1,0:T(4,128)S(1)} all-to-all(f32[8,3,10,4,128]{4,3,2,1,0:T(4,128)} %last_pack.1), channel_id=1, replica_groups=mesh['space'=64,'spec'=8] {'spec'}, dimensions={0} | all-to-all | bytes 983040 | tf_op jit(solution)/shard_map/all_to_all | solution.py:527
  33.7 0.7 halo.3
  34.3 1.9 %collective-permute-start.2 = (f32[406,4,128]{2,1,0:T(4,128)S(1)}, f32[406,4,128]{2,1,0:T(4,128)S(1)}, u32[]{:S(2)}, u32[]{:S(2)}) collective-permute-start(f32[406,4,128]{2,1,0:T(4,128)S(1)} %get-tuple-element.23), channel_id=1, source_target_pairs={{0,8},{16,24},{32,40},{48,56},{64,72},{80,88},{96,104},{112,120},{... | collective-permute-start | bytes 2494472 | tf_op jit(solution)/shard_map/ppermute | solution.py:531
  36.3 5.4 %collective-permute-start.1 = (f32[256,4,128]{2,1,0:T(4,128)S(1)}, f32[256,4,128]{2,1,0:T(4,128)S(1)}, u32[]{:S(2)}, u32[]{:S(2)}) collective-permute-start(f32[256,4,128]{2,1,0:T(4,128)S(1)} %get-tuple-element.22), channel_id=1, source_target_pairs={{8,16},{24,32},{40,48},{56,64},{72,80},{88,96},{104,112},{120,128}... | collective-permute-start | bytes 1572872 | tf_op jit(solution)/shard_map/ppermute | solution.py:531
  41.6 3.2 %collective-permute-start = (f32[150,4,128]{2,1,0:T(4,128)S(1)}, f32[150,4,128]{2,1,0:T(4,128)S(1)}, u32[]{:S(2)}, u32[]{:S(2)}) collective-permute-start(f32[150,4,128]{2,1,0:T(4,128)S(1)} %get-tuple-element.21), channel_id=1, source_target_pairs={{8,16},{24,32},{40,48},{56,64},{72,80},{88,96},{104,112},{120,128}... | collective-permute-start | bytes 921608 | tf_op jit(solution)/shard_map/ppermute | solution.py:533
  44.9 11.5 %collective-permute-done.1.far = f32[256,4,128]{2,1,0:T(4,128)S(1)} collective-permute-done((f32[256,4,128]{2,1,0:T(4,128)S(1)}, f32[256,4,128]{2,1,0:T(4,128)S(1)}, u32[]{:S(2)}, u32[]{:S(2)}) %collective-permute-start.1) | collective-permute-done | bytes 524320 | tf_op jit(solution)/shard_map/ppermute | solution.py:531
  56.4 0.0 collective-permute-done.2.near
  56.4 0.0 copy-done
  56.4 0.0 copy-done.3
  56.4 0.0 copy-done.4
  56.4 5.5 %steps.2 = (f32[8,48,4,128]{3,2,1,0:T(4,128)S(1)}, f32[2,2,12,8,128]{4,3,2,1,0:T(8,128)S(1)}, f32[16,4,128]{2,1,0:T(4,128)S(1)}) custom-call(s32[2]{0:T(128)S(1)} %pad_add_fusion.group, f32[25,18]{1,0:T(8,128)S(1)} %copy-done, f32[25]{0:T(128)S(1)} %copy-done.3, f32[25]{0:T(128)S(1)} %copy-done.4, f32[24,16,4,128]{3,2,1,0:T(4,128)S(1)} %bitcast.12, ...), custom_call_target="tpu_custom_call" | custom-call | flops 1000 | bytes 20000000 | tf_op jit(solution)/shard_map/steps/pallas_call | solution.py:468
  62.0 0.0 collective-permute-done.far
  62.0 4.1 %steps.3 = f32[8,91,4,128]{3,2,1,0:T(4,128)} custom-call(s32[2]{0:T(128)S(1)} %pad_add_fusion.group, f32[25,18]{1,0:T(8,128)S(1)} %copy-done, f32[25]{0:T(128)S(1)} %copy-done.3, f32[25]{0:T(128)S(1)} %copy-done.4, f32[24,10,4,128]{3,2,1,0:T(4,128)S(1)} %bitcast.14, f32[150,4,128]{2,1,0:T(4,128)S(1)} %collective-permute-done.far, ...), custom_call_target="tpu_custom_call" | custom-call | flops 1000 | bytes 20000000 | tf_op jit(solution)/shard_map/steps/pallas_call | solution.py:468
  66.1 0.0 copy-start.8
  66.1 0.0 copy-start.7
  66.1 0.0 copy-start.1
  66.1 0.0 copy-start.2
  66.1 5.2 %all-to-all-start.2 = ((f32[8,91,4,128]{3,2,1,0:T(4,128)}), f32[8,91,4,128]{3,2,1,0:T(4,128)S(1)}, u32[]{:S(2)}, u32[]{:S(2)}) async-start(f32[8,91,4,128]{3,2,1,0:T(4,128)} %steps.3), calls=%async_computation.2 | async-start | bytes 2981888 | tf_op jit(solution)/shard_map/all_to_all | solution.py:536
  71.3 0.0 copy-done.8
  71.3 0.1 dynamic_slice.6.cos
  71.4 0.0 copy-done.7
  71.4 0.1 dynamic_slice.7.sin
  71.5 19.3 %all-to-all-done.2.got = f32[8,91,4,128]{3,2,1,0:T(4,128)S(1)} async-done(((f32[8,91,4,128]{3,2,1,0:T(4,128)}), f32[8,91,4,128]{3,2,1,0:T(4,128)S(1)}, u32[]{:S(2)}, u32[]{:S(2)}) %all-to-all-start.2) | async-done | bytes 1490976 | tf_op jit(solution)/shard_map/all_to_all | solution.py:536
  90.8 0.0 copy-done.1
  90.8 0.0 copy-done.2
  90.8 1.9 %source.1 = f32[3,25,4,1024]{3,2,1,0:T(4,128)} custom-call(f32[3]{0:T(128)S(1)} %dynamic_slice.6.cos, f32[3]{0:T(128)S(1)} %dynamic_slice.7.sin, f32[8,91,4,128]{3,2,1,0:T(4,128)S(1)} %all-to-all-done.2.got, f32[4,1024]{1,0:T(4,128)S(1)} %copy-done.1, f32[4,1024]{1,0:T(4,128)S(1)} %copy-done.2), custom_call_target="tpu_custom_call" | custom-call | flops 1000 | bytes 4000000 | tf_op jit(solution)/shard_map/source/pallas_call | solution.py:468
  (2 shorter events, 0.0 us)
Async XLA Ops:
  2.0 7.6 %copy-start.5 = (s32[4,1024]{1,0:T(4,128)S(1)}, s32[4,1024]{1,0:T(4,128)}, u32[]{:S(2)}) copy-start(s32[4,1024]{1,0:T(4,128)} %param.12) | copy-start | bytes 49156
  2.0 7.6 %copy-start.6 = (f32[4,1024]{1,0:T(4,128)S(1)}, f32[4,1024]{1,0:T(4,128)}, u32[]{:S(2)}) copy-start(f32[4,1024]{1,0:T(4,128)} %param.13) | copy-start | bytes 49156
  2.1 17.3 %all-to-all-start = ((f32[8,3,2,4,1024]{4,3,2,1,0:T(4,128)}), f32[8,3,2,4,1024]{4,3,2,1,0:T(4,128)S(1)}, u32[]{:S(2)}, u32[]{:S(2)}) async-start(f32[8,3,2,4,1024]{4,3,2,1,0:T(4,128)} %first_pack.1), calls=%async_computation | async-start | bytes 1572864 | tf_op jit(solution)/shard_map/all_to_all | solution.py:523
  9.5 46.9 %copy-start = (f32[25,18]{1,0:T(8,128)S(1)}, f32[25,18]{1,0:T(8,128)}, u32[]{:S(2)}) copy-start(f32[25,18]{1,0:T(8,128)} %constant.38.clone.coef) | copy-start | bytes 5404
  9.5 46.8 %copy-start.3 = (f32[25]{0:T(128)S(1)}, f32[25]{0:T(128)}, u32[]{:S(2)}) copy-start(f32[25]{0:T(128)} %constant.39.clone.rfac) | copy-start | bytes 304
  9.6 46.8 %copy-start.4 = (f32[25]{0:T(128)S(1)}, f32[25]{0:T(128)}, u32[]{:S(2)}) copy-start(f32[25]{0:T(128)} %constant.40.clone.frsq) | copy-start | bytes 304
  34.3 22.0 %collective-permute-start.2 = (f32[406,4,128]{2,1,0:T(4,128)S(1)}, f32[406,4,128]{2,1,0:T(4,128)S(1)}, u32[]{:S(2)}, u32[]{:S(2)}) collective-permute-start(f32[406,4,128]{2,1,0:T(4,128)S(1)} %get-tuple-element.23), channel_id=1, source_target_pairs={{0,8},{16,24},{32,40},{48,56},{64,72},{80,88},{96,104},{112,120},{... | collective-permute-start | bytes 2494472 | tf_op jit(solution)/shard_map/ppermute | solution.py:531
  36.3 20.1 %collective-permute-start.1 = (f32[256,4,128]{2,1,0:T(4,128)S(1)}, f32[256,4,128]{2,1,0:T(4,128)S(1)}, u32[]{:S(2)}, u32[]{:S(2)}) collective-permute-start(f32[256,4,128]{2,1,0:T(4,128)S(1)} %get-tuple-element.22), channel_id=1, source_target_pairs={{8,16},{24,32},{40,48},{56,64},{72,80},{88,96},{104,112},{120,128}... | collective-permute-start | bytes 1572872 | tf_op jit(solution)/shard_map/ppermute | solution.py:531
  41.6 20.3 %collective-permute-start = (f32[150,4,128]{2,1,0:T(4,128)S(1)}, f32[150,4,128]{2,1,0:T(4,128)S(1)}, u32[]{:S(2)}, u32[]{:S(2)}) collective-permute-start(f32[150,4,128]{2,1,0:T(4,128)S(1)} %get-tuple-element.21), channel_id=1, source_target_pairs={{8,16},{24,32},{40,48},{56,64},{72,80},{88,96},{104,112},{120,128}... | collective-permute-start | bytes 921608 | tf_op jit(solution)/shard_map/ppermute | solution.py:533
  66.1 5.2 %copy-start.8 = (f32[24]{0:T(128)S(1)}, f32[24]{0:T(128)}, u32[]{:S(2)}) copy-start(f32[24]{0:T(128)} %constant.41.clone) | copy-start | bytes 292
  66.1 5.3 %copy-start.7 = (f32[24]{0:T(128)S(1)}, f32[24]{0:T(128)}, u32[]{:S(2)}) copy-start(f32[24]{0:T(128)} %constant.42.clone) | copy-start | bytes 292
  66.1 24.7 %copy-start.1 = (f32[4,1024]{1,0:T(4,128)S(1)}, f32[4,1024]{1,0:T(4,128)}, u32[]{:S(2)}) copy-start(f32[4,1024]{1,0:T(4,128)} %wind_u.1) | copy-start | bytes 49156
  66.1 24.7 %copy-start.2 = (f32[4,1024]{1,0:T(4,128)S(1)}, f32[4,1024]{1,0:T(4,128)}, u32[]{:S(2)}) copy-start(f32[4,1024]{1,0:T(4,128)} %wind_v.1) | copy-start | bytes 49156
  66.1 24.7 %all-to-all-start.2 = ((f32[8,91,4,128]{3,2,1,0:T(4,128)}), f32[8,91,4,128]{3,2,1,0:T(4,128)S(1)}, u32[]{:S(2)}, u32[]{:S(2)}) async-start(f32[8,91,4,128]{3,2,1,0:T(4,128)} %steps.3), calls=%async_computation.2 | async-start | bytes 2981888 | tf_op jit(solution)/shard_map/all_to_all | solution.py:536

commit v11 on v9

--- a/solution.py
+++ b/solution.py
@@ -280,7 +280,7 @@
                     ex_a[EXTRA_AT[w, d % DIRS], slot] = whole_tile(w, d % DIRS, rows)
             return carry
 
-        lax.fori_loop(0, tiles, fill, 0)
+        lax.fori_loop(0, tiles, fill, 0, unroll=2 if UNROLL else 1)
 
     pl.when(group[1] == 1)(lambda: load(near, far))
     pl.when(group[1] == 0)(lambda: load(far, near))

time: 83 us -> 83 us (level)
  no operation moved by 1% of the time
where the time goes in v11:
time: 83 us; the launch traced here: 81.6 us
  waiting for transfers between devices  40.1 us (48%)
  starting transfers between devices  24.2 us (29%)
  Pallas kernels  16.8 us (20%)
    all_to_all x1, waiting for transfers between devices, on_device(): got = lax.all_to_all(made, 'spec', 0, 0, tiled=True)  18.4 us
    pallas_call x5, Pallas kernels, moving(): pl.pallas_call(kernel, out_shape=[jax.ShapeDtypeStruct(s, jnp.float32) fo...  15.4 us
    all_to_all x1, waiting for transfers between devices, on_device(): own = lax.all_to_all(pack, 'spec', 0, 0, tiled=True)  9.67 us
    all_to_all x1, waiting for transfers between devices, on_device(): own_2 = lax.all_to_all(pack_2, 'spec', 0, 0, tiled=True)  8.39 us
    all_to_all x1, starting transfers between devices, on_device(): own = lax.all_to_all(pack, 'spec', 0, 0, tiled=True)  5.32 us
    ppermute x1, starting transfers between devices, on_device(): lax.ppermute(far, 'space', over)  4.58 us
    all_to_all x1, starting transfers between devices, on_device(): got = lax.all_to_all(made, 'spec', 0, 0, tiled=True)  3.72 us
    all_to_all x1, starting transfers between devices, on_device(): own_2 = lax.all_to_all(pack_2, 'spec', 0, 0, tiled=True)  3.65 us
  transfers between devices with their start and end apart: 7, of which 5 were waited for; matrix products, arithmetic and copies ran while one was open for 0% of the time, Pallas kernels for 10%

profile of v11, /device:TPU:448, one launch (start us, length us, event | category | flops | bytes accessed | tf_op | source)
XLA Modules:
  0.0 81.6 jit_solution(3691877806216548658)
XLA Ops:
  0.0 2.0 %first_pack.1 = f32[8,3,2,4,1024]{4,3,2,1,0:T(4,128)} custom-call(f32[3,25,4,1024]{3,2,1,0:T(4,128)} %spectrum.3), custom_call_target="tpu_custom_call" | custom-call | flops 1000 | bytes 4000000 | tf_op jit(solution)/shard_map/first_pack/pallas_call | solution.py:461
  2.0 0.0 copy-start.5
  2.0 0.0 copy-start.6
  2.1 5.3 %all-to-all-start = ((f32[8,3,2,4,1024]{4,3,2,1,0:T(4,128)}), f32[8,3,2,4,1024]{4,3,2,1,0:T(4,128)S(1)}, u32[]{:S(2)}, u32[]{:S(2)}) async-start(f32[8,3,2,4,1024]{4,3,2,1,0:T(4,128)} %first_pack.1), calls=%async_computation | async-start | bytes 1572864 | tf_op jit(solution)/shard_map/all_to_all | solution.py:516
  7.4 2.1 %last_pack.1 = f32[8,3,10,4,128]{4,3,2,1,0:T(4,128)} custom-call(f32[3,25,4,1024]{3,2,1,0:T(4,128)} %spectrum.3), custom_call_target="tpu_custom_call" | custom-call | flops 1000 | bytes 4000000 | tf_op jit(solution)/shard_map/last_pack/pallas_call | solution.py:461
  9.5 0.0 copy-start
  9.5 0.0 copy-start.3
  9.6 0.0 copy-start.4
  9.6 0.1 pad_add_fusion.group
  9.7 0.0 copy-done.5
  9.7 0.0 copy-done.6
  9.7 9.7 %all-to-all-done = f32[8,3,2,4,1024]{4,3,2,1,0:T(4,128)S(1)} async-done(((f32[8,3,2,4,1024]{4,3,2,1,0:T(4,128)}), f32[8,3,2,4,1024]{4,3,2,1,0:T(4,128)S(1)}, u32[]{:S(2)}, u32[]{:S(2)}) %all-to-all-start) | async-done | bytes 786464 | tf_op jit(solution)/shard_map/all_to_all | solution.py:516
  19.4 0.7 halo.2
  20.1 3.6 %all-to-all-start.1 = ((f32[8,3,10,4,128]{4,3,2,1,0:T(4,128)}), f32[8,3,10,4,128]{4,3,2,1,0:T(4,128)S(1)}, u32[]{:S(2)}, u32[]{:S(2)}) async-start(f32[8,3,10,4,128]{4,3,2,1,0:T(4,128)} %last_pack.1), calls=%async_computation.1 | async-start | bytes 983040 | tf_op jit(solution)/shard_map/all_to_all | solution.py:520
  23.7 4.6 %collective-permute-start.2 = (f32[16,16,4,128]{3,2,1,0:T(4,128)S(1)}, f32[16,16,4,128]{3,2,1,0:T(4,128)S(1)}, u32[]{:S(2)}, u32[]{:S(2)}) collective-permute-start(f32[16,16,4,128]{3,2,1,0:T(4,128)S(1)} %get-tuple-element.22), channel_id=1, source_target_pairs={{8,16},{24,32},{40,48},{56,64},{72,80},{88,96},{104,112},{120,128}... | collective-permute-start | bytes 1572872 | tf_op jit(solution)/shard_map/ppermute | solution.py:523
  28.3 1.9 %collective-permute-start.3 = (f32[16,16,4,128]{3,2,1,0:T(4,128)S(1)}, f32[16,16,4,128]{3,2,1,0:T(4,128)S(1)}, u32[]{:S(2)}, u32[]{:S(2)}) collective-permute-start(f32[16,16,4,128]{3,2,1,0:T(4,128)S(1)} %get-tuple-element.23), channel_id=1, source_target_pairs={{0,8},{16,24},{32,40},{48,56},{64,72},{80,88},{96,104},{112,120},{... | collective-permute-start | bytes 1572872 | tf_op jit(solution)/shard_map/ppermute | solution.py:523
  30.3 8.4 %all-to-all-done.1 = f32[8,3,10,4,128]{4,3,2,1,0:T(4,128)S(1)} async-done(((f32[8,3,10,4,128]{4,3,2,1,0:T(4,128)}), f32[8,3,10,4,128]{4,3,2,1,0:T(4,128)S(1)}, u32[]{:S(2)}, u32[]{:S(2)}) %all-to-all-start.1) | async-done | bytes 491552 | tf_op jit(solution)/shard_map/all_to_all | solution.py:520
  38.7 0.6 halo.3
  39.3 1.9 %collective-permute-start = (f32[15,10,4,128]{3,2,1,0:T(4,128)S(1)}, f32[15,10,4,128]{3,2,1,0:T(4,128)S(1)}, u32[]{:S(2)}, u32[]{:S(2)}) collective-permute-start(f32[15,10,4,128]{3,2,1,0:T(4,128)S(1)} %get-tuple-element.20), channel_id=1, source_target_pairs={{8,16},{24,32},{40,48},{56,64},{72,80},{88,96},{104,112},{120,128}... | collective-permute-start | bytes 921608 | tf_op jit(solution)/shard_map/ppermute | solution.py:525
  41.2 3.1 %collective-permute-start.1 = (f32[15,10,4,128]{3,2,1,0:T(4,128)S(1)}, f32[15,10,4,128]{3,2,1,0:T(4,128)S(1)}, u32[]{:S(2)}, u32[]{:S(2)}) collective-permute-start(f32[15,10,4,128]{3,2,1,0:T(4,128)S(1)} %get-tuple-element.21), channel_id=1, source_target_pairs={{0,8},{16,24},{32,40},{48,56},{64,72},{80,88},{96,104},{112,120},{... | collective-permute-start | bytes 921608 | tf_op jit(solution)/shard_map/ppermute | solution.py:525
  44.3 0.1 collective-permute-done.2.far
  44.4 0.0 collective-permute-done.3.near
  44.4 0.0 copy-done
  44.4 0.0 copy-done.3
  44.4 0.0 copy-done.4
  44.4 5.3 %steps.2 = (f32[8,48,4,128]{3,2,1,0:T(4,128)S(1)}, f32[2,2,12,8,128]{4,3,2,1,0:T(8,128)S(1)}, f32[16,4,128]{2,1,0:T(4,128)S(1)}) custom-call(s32[2]{0:T(128)S(1)} %pad_add_fusion.group, f32[25,18]{1,0:T(8,128)S(1)} %copy-done, f32[25]{0:T(128)S(1)} %copy-done.3, f32[25]{0:T(128)S(1)} %copy-done.4, f32[24,16,4,128]{3,2,1,0:T(4,128)S(1)} %bitcast.12, ...), custom_call_target="tpu_custom_call" | custom-call | flops 1000 | bytes 20000000 | tf_op jit(solution)/shard_map/steps/pallas_call | solution.py:461
  49.8 3.5 %collective-permute-done.far = f32[15,10,4,128]{3,2,1,0:T(4,128)S(1)} collective-permute-done((f32[15,10,4,128]{3,2,1,0:T(4,128)S(1)}, f32[15,10,4,128]{3,2,1,0:T(4,128)S(1)}, u32[]{:S(2)}, u32[]{:S(2)}) %collective-permute-start) | collective-permute-done | bytes 307232 | tf_op jit(solution)/shard_map/ppermute | solution.py:525
  53.3 0.0 collective-permute-done.1.near
  53.3 4.0 %steps.3 = f32[8,91,4,128]{3,2,1,0:T(4,128)} custom-call(s32[2]{0:T(128)S(1)} %pad_add_fusion.group, f32[25,18]{1,0:T(8,128)S(1)} %copy-done, f32[25]{0:T(128)S(1)} %copy-done.3, f32[25]{0:T(128)S(1)} %copy-done.4, f32[24,10,4,128]{3,2,1,0:T(4,128)S(1)} %bitcast.14, f32[15,10,4,128]{3,2,1,0:T(4,128)S(1)} %collective-permute-done.far, ...), custom_call_target="tpu_custom_call" | custom-call | flops 1000 | bytes 20000000 | tf_op jit(solution)/shard_map/steps/pallas_call | solution.py:461
  57.3 0.0 copy-start.8
  57.3 0.0 copy-start.7
  57.3 0.0 copy-start.1
  57.3 0.0 copy-start.2
  57.3 3.7 %all-to-all-start.2 = ((f32[8,91,4,128]{3,2,1,0:T(4,128)}), f32[8,91,4,128]{3,2,1,0:T(4,128)S(1)}, u32[]{:S(2)}, u32[]{:S(2)}) async-start(f32[8,91,4,128]{3,2,1,0:T(4,128)} %steps.3), calls=%async_computation.2 | async-start | bytes 2981888 | tf_op jit(solution)/shard_map/all_to_all | solution.py:528
  61.1 0.0 copy-done.8
  61.1 0.1 dynamic_slice.6.cos
  61.2 0.0 copy-done.7
  61.2 0.1 dynamic_slice.7.sin
  61.2 18.4 %all-to-all-done.2.got = f32[8,91,4,128]{3,2,1,0:T(4,128)S(1)} async-done(((f32[8,91,4,128]{3,2,1,0:T(4,128)}), f32[8,91,4,128]{3,2,1,0:T(4,128)S(1)}, u32[]{:S(2)}, u32[]{:S(2)}) %all-to-all-start.2) | async-done | bytes 1490976 | tf_op jit(solution)/shard_map/all_to_all | solution.py:528
  79.7 0.0 copy-done.1
  79.7 0.0 copy-done.2
  79.7 1.9 %source.1 = f32[3,25,4,1024]{3,2,1,0:T(4,128)} custom-call(f32[3]{0:T(128)S(1)} %dynamic_slice.6.cos, f32[3]{0:T(128)S(1)} %dynamic_slice.7.sin, f32[8,91,4,128]{3,2,1,0:T(4,128)S(1)} %all-to-all-done.2.got, f32[4,1024]{1,0:T(4,128)S(1)} %copy-done.1, f32[4,1024]{1,0:T(4,128)S(1)} %copy-done.2), custom_call_target="tpu_custom_call" | custom-call | flops 1000 | bytes 4000000 | tf_op jit(solution)/shard_map/source/pallas_call | solution.py:461
  (2 shorter events, 0.0 us)
Async XLA Ops:
  2.0 7.6 %copy-start.5 = (s32[4,1024]{1,0:T(4,128)S(1)}, s32[4,1024]{1,0:T(4,128)}, u32[]{:S(2)}) copy-start(s32[4,1024]{1,0:T(4,128)} %param.12) | copy-start | bytes 49156
  2.0 7.6 %copy-start.6 = (f32[4,1024]{1,0:T(4,128)S(1)}, f32[4,1024]{1,0:T(4,128)}, u32[]{:S(2)}) copy-start(f32[4,1024]{1,0:T(4,128)} %param.13) | copy-start | bytes 49156
  2.1 17.3 %all-to-all-start = ((f32[8,3,2,4,1024]{4,3,2,1,0:T(4,128)}), f32[8,3,2,4,1024]{4,3,2,1,0:T(4,128)S(1)}, u32[]{:S(2)}, u32[]{:S(2)}) async-start(f32[8,3,2,4,1024]{4,3,2,1,0:T(4,128)} %first_pack.1), calls=%async_computation | async-start | bytes 1572864 | tf_op jit(solution)/shard_map/all_to_all | solution.py:516
  9.5 34.9 %copy-start = (f32[25,18]{1,0:T(8,128)S(1)}, f32[25,18]{1,0:T(8,128)}, u32[]{:S(2)}) copy-start(f32[25,18]{1,0:T(8,128)} %constant.38.clone.coef) | copy-start | bytes 5404
  9.5 34.9 %copy-start.3 = (f32[25]{0:T(128)S(1)}, f32[25]{0:T(128)}, u32[]{:S(2)}) copy-start(f32[25]{0:T(128)} %constant.39.clone.rfac) | copy-start | bytes 304
  9.6 34.9 %copy-start.4 = (f32[25]{0:T(128)S(1)}, f32[25]{0:T(128)}, u32[]{:S(2)}) copy-start(f32[25]{0:T(128)} %constant.40.clone.frsq) | copy-start | bytes 304
  20.1 18.6 %all-to-all-start.1 = ((f32[8,3,10,4,128]{4,3,2,1,0:T(4,128)}), f32[8,3,10,4,128]{4,3,2,1,0:T(4,128)S(1)}, u32[]{:S(2)}, u32[]{:S(2)}) async-start(f32[8,3,10,4,128]{4,3,2,1,0:T(4,128)} %last_pack.1), calls=%async_computation.1 | async-start | bytes 983040 | tf_op jit(solution)/shard_map/all_to_all | solution.py:520
  23.7 20.7 %collective-permute-start.2 = (f32[16,16,4,128]{3,2,1,0:T(4,128)S(1)}, f32[16,16,4,128]{3,2,1,0:T(4,128)S(1)}, u32[]{:S(2)}, u32[]{:S(2)}) collective-permute-start(f32[16,16,4,128]{3,2,1,0:T(4,128)S(1)} %get-tuple-element.22), channel_id=1, source_target_pairs={{8,16},{24,32},{40,48},{56,64},{72,80},{88,96},{104,112},{120,128}... | collective-permute-start | bytes 1572872 | tf_op jit(solution)/shard_map/ppermute | solution.py:523
  28.3 16.1 %collective-permute-start.3 = (f32[16,16,4,128]{3,2,1,0:T(4,128)S(1)}, f32[16,16,4,128]{3,2,1,0:T(4,128)S(1)}, u32[]{:S(2)}, u32[]{:S(2)}) collective-permute-start(f32[16,16,4,128]{3,2,1,0:T(4,128)S(1)} %get-tuple-element.23), channel_id=1, source_target_pairs={{0,8},{16,24},{32,40},{48,56},{64,72},{80,88},{96,104},{112,120},{... | collective-permute-start | bytes 1572872 | tf_op jit(solution)/shard_map/ppermute | solution.py:523
  39.3 14.0 %collective-permute-start = (f32[15,10,4,128]{3,2,1,0:T(4,128)S(1)}, f32[15,10,4,128]{3,2,1,0:T(4,128)S(1)}, u32[]{:S(2)}, u32[]{:S(2)}) collective-permute-start(f32[15,10,4,128]{3,2,1,0:T(4,128)S(1)} %get-tuple-element.20), channel_id=1, source_target_pairs={{8,16},{24,32},{40,48},{56,64},{72,80},{88,96},{104,112},{120,128}... | collective-permute-start | bytes 921608 | tf_op jit(solution)/shard_map/ppermute | solution.py:525
  41.2 12.0 %collective-permute-start.1 = (f32[15,10,4,128]{3,2,1,0:T(4,128)S(1)}, f32[15,10,4,128]{3,2,1,0:T(4,128)S(1)}, u32[]{:S(2)}, u32[]{:S(2)}) collective-permute-start(f32[15,10,4,128]{3,2,1,0:T(4,128)S(1)} %get-tuple-element.21), channel_id=1, source_target_pairs={{0,8},{16,24},{32,40},{48,56},{64,72},{80,88},{96,104},{112,120},{... | collective-permute-start | bytes 921608 | tf_op jit(solution)/shard_map/ppermute | solution.py:525
  57.3 3.8 %copy-start.8 = (f32[24]{0:T(128)S(1)}, f32[24]{0:T(128)}, u32[]{:S(2)}) copy-start(f32[24]{0:T(128)} %constant.41.clone) | copy-start | bytes 292
  57.3 3.9 %copy-start.7 = (f32[24]{0:T(128)S(1)}, f32[24]{0:T(128)}, u32[]{:S(2)}) copy-start(f32[24]{0:T(128)} %constant.42.clone) | copy-start | bytes 292
  57.3 22.4 %copy-start.1 = (f32[4,1024]{1,0:T(4,128)S(1)}, f32[4,1024]{1,0:T(4,128)}, u32[]{:S(2)}) copy-start(f32[4,1024]{1,0:T(4,128)} %wind_u.1) | copy-start | bytes 49156
  57.3 22.3 %copy-start.2 = (f32[4,1024]{1,0:T(4,128)S(1)}, f32[4,1024]{1,0:T(4,128)}, u32[]{:S(2)}) copy-start(f32[4,1024]{1,0:T(4,128)} %wind_v.1) | copy-start | bytes 49156
  57.3 22.3 %all-to-all-start.2 = ((f32[8,91,4,128]{3,2,1,0:T(4,128)}), f32[8,91,4,128]{3,2,1,0:T(4,128)S(1)}, u32[]{:S(2)}, u32[]{:S(2)}) async-start(f32[8,91,4,128]{3,2,1,0:T(4,128)} %steps.3), calls=%async_computation.2 | async-start | bytes 2981888 | tf_op jit(solution)/shard_map/all_to_all | solution.py:528
